TPU v7x, 32 devices: a whole 2x2x4 slice. The times are simulated.
32 devices in a mesh: groups: 2 (over y), dp: 4 (over z), nbr: 2 (over x), mp: 2 (over core).
Axes of the slice: x: 2, y: 2, z: 4, core: 2. Of those that a mesh axis runs over, the one named last changes fastest.
Arguments:
- hidden: bfloat16 [2048, 4096], P(('groups', 'dp', 'nbr'), 'mp'), parts along dimension 0, may hold values from -6 to 6
- grad_out: bfloat16 [2048, 4096], P(('groups', 'dp', 'nbr'), 'mp'), parts along dimension 0, may hold values from -6 to 6
- database: bfloat16 [128, 64, 896], P(('groups', 'dp', 'nbr')), parts along dimension 0, may hold values from -6 to 6
- enc_gain: float32 [896], replicated, may hold values from 0.25 to 1.75
- query_weight: bfloat16 [4096, 2048], P('dp', 'mp'), may hold values from -0.1875 to 0.1875
- key_weight: bfloat16 [896, 2048], P('dp', 'mp'), may hold values from -0.1875 to 0.1875
- value_weight: bfloat16 [896, 2048], P('dp', 'mp'), may hold values from -0.1875 to 0.1875
- out_weight: bfloat16 [2048, 4096], P('mp', 'dp'), may hold values from -0.375 to 0.375
- block_ids: int32 [32, 4], P(('groups', 'dp', 'nbr')), parts along dimension 0, may hold values from 0 to 7
- owners: int32 [32, 4], P(('groups', 'dp', 'nbr')), parts along dimension 0, may hold values from 0 to 1, as said below
Outputs:
- output: bfloat16 [2048, 4096], P(('groups', 'dp', 'nbr'), 'mp'), parts along dimension 0
- grad_hidden: bfloat16 [2048, 4096], P(('groups', 'dp', 'nbr'), 'mp'), parts along dimension 0
There are 2 independent parts, one for each index of `groups`. A program takes and returns all parts, laid end to end along the dimension named above; an argument that names none is the same for every part. Nothing has to cross between parts.
Inputs may be any that keep to these rules, and one draw needn't show every extreme that they name: `owners`: of the 8 blocks named by one device's spans, exactly 4 have each owner.
All inputs are finite; a program needn't handle non-finite values.
Results may differ from a plain program's by a relative error of at most 0.0098.
Values may be sent and summed in bfloat16 or wider, within the bound.
No kernel may reach another device: no remote copies, remote signals or barrier semaphores. Data moves between devices by JAX's collectives and lax.ppermute only.
A program may use at most 128 MiB of HBM per device.

v0:
```python
import math

import jax
import jax.numpy as jnp
from jax import lax
from jax.sharding import PartitionSpec as P

HD = 128
SPAN = 64
BLOCK = 64
UPC = 4
UNITS = 8


def encode_rows(states, enc_gain):
    widened = states.astype(jnp.float32)
    inverse = lax.rsqrt(jnp.mean(widened * widened, axis=-1, keepdims=True) + 1e-06)
    return (widened * inverse * enc_gain).astype(jnp.bfloat16)


def local(
    hidden,
    grad_out,
    database,
    enc_gain,
    query_weight,
    key_weight,
    value_weight,
    out_weight,
    block_ids,
    owners,
):
    tok_rows = hidden.shape[0]
    span_count = block_ids.shape[0]
    local_width = query_weight.shape[1]
    local_heads = local_width // HD
    owner_count = lax.axis_size("nbr")
    capacity = UNITS // owner_count
    score_scale = 1.0 / math.sqrt(HD)
    full_hidden, full_grad = (
        lax.all_gather(hidden, "mp", axis=1, tiled=True),
        lax.all_gather(grad_out, "mp", axis=1, tiled=True),
    )
    query_full, key_full, value_full, out_full = (
        lax.all_gather(query_weight, "dp", axis=0, tiled=True),
        lax.all_gather(key_weight, "dp", axis=0, tiled=True),
        lax.all_gather(value_weight, "dp", axis=0, tiled=True),
        lax.all_gather(out_weight, "dp", axis=1, tiled=True),
    )
    queries = jnp.dot(full_hidden, query_full, preferred_element_type=jnp.float32)
    queries = queries.astype(jnp.bfloat16).reshape(span_count, SPAN, local_heads, HD)
    owner_flat = owners.reshape(UNITS)
    id_flat = block_ids.reshape(UNITS)
    positions = jnp.arange(UNITS, dtype=jnp.int32)
    send_order = jnp.argsort(owner_flat * UNITS + positions)
    restore = jnp.argsort(send_order)
    requests = id_flat[send_order].reshape(owner_count, capacity)
    fetched = database[lax.all_to_all(requests, "nbr", split_axis=0, concat_axis=0, tiled=True)]
    encoded = encode_rows(fetched, enc_gain)
    key_part = jnp.einsum(
        "osbe,ef->osbf", encoded, key_full, preferred_element_type=jnp.float32
    ).astype(jnp.bfloat16)
    value_part = jnp.einsum(
        "osbe,ef->osbf", encoded, value_full, preferred_element_type=jnp.float32
    ).astype(jnp.bfloat16)
    stacked = jnp.concatenate((key_part, value_part), axis=-1)
    answers = lax.all_to_all(stacked, "nbr", split_axis=0, concat_axis=0, tiled=True)
    gathered = answers.reshape((UNITS,) + answers.shape[2:])[restore]
    kv_rows = gathered.reshape(span_count, UPC * BLOCK, 2 * local_width)
    key_rows = kv_rows[:, :, :local_width]
    value_rows = kv_rows[:, :, local_width:]
    key_rows = key_rows.reshape(span_count, UPC * BLOCK, local_heads, HD)
    value_rows = value_rows.reshape(span_count, UPC * BLOCK, local_heads, HD)
    scores = (
        jnp.einsum("cthd,cjhd->chtj", queries, key_rows, preferred_element_type=jnp.float32)
        * score_scale
    )
    attention = jax.nn.softmax(scores, axis=-1)
    attention_low = attention.astype(jnp.bfloat16)
    mixture = jnp.einsum(
        "chtj,cjhd->cthd", attention_low, value_rows, preferred_element_type=jnp.float32
    )
    mixture = mixture.astype(jnp.bfloat16).reshape(tok_rows, local_width)
    partial_out = jnp.dot(mixture, out_full, preferred_element_type=jnp.float32)
    summed = lax.psum_scatter(partial_out, "mp", scatter_dimension=1, tiled=True)
    output = (hidden.astype(jnp.float32) + summed).astype(jnp.bfloat16)
    grad_mixture = jnp.einsum("td,hd->th", full_grad, out_full, preferred_element_type=jnp.float32)
    grad_mixture = grad_mixture.astype(jnp.bfloat16).reshape(span_count, SPAN, local_heads, HD)
    grad_attention = jnp.einsum(
        "cthd,cjhd->chtj", grad_mixture, value_rows, preferred_element_type=jnp.float32
    )
    grad_scores = (
        attention
        * (grad_attention - jnp.sum(attention * grad_attention, axis=-1, keepdims=True))
        * score_scale
    )
    grad_scores = grad_scores.astype(jnp.bfloat16)
    grad_queries = jnp.einsum(
        "chtj,cjhd->cthd", grad_scores, key_rows, preferred_element_type=jnp.float32
    )
    grad_queries = grad_queries.astype(jnp.bfloat16).reshape(tok_rows, local_width)
    partial_grad = jnp.einsum(
        "th,dh->td", grad_queries, query_full, preferred_element_type=jnp.float32
    )
    grad_sum = lax.psum_scatter(partial_grad, "mp", scatter_dimension=1, tiled=True)
    grad_hidden = (grad_out.astype(jnp.float32) + grad_sum).astype(jnp.bfloat16)
    return (output, grad_hidden)


def solution(mesh):
    in_specs = (
        P(("groups", "dp", "nbr"), "mp"),
        P(("groups", "dp", "nbr"), "mp"),
        P(("groups", "dp", "nbr"), None, None),
        P(),
        P("dp", "mp"),
        P("dp", "mp"),
        P("dp", "mp"),
        P("mp", "dp"),
        P(("groups", "dp", "nbr"), None),
        P(("groups", "dp", "nbr"), None),
    )
    out_specs = (P(("groups", "dp", "nbr"), "mp"), P(("groups", "dp", "nbr"), "mp"))
    return jax.shard_map(local, mesh=mesh, in_specs=in_specs, out_specs=out_specs, check_vma=False)
```

profile of v0, /device:TPU:0, one launch (start us, length us, event | category | flops | bytes accessed | tf_op | source)
XLA Modules:
  0.0 472.1 jit_solution(4145279502650904091)
XLA Ops:
  7.2 0.7 all-gather.7.cloned.1.call-update
  8.0 0.7 all-gather.9.cloned.1.call-update
  11.4 1.0 sort.31
  13.1 7.7 %all_to_all.17 = s32[2,1,4]{2,1,0:T(1,128)S(1)} all-to-all(s32[2,1,4]{2,1,0:T(1,128)S(1)} %bitcast.72), channel_id=1, replica_groups=mesh['groups'=2,'dp'=4,'nbr'=2,'mp'=2] {'nbr'}, dimensions={0} | all-to-all | bytes 64 | tf_op jit(solution)/shard_map/all_to_all | solution.py:58
  20.9 0.7 gather_fusion.1
  21.9 31.8 %all-gather.7.cloned.1.call-done = bf16[896,1024]{1,0:T(8,128)(2,1)} async-done(((bf16[224,1024]{1,0:T(8,128)(2,1)}), bf16[896,1024]{1,0:T(8,128)(2,1)}) %all-gather.7.cloned.1.call-update) | async-done | bytes 1835024 | tf_op jit(solution)/shard_map/all_gather | solution.py:46
  53.7 2.8 fusion.9
  56.5 39.0 %all-gather.9.cloned.1.call-done = bf16[896,1024]{1,0:T(8,128)(2,1)} async-done(((bf16[224,1024]{1,0:T(8,128)(2,1)}), bf16[896,1024]{1,0:T(8,128)(2,1)}) %all-gather.9.cloned.1.call-update) | async-done | bytes 1835024 | tf_op jit(solution)/shard_map/all_gather | solution.py:47
  95.6 2.8 fusion.12
  98.4 1.5 pad_maximum_fusion
  99.9 3.8 all-to-all-start.1
  103.8 1.0 sort.32
  104.8 24.0 %all-to-all-done.1 = bf16[2,4,64,2048]{3,2,1,0:T(8,128)(2,1)S(1)} async-done(((bf16[2,4,64,2048]{3,2,1,0:T(8,128)(2,1)}), bf16[2,4,64,2048]{3,2,1,0:T(8,128)(2,1)S(1)}, u32[]{:S(2)}, u32[]{:S(2)}) %all-to-all-start.1) | async-done | bytes 2097184 | tf_op jit(solution)/shard_map/all_to_all | solution.py:67
  128.9 2.0 gather_fusion.2
  130.9 1.7 fusion.44
  132.6 1.3 copy.34
  134.5 122.8 %all-gather.13.cloned.1.call-done = bf16[4096,1024]{1,0:T(8,128)(2,1)} async-done(((bf16[1024,1024]{1,0:T(8,128)(2,1)}), bf16[4096,1024]{1,0:T(8,128)(2,1)}) %all-gather.13.cloned.1.call-update) | async-done | bytes 8388624 | tf_op jit(solution)/shard_map/all_gather | solution.py:45
  257.3 5.0 %fusion.24 = bf16[16,8,8,128]{3,1,2,0:T(8,128)(2,1)S(1)} fusion(bf16[128,4096]{1,0:T(8,128)(2,1)} %all-gather.11.cloned.1.call-done, bf16[4096,1024]{1,0:T(8,128)(2,1)} %all-gather.13.cloned.1.call-done), kind=kOutput, calls=%fused_computation.30 | convolution fusion | flops 1073872896 | bytes 9699328 | tf_op jit(solution)/shard_map/dot_general | solution.py:50
  262.4 1.6 convolution_multiply_fusion
  263.9 1.3 fusion.45
  265.2 0.8 all-gather.17.cloned.1.call-done
  266.0 152.3 %all-gather.15.cloned.1.call-done = bf16[1024,4096]{1,0:T(8,128)(2,1)} async-done(((bf16[1024,1024]{1,0:T(8,128)(2,1)}), bf16[1024,4096]{1,0:T(8,128)(2,1)}) %all-gather.15.cloned.1.call-update) | async-done | bytes 8388624 | tf_op jit(solution)/shard_map/all_gather | solution.py:48
  418.3 6.6 %fusion.26 = bf16[16,8,8,128]{3,1,2,0:T(8,128)(2,1)S(1)} fusion(bf16[128,4096]{1,0:T(8,128)(2,1)} %all-gather.17.cloned.1.call-done, bf16[1024,4096]{1,0:T(8,128)(2,1)} %all-gather.15.cloned.1.call-done), kind=kOutput, calls=%fused_computation.32 | convolution fusion | flops 1073872896 | bytes 9699328 | tf_op jit(solution)/shard_map/td,hd->th/dot_general | solution.py:87
  425.0 1.3 fusion.39
  426.2 7.9 %fusion.23 = bf16[2,64,8,128]{3,1,2,0:T(8,128)(2,1)S(1)} fusion(bf16[2,256,8,128]{1,3,2,0:T(8,128)(2,1)} %bitcast.63, f32[2,8,64,256]{3,2,1,0:T(8,128)} %fusion.39, f32[2,8,64,256]{3,2,1,0:T(8,128)} %get-tuple-element.9, f32[2,8,64]{2,1,0:T(8,128)S(1)} %get-tuple-element.8), kind=kOutput, calls=%fused_computation.29 | convolution fusion | flops 69076224 | bytes 3411968 | tf_op jit(solution)/shard_map/chtj,cjhd->cthd/dot_general | solution.py:98
  434.4 7.6 %fusion.33 = f32[128,4096]{1,0:T(8,128)} fusion(bf16[4096,1024]{1,0:T(8,128)(2,1)} %all-gather.13.cloned.1.call-done, bf16[16,8,8,128]{3,2,1,0:T(8,128)(2,1)S(1)} %bitcast.70), kind=kOutput, calls=%fused_computation.40 | convolution fusion | flops 1073741824 | bytes 10747904 | tf_op jit(solution)/shard_map/th,dh->td/dot_general | solution.py:102
  442.2 1.8 fusion.25
  444.3 6.7 %fusion.36 = f32[128,4096]{1,0:T(8,128)} fusion(bf16[1024,4096]{1,0:T(8,128)(2,1)} %all-gather.15.cloned.1.call-done, bf16[16,8,8,128]{3,2,1,0:T(8,128)(2,1)S(1)} %bitcast.67), kind=kOutput, calls=%fused_computation.43 | convolution fusion | flops 1073741824 | bytes 10747904 | tf_op jit(solution)/shard_map/dot_general | solution.py:84
  451.1 1.0 copy-done.1
  452.1 2.1 add_convert_fusion
  454.2 8.9 %reduce-scatter.3.cloned.1.call-done = f32[128,2048]{1,0:T(8,128)} async-done(((f32[128,4096]{1,0:T(8,128)}), f32[128,2048]{1,0:T(8,128)}) %reduce-scatter.3.cloned.1.call-update) | async-done | bytes 1048592 | tf_op jit(solution)/shard_map/reduce_scatter | solution.py:85
  463.1 2.1 add_convert_fusion.1
  (49 shorter events, 5.1 us)
Async XLA Ops:
  7.2 13.7 %copy-start = (bf16[8,64,896]{2,1,0:T(8,128)(2,1)S(1)}, bf16[8,64,896]{2,1,0:T(8,128)(2,1)}, u32[]{:S(2)}) copy-start(bf16[8,64,896]{2,1,0:T(8,128)(2,1)} %param.12) | copy-start | bytes 2752516
  7.2 46.5 %all-gather.7.cloned.1.call-start = ((), (), s32[]{:S(2)}) async-start(), calls=%async_computation.4 | async-start | bytes 2293760 | tf_op jit(solution)/shard_map/all_gather | solution.py:46
  7.9 87.7 %all-gather.9.cloned.1.call-start = ((), (), s32[]{:S(2)}) async-start(), calls=%async_computation.5 | async-start | bytes 2293760 | tf_op jit(solution)/shard_map/all_gather | solution.py:47
  8.7 125.8 %all-gather.11.cloned.1.call-start = ((), (), s32[]{:S(2)}) async-start(), calls=%async_computation.6 | async-start | bytes 1572864 | tf_op jit(solution)/shard_map/all_gather | solution.py:41
  9.4 1.8 copy-start.3
  9.4 1.9 copy-start.5
  9.4 247.9 %all-gather.13.cloned.1.call-start = ((), (), s32[]{:S(2)}) async-start(), calls=%async_computation.7 | async-start | bytes 10485760 | tf_op jit(solution)/shard_map/all_gather | solution.py:45
  10.0 256.0 %all-gather.17.cloned.1.call-start = ((), (), s32[]{:S(2)}) async-start(), calls=%async_computation.10 | async-start | bytes 1572864 | tf_op jit(solution)/shard_map/all_gather | solution.py:42
  10.6 407.7 %all-gather.15.cloned.1.call-start = ((), (), s32[]{:S(2)}) async-start(), calls=%async_computation.8 | async-start | bytes 10485760 | tf_op jit(solution)/shard_map/all_gather | solution.py:48
  11.2 42.5 %copy-start.4 = (f32[896]{0:T(1024)S(1)}, f32[896]{0:T(1024)}, u32[]{:S(2)}) copy-start(f32[896]{0:T(1024)} %param.13) | copy-start | bytes 10756
  99.9 28.9 %all-to-all-start.1 = ((bf16[2,4,64,2048]{3,2,1,0:T(8,128)(2,1)}), bf16[2,4,64,2048]{3,2,1,0:T(8,128)(2,1)S(1)}, u32[]{:S(2)}, u32[]{:S(2)}) async-start(bf16[2,4,64,2048]{3,2,1,0:T(8,128)(2,1)} %pad_maximum_fusion), calls=%async_computation.1 | async-start | bytes 4194304 | tf_op jit(solution)/shard_map/all_to_all | solution.py:67
  103.8 347.3 %reduce-scatter.5.cloned.1.call-start = ((), (), s32[]{:S(2)}) async-start(), calls=%async_computation.11 | async-start | bytes 3145728 | tf_op jit(solution)/shard_map/reduce_scatter | solution.py:105
  442.0 21.1 %reduce-scatter.3.cloned.1.call-start = ((), (), s32[]{:S(2)}) async-start(), calls=%async_computation.9 | async-start | bytes 3145728 | tf_op jit(solution)/shard_map/reduce_scatter | solution.py:85
  451.0 1.0 copy-start.1
  451.0 12.1 %copy-start.2 = (bf16[128,2048]{1,0:T(8,128)(2,1)S(1)}, bf16[128,2048]{1,0:T(8,128)(2,1)}, u32[]{:S(2)}) copy-start(bf16[128,2048]{1,0:T(8,128)(2,1)} %param.10) | copy-start | bytes 1572868
Sparse Core Ops, SparseCore 0:
  9.6 44.0 all-gather.6
  55.3 40.2 all-gather.8
  97.1 7.8 all-gather.10
  106.5 150.7 all-gather.12
  258.7 7.2 all-gather.16
  267.4 150.7 all-gather.14
  442.1 7.7 reduce-scatter.4
  452.3 10.7 reduce-scatter.2
where the time goes:
time: 473 us; the launch traced here: 472 us
  waiting for transfers between devices  383 us (81%)
  matrix products  44.2 us (9%)
  between operations  14.3 us (3%)
  other arithmetic  9.29 us (2%)
  local copies, waits for them, and re-layouts  8.74 us (2%)
  blocking collectives  7.74 us (2%)
    all_gather x1, waiting for transfers between devices, local(): lax.all_gather(out_weight, 'dp', axis=1, tiled=True)  152 us
    all_gather x1, waiting for transfers between devices, local(): lax.all_gather(query_weight, 'dp', axis=0, tiled=True)  123 us
    all_gather x1, waiting for transfers between devices, local(): lax.all_gather(value_weight, 'dp', axis=0, tiled=True)  39 us
    all_gather x1, waiting for transfers between devices, local(): lax.all_gather(key_weight, 'dp', axis=0, tiled=True)  31.8 us
    all_to_all x1, waiting for transfers between devices, local(): lax.all_to_all(stacked, 'nbr', split_axis=0, concat_axis=0, tiled=True)  24 us
  transfers between devices with their start and end apart: 9, of which 7 were waited for; matrix products, arithmetic and copies ran while one was open for 7% of the time, Pallas kernels for 0%

commit v1 on v0

--- a/solution.py
+++ b/solution.py
@@ -1,8 +1,11 @@
+import functools
 import math
 
 import jax
 import jax.numpy as jnp
 from jax import lax
+from jax.experimental import pallas as pl
+from jax.experimental.pallas import tpu as pltpu
 from jax.sharding import PartitionSpec as P
 
 HD = 128
@@ -10,15 +13,247 @@
 BLOCK = 64
 UPC = 4
 UNITS = 8
+AXES = ("groups", "dp", "nbr", "mp")
+F32 = jnp.float32
+BF16 = jnp.bfloat16
 
 
 def encode_rows(states, enc_gain):
-    widened = states.astype(jnp.float32)
+    widened = states.astype(F32)
     inverse = lax.rsqrt(jnp.mean(widened * widened, axis=-1, keepdims=True) + 1e-06)
-    return (widened * inverse * enc_gain).astype(jnp.bfloat16)
-
-
-def local(
+    return (widened * inverse * enc_gain).astype(BF16)
+
+
+def dot(a, b):
+    return jnp.dot(a, b, preferred_element_type=F32)
+
+
+def dot_t(a, b):
+    return lax.dot_general(a, b, (((1,), (1,)), ((), ())), preferred_element_type=F32)
+
+
+def take_blocks(idx_ref, kv_ref, span, cols):
+    parts = []
+    for u in range(UPC):
+        row = pl.multiple_of(idx_ref[span, u] * BLOCK, BLOCK)
+        parts.append(kv_ref[pl.ds(row, BLOCK), cols])
+    return jnp.concatenate(parts, axis=0)
+
+
+def forward_kernel(idx_ref, q_ref, kv_ref, mix_ref, att_ref):
+    span = pl.program_id(0)
+    width = q_ref.shape[1]
+    for h in range(width // HD):
+        cols = slice(h * HD, (h + 1) * HD)
+        keys = take_blocks(idx_ref, kv_ref, span, cols)
+        values = take_blocks(idx_ref, kv_ref, span, slice(width + h * HD, width + (h + 1) * HD))
+        scores = dot_t(q_ref[:, cols], keys) * (1.0 / math.sqrt(HD))
+        scores = jnp.exp(scores - jnp.max(scores, axis=-1, keepdims=True))
+        attention = scores / jnp.sum(scores, axis=-1, keepdims=True)
+        att_ref[0, h] = attention
+        mix_ref[:, cols] = dot(attention.astype(BF16), values).astype(BF16)
+
+
+def backward_kernel(idx_ref, gm_ref, kv_ref, att_ref, gq_ref):
+    span = pl.program_id(0)
+    width = gm_ref.shape[1]
+    for h in range(width // HD):
+        cols = slice(h * HD, (h + 1) * HD)
+        keys = take_blocks(idx_ref, kv_ref, span, cols)
+        values = take_blocks(idx_ref, kv_ref, span, slice(width + h * HD, width + (h + 1) * HD))
+        grad_attention = dot_t(gm_ref[:, cols], values)
+        attention = att_ref[0, h]
+        inner = jnp.sum(attention * grad_attention, axis=-1, keepdims=True)
+        grad_scores = attention * (grad_attention - inner) * (1.0 / math.sqrt(HD))
+        gq_ref[:, cols] = dot(grad_scores.astype(BF16), keys).astype(BF16)
+
+
+def attention_specs(kv, width, heads):
+    row = pl.BlockSpec((SPAN, width), lambda i, idx: (i, 0))
+    bank = pl.BlockSpec(kv.shape, lambda i, idx: (0, 0))
+    att = pl.BlockSpec((1, heads, SPAN, UPC * BLOCK), lambda i, idx: (i, 0, 0, 0))
+    return row, bank, att
+
+
+def attention_forward(idx, q, kv):
+    tokens, width = q.shape
+    heads, spans = width // HD, tokens // SPAN
+    row, bank, att = attention_specs(kv, width, heads)
+    return pl.pallas_call(
+        forward_kernel,
+        grid_spec=pltpu.PrefetchScalarGridSpec(
+            num_scalar_prefetch=1, grid=(spans,), in_specs=[row, bank], out_specs=[row, att]
+        ),
+        out_shape=(
+            jax.ShapeDtypeStruct((tokens, width), BF16),
+            jax.ShapeDtypeStruct((spans, heads, SPAN, UPC * BLOCK), F32),
+        ),
+        compiler_params=pltpu.CompilerParams(vmem_limit_bytes=32 << 20),
+        name="attention_forward",
+    )(idx, q, kv)
+
+
+def attention_backward(idx, gm, kv, att):
+    tokens, width = gm.shape
+    heads, spans = width // HD, tokens // SPAN
+    row, bank, att_spec = attention_specs(kv, width, heads)
+    return pl.pallas_call(
+        backward_kernel,
+        grid_spec=pltpu.PrefetchScalarGridSpec(
+            num_scalar_prefetch=1, grid=(spans,), in_specs=[row, bank, att_spec], out_specs=row
+        ),
+        out_shape=jax.ShapeDtypeStruct((tokens, width), BF16),
+        compiler_params=pltpu.CompilerParams(vmem_limit_bytes=32 << 20),
+        name="attention_backward",
+    )(idx, gm, kv, att)
+
+
+def flat(y, z, x, m):
+    return ((y * 4 + z) * 2 + x) * 2 + m
+
+
+def permutation(move):
+    pairs = []
+    for y in range(2):
+        for z in range(4):
+            for x in range(2):
+                for m in range(2):
+                    pairs.append((flat(y, z, x, m), flat(*move(y, z, x, m))))
+    return pairs
+
+
+RING = (0, 1, 3, 2)
+NEXT = {RING[i]: RING[(i + 1) % 4] for i in range(4)}
+PREV = {RING[i]: RING[(i + 3) % 4] for i in range(4)}
+FIRST = permutation(lambda y, z, x, m: (y, z, 1 - x, m) if m == 0 else (1 - y, z, x, m))
+SECOND = permutation(lambda y, z, x, m: (1 - y, z, x, m) if m == 0 else (y, z, 1 - x, m))
+CORE = permutation(lambda y, z, x, m: (y, z, x, 1 - m))
+UP = permutation(lambda y, z, x, m: (y, NEXT[z], x, m))
+DOWN = permutation(lambda y, z, x, m: (y, PREV[z], x, m))
+
+
+def move(array, pairs):
+    return lax.ppermute(array, AXES, pairs)
+
+
+def plane_gather(mine):
+    first = move(mine, FIRST)
+    far = move(jnp.stack((mine, first)), SECOND)
+    return jnp.stack((mine, far[0], first, far[1]))
+
+
+def core_swap(slots):
+    other = move(slots, CORE)
+    return jnp.stack((other[0], other[2], other[1], other[3]))
+
+
+def plane_reduce(own_half, other_half):
+    rows = own_half.shape[0] // 4
+    total = own_half.reshape(4, rows, -1) + core_swap(
+        other_half.astype(BF16).reshape(4, rows, -1)
+    ).astype(F32)
+    pair = total[:2] + move(total[2:].astype(BF16), FIRST).astype(F32)
+    return pair[0] + move(pair[1].astype(BF16), SECOND).astype(F32)
+
+
+def ring_gather(mine):
+    up = move(mine, UP)
+    down = move(mine, DOWN)
+    far = move(up, UP)
+    return up, down, far
+
+
+def local_plane(
+    hidden,
+    grad_out,
+    database,
+    enc_gain,
+    query_weight,
+    key_weight,
+    value_weight,
+    out_weight,
+    block_ids,
+    owners,
+):
+    y, z, x, m = (lax.axis_index(a) for a in AXES)
+    chip = y * 2 + x
+    rows, half = hidden.shape
+    width = query_weight.shape[1] // 4
+    depth = query_weight.shape[0]
+    nxt = jnp.array([NEXT[i] for i in range(4)], jnp.int32)[z]
+    prv = jnp.array([PREV[i] for i in range(4)], jnp.int32)[z]
+    sources = (z, prv, nxt, 3 - z)
+
+    wq = lax.dynamic_slice_in_dim(query_weight, chip * width, width, 1)
+    wkv = jnp.concatenate(
+        (
+            lax.dynamic_slice_in_dim(key_weight, chip * width, width, 1),
+            lax.dynamic_slice_in_dim(value_weight, chip * width, width, 1),
+        ),
+        axis=1,
+    )
+    wo = lax.dynamic_slice_in_dim(out_weight, chip * width, width, 0)
+    wq_parts = (wq,) + ring_gather(wq)
+    wkv_parts = (wkv,) + ring_gather(wkv)
+    wo_parts = (wo,) + ring_gather(wo)
+
+    blocks = database.shape[0] // 2
+    encoded = encode_rows(lax.dynamic_slice_in_dim(database, m * blocks, blocks, 0), enc_gain)
+    encoded = encoded.reshape(blocks * BLOCK, -1)
+    h_own = plane_gather(hidden)
+    h_other = core_swap(h_own).reshape(4 * rows, half)
+    h_own = h_own.reshape(4 * rows, half)
+    e_own = plane_gather(encoded)
+    e_other = core_swap(e_own)
+    e_all = jnp.concatenate((e_own, e_other)).reshape(8 * blocks * BLOCK, -1)
+    g_own = plane_gather(grad_out)
+    g_other = core_swap(g_own).reshape(4 * rows, half)
+    g_own = g_own.reshape(4 * rows, half)
+
+    codes = lax.all_gather(jnp.stack((owners, block_ids)), ("groups", "nbr"), axis=0)
+    slot = jnp.arange(4, dtype=jnp.int32)
+    hi, lo = slot // 2, slot % 2
+    slot_y = jnp.where(m == 0, lo, hi)
+    slot_x = jnp.where(m == 0, hi, lo)
+    codes = codes[(slot_y ^ y) * 2 + (slot_x ^ x)]
+    own_of, id_of = codes[:, 0], codes[:, 1]
+    rel_x = own_of ^ x
+    rel_y = slot_y[:, None, None]
+    bank = jnp.where(m == 0, rel_x * 2 + rel_y, rel_y * 2 + rel_x)
+    idx = ((id_of // blocks) ^ m) * (4 * blocks) + bank * blocks + id_of % blocks
+    idx = idx.reshape(-1, UPC)
+
+    def assemble(parts, axis, places):
+        shape = list(parts[0].shape)
+        step = shape[axis]
+        shape[axis] = 4 * step
+        whole = jnp.zeros(shape, BF16)
+        for part, place in zip(parts, places):
+            whole = lax.dynamic_update_slice_in_dim(whole, part, place * step, axis)
+        return whole
+
+    halves = tuple(s ^ (2 * m) for s in sources)
+    wq_all = assemble(wq_parts, 0, halves)
+    wkv_all = assemble(wkv_parts, 0, sources)
+    wo_all = assemble(wo_parts, 1, halves)
+    wq_own, wq_other = wq_all[: 2 * depth], wq_all[2 * depth :]
+    wo_own, wo_other = wo_all[:, : 2 * depth], wo_all[:, 2 * depth :]
+
+    queries = (dot(h_own, wq_own) + dot(h_other, wq_other)).astype(BF16)
+    kv = dot(e_all, wkv_all).astype(BF16)
+    mixture, attention = attention_forward(idx, queries, kv)
+
+    summed = plane_reduce(dot(mixture, wo_own), dot(mixture, wo_other))
+    output = (hidden.astype(F32) + summed).astype(BF16)
+
+    grad_mixture = (dot_t(g_own, wo_own) + dot_t(g_other, wo_other)).astype(BF16)
+    grad_queries = attention_backward(idx, grad_mixture, kv, attention)
+    grad_sum = plane_reduce(dot_t(grad_queries, wq_own), dot_t(grad_queries, wq_other))
+    grad_hidden = (grad_out.astype(F32) + grad_sum).astype(BF16)
+    return (output, grad_hidden)
+
+
+def local_any(
     hidden,
     grad_out,
     database,
@@ -121,4 +356,6 @@
         P(("groups", "dp", "nbr"), None),
     )
     out_specs = (P(("groups", "dp", "nbr"), "mp"), P(("groups", "dp", "nbr"), "mp"))
+    sizes = tuple(mesh.shape[a] for a in AXES)
+    local = local_plane if sizes == (2, 4, 2, 2) else local_any
     return jax.shard_map(local, mesh=mesh, in_specs=in_specs, out_specs=out_specs, check_vma=False)

time: 473 us -> 177 us (0.37)
  waiting for transfers between devices: 383 us -> 74 us
  matrix products: 44.2 us -> 13.1 us
  starting transfers between devices: 4.32 us -> 30.9 us
  Pallas kernels: 0 us -> 12.4 us
  local copies, waits for them, and re-layouts: 8.74 us -> 19.3 us
  between operations: 14.3 us -> 3.74 us
  blocking collectives: 7.74 us -> 14.7 us
    all_gather x6 -> x0, waiting for transfers between devices: 347 us -> none  [the longest x1 152 us: local(): lax.all_gather(out_weight, 'dp', axis=1, tiled=True)]
    ppermute x0 -> x24, waiting for transfers between devices: none -> 74 us  [move(): return lax.ppermute(array, AXES, pairs)]
    dot_general x10 -> x9, matrix products: 44.2 us -> 13.1 us  [the longest x5 7.67 us: dot(): return jnp.dot(a, b, preferred_element_type=F32)]
    ppermute x0 -> x24, starting transfers between devices: none -> 30.9 us  [move(): return lax.ppermute(array, AXES, pairs)]
    all_to_all x1 -> x0, waiting for transfers between devices: 24 us -> none  [local(): lax.all_to_all(stacked, 'nbr', split_axis=0, concat_axis=0, tiled=True)]
    all_gather x0 -> x1, blocking collectives: none -> 14.7 us  [local_plane(): lax.all_gather(jnp.stack((owners, block_ids)), ('groups', 'nbr'), axis=0)]
    pallas_call x0 -> x2, Pallas kernels: none -> 12.4 us  [the longest x1 7.01 us: attention_forward(): pl.pallas_call(forward_kernel, grid_spec=pltpu.PrefetchScalarGridSpec(num...]
    dynamic_update_slice x0 -> x11, local copies, waits for them, and re-layouts: none -> 11.8 us  [assemble(): whole = lax.dynamic_update_slice_in_dim(whole, part, place * step, axis)]
  transfers between devices with their start and end apart: 9 -> 24, of which waited for: 7 -> 11; matrix products, arithmetic and copies ran while one was open for 7% -> 20% of each run, Pallas kernels for 0% -> 0%
where the time goes in v1:
time: 177 us
  waiting for transfers between devices  74 us (42%)
  starting transfers between devices  30.9 us (17%)
  local copies, waits for them, and re-layouts  19.3 us (11%)
  blocking collectives  14.7 us (8%)
  matrix products  13.1 us (7%)
  Pallas kernels  12.4 us (7%)
  other arithmetic  8.61 us (5%)
  between operations  3.74 us (2%)
    ppermute x24, waiting for transfers between devices, move(): return lax.ppermute(array, AXES, pairs)  74 us
    ppermute x24, starting transfers between devices, move(): return lax.ppermute(array, AXES, pairs)  30.9 us
    all_gather x1, blocking collectives, local_plane(): lax.all_gather(jnp.stack((owners, block_ids)), ('groups', 'nbr'), axis=0)  14.7 us
    dynamic_update_slice x11, local copies, waits for them, and re-layouts, assemble(): whole = lax.dynamic_update_slice_in_dim(whole, part, place * step, axis)  11.8 us
    dot_general x5, matrix products, dot(): return jnp.dot(a, b, preferred_element_type=F32)  7.67 us
    pallas_call x1, Pallas kernels, attention_forward(): pl.pallas_call(forward_kernel, grid_spec=pltpu.PrefetchScalarGridSpec(num...  7.01 us
    pallas_call x1, Pallas kernels, attention_backward(): pl.pallas_call(backward_kernel, grid_spec=pltpu.PrefetchScalarGridSpec(nu...  5.43 us
    dot_general x4, matrix products, dot_t(): lax.dot_general(a, b, (((1,), (1,)), ((), ())), preferred_element_type=F32)  5.42 us
  transfers between devices with their start and end apart: 24, of which 11 were waited for; matrix products, arithmetic and copies ran while one was open for 20% of the time, Pallas kernels for 0%

profile of v1, /device:TPU:0, one launch (start us, length us, event | category | flops | bytes accessed | tf_op | source)
XLA Modules:
  0.0 176.9 jit_solution(12809779824796851075)
XLA Ops:
  2.5 3.0 %collective-permute-start.9 = (bf16[224,512]{1,0:T(8,128)(2,1)}, bf16[224,512]{1,0:T(8,128)(2,1)}, u32[]{:S(2)}, u32[]{:S(2)}) collective-permute-start(bf16[224,512]{1,0:T(8,128)(2,1)} %get-tuple-element.33), channel_id=1, source_target_pairs={{0,4},{1,5},{2,6},{3,7},{4,12},{5,13},{6,14},{7,15},{8,0},{9,1},{1... | collective-permute-start | bytes 688136 | tf_op jit(solution)/shard_map/ppermute | solution.py:136
  6.5 1.6 broadcast_in_dim.15
  8.1 2.2 %constant_dynamic-update-slice_fusion.7 = (bf16[256,4096]{1,0:T(8,128)(2,1)}, bf16[256,1024]{1,0:T(8,128)(2,1)}) fusion(bf16[256,4096]{1,0:T(8,128)(2,1)} %broadcast_in_dim.15, s32[]{:T(128)S(6)} %select_n.173, bf16[1024,1024]{1,0:T(8,128)(2,1)} %param.19, s32[]{:T(128)S(6)} %select_n.172), kind=kLoop, calls=%fused_computation.68 | loop fusion | bytes 1572872 | tf_op jit(solution)/shard_map/dynamic_update_slice | solution.py:232
  10.2 1.6 collective-permute-start.12
  14.4 14.7 %all-gather = s32[8,2,4]{2,1,0:T(2,128)S(1)} all-gather(s32[2,2,4]{2,1,0:T(2,128)S(1)} %pad_add_fusion), channel_id=2, replica_groups=mesh['groups'=2,'dp'=4,'nbr'=2,'mp'=2] {'groups','nbr'}, dimensions={0}, use_global_device_ids=true | all-gather | bytes 320 | tf_op jit(solution)/shard_map/all_gather | solution.py:213
  30.2 1.9 %constant_dynamic-update-slice_fusion.15 = (bf16[4096,256]{1,0:T(8,128)(2,1)S(1)}, bf16[1024,256]{1,0:T(8,128)(2,1)}) fusion(bf16[4096,256]{1,0:T(8,128)(2,1)S(1)} %broadcast_in_dim.6, s32[]{:T(128)S(6)} %select_n.173, bf16[1024,1024]{1,0:T(8,128)(2,1)} %param.16, s32[]{:T(128)S(6)} %select_n.172), kind=kLoop, calls=%fused_computation.79 | loop fusion | bytes 1572872 | tf_op jit(solution)/shard_map/dynamic_update_slice | solution.py:232
  36.8 1.7 collective-permute-start.13
  38.6 1.6 constant_dynamic-update-slice_fusion.10
  41.5 1.6 constant_dynamic-update-slice_fusion.9
  43.2 2.9 %collective-permute-start.2 = (bf16[1024,256]{1,0:T(8,128)(2,1)}, bf16[1024,256]{1,0:T(8,128)(2,1)S(1)}, u32[]{:S(2)}, u32[]{:S(2)}) collective-permute-start(bf16[1024,256]{1,0:T(8,128)(2,1)} %get-tuple-element.9), channel_id=1, source_target_pairs={{0,4},{1,5},{2,6},{3,7},{4,12},{5,13},{6,14},{7,15},{8,0},{9,1},{1... | collective-permute-start | bytes 1572872 | tf_op jit(solution)/shard_map/ppermute | solution.py:136
  46.1 10.5 %collective-permute-done.11 = bf16[224,512]{1,0:T(8,128)(2,1)S(1)} collective-permute-done((bf16[224,512]{1,0:T(8,128)(2,1)}, bf16[224,512]{1,0:T(8,128)(2,1)S(1)}, u32[]{:S(2)}, u32[]{:S(2)}) %collective-permute-start.11) | collective-permute-done | bytes 229408 | tf_op jit(solution)/shard_map/ppermute | solution.py:136
  56.6 4.1 %collective-permute-start.3 = (bf16[1024,256]{1,0:T(8,128)(2,1)S(1)}, bf16[1024,256]{1,0:T(8,128)(2,1)S(1)}, u32[]{:S(2)}, u32[]{:S(2)}) collective-permute-start(bf16[1024,256]{1,0:T(8,128)(2,1)S(1)} %copy-done.5), channel_id=1, source_target_pairs={{0,8},{1,9},{2,10},{3,11},{4,0},{5,1},{6,2},{7,3},{8,12},{9,13},{1... | collective-permute-start | bytes 1572872 | tf_op jit(solution)/shard_map/ppermute | solution.py:136
  61.4 1.5 collective-permute-start
  64.7 1.9 %constant_dynamic-update-slice_fusion.6 = bf16[256,4096]{1,0:T(8,128)(2,1)} fusion(bf16[256,4096]{1,0:T(8,128)(2,1)} %get-tuple-element.6, bf16[256,1024]{1,0:T(8,128)(2,1)} %collective-permute-done.12, s32[]{:T(128)S(6)} %select_n.175), kind=kLoop, calls=%fused_computation.67 | loop fusion | bytes 1048580 | tf_op jit(solution)/shard_map/dynamic_update_slice | solution.py:232
  66.6 4.8 %collective-permute-done.2 = bf16[1024,256]{1,0:T(8,128)(2,1)S(1)} collective-permute-done((bf16[1024,256]{1,0:T(8,128)(2,1)}, bf16[1024,256]{1,0:T(8,128)(2,1)S(1)}, u32[]{:S(2)}, u32[]{:S(2)}) %collective-permute-start.2) | collective-permute-done | bytes 524320 | tf_op jit(solution)/shard_map/ppermute | solution.py:136
  73.1 3.2 %collective-permute-done = bf16[128,2048]{1,0:T(8,128)(2,1)S(1)} collective-permute-done((bf16[128,2048]{1,0:T(8,128)(2,1)S(1)}, bf16[128,2048]{1,0:T(8,128)(2,1)S(1)}, u32[]{:S(2)}, u32[]{:S(2)}) %collective-permute-start) | collective-permute-done | bytes 524320 | tf_op jit(solution)/shard_map/ppermute | solution.py:136
  77.9 4.6 %collective-permute-done.3 = bf16[1024,256]{1,0:T(8,128)(2,1)S(1)} collective-permute-done((bf16[1024,256]{1,0:T(8,128)(2,1)S(1)}, bf16[1024,256]{1,0:T(8,128)(2,1)S(1)}, u32[]{:S(2)}, u32[]{:S(2)}) %collective-permute-start.3) | collective-permute-done | bytes 524320 | tf_op jit(solution)/shard_map/ppermute | solution.py:136
  84.1 6.5 %collective-permute-done.14 = bf16[256,1024]{1,0:T(8,128)(2,1)S(1)} collective-permute-done((bf16[256,1024]{1,0:T(8,128)(2,1)}, bf16[256,1024]{1,0:T(8,128)(2,1)S(1)}, u32[]{:S(2)}, u32[]{:S(2)}) %collective-permute-start.14) | collective-permute-done | bytes 524320 | tf_op jit(solution)/shard_map/ppermute | solution.py:136
  91.4 10.1 %collective-permute-done.4 = bf16[1024,256]{1,0:T(8,128)(2,1)S(1)} collective-permute-done((bf16[1024,256]{1,0:T(8,128)(2,1)S(1)}, bf16[1024,256]{1,0:T(8,128)(2,1)S(1)}, u32[]{:S(2)}, u32[]{:S(2)}) %collective-permute-start.4) | collective-permute-done | bytes 524320 | tf_op jit(solution)/shard_map/ppermute | solution.py:136
  106.1 2.3 %convolution_convert_fusion.2.kv_ref = bf16[2048,512]{1,0:T(8,128)(2,1)S(1)} fusion(bf16[2048,896]{1,0:T(8,128)(2,1)S(1)} %bitcast.78, bf16[896,512]{1,0:T(8,128)(2,1)S(1)} %copy-done.4), kind=kOutput, calls=%fused_computation.5 | convolution fusion | flops 1880096768 | bytes 6684672 | tf_op jit(solution)/shard_map/dot_general | solution.py:28
  109.2 2.0 %fusion.8 = f32[512,256]{1,0:T(8,128)S(1)} fusion(bf16[512,2048]{1,0:T(8,128)(2,1)S(1)} %bitcast.72, bf16[256,4096]{1,0:T(8,128)(2,1)} %constant_dynamic-update-slice_fusion.4), kind=kOutput, calls=%fused_computation.33 | convolution fusion | flops 536870912 | bytes 3670016 | tf_op jit(solution)/shard_map/dot_general | solution.py:32
  111.2 2.0 %fusion.1.gm_ref = bf16[512,256]{1,0:T(8,128)(2,1)S(1)} fusion(f32[512,256]{1,0:T(8,128)S(1)} %fusion.8, bf16[512,2048]{1,0:T(8,128)(2,1)S(1)} %bitcast.71, bf16[256,4096]{1,0:T(8,128)(2,1)} %constant_dynamic-update-slice_fusion.4), kind=kOutput, calls=%fused_computation.18 | convolution fusion | flops 537133056 | bytes 3932160 | tf_op jit(solution)/shard_map/dot_general | solution.py:32
  115.2 7.0 %attention_forward.1 = (bf16[512,256]{1,0:T(8,128)(2,1)S(1)}, f32[8,2,64,256]{3,2,1,0:T(8,128)S(1)}) custom-call(s32[8,4]{1,0:T(8,128)S(1)} %fusion.28.idx_ref, bf16[512,256]{1,0:T(8,128)(2,1)S(1)} %fusion.q_ref, bf16[2048,512]{1,0:T(8,128)(2,1)S(1)} %convolution_convert_fusion.2.kv_ref), custom_call_target="tpu_custom_call" | custom-call | tf_op jit(solution)/shard_map/attention_forward/pallas_call | solution.py:82
  122.2 5.4 %attention_backward.1 = bf16[512,256]{1,0:T(8,128)(2,1)S(1)} custom-call(s32[8,4]{1,0:T(8,128)S(1)} %fusion.28.idx_ref, bf16[512,256]{1,0:T(8,128)(2,1)S(1)} %fusion.1.gm_ref, bf16[2048,512]{1,0:T(8,128)(2,1)S(1)} %convolution_convert_fusion.2.kv_ref, f32[8,2,64,256]{3,2,1,0:T(8,128)S(1)} %get-tuple-element.5.att_ref), custom_call_target="tpu_custom_call" | custom-call | tf_op jit(solution)/shard_map/attention_backward/pallas_call | solution.py:100
  128.6 1.9 %convolution_convert_fusion.1 = bf16[512,2048]{1,0:T(8,128)(2,1)S(1)} fusion(bf16[512,256]{1,0:T(8,128)(2,1)S(1)} %get-tuple-element.4, bf16[256,4096]{1,0:T(8,128)(2,1)} %constant_dynamic-update-slice_fusion.4), kind=kOutput, calls=%fused_computation.4 | convolution fusion | flops 537919488 | bytes 3407872 | tf_op jit(solution)/shard_map/dot_general | solution.py:28
  131.7 1.9 %fusion.12 = f32[512,2048]{1,0:T(8,128)S(1)} fusion(bf16[512,256]{1,0:T(8,128)(2,1)S(1)} %get-tuple-element.4, bf16[256,4096]{1,0:T(8,128)(2,1)} %constant_dynamic-update-slice_fusion.4), kind=kOutput, calls=%fused_computation.37 | convolution fusion | flops 536870912 | bytes 5505024 | tf_op jit(solution)/shard_map/dot_general | solution.py:28
  134.5 1.6 collective-permute-start.22
  138.1 11.3 %collective-permute-done.22 = bf16[2,128,2048]{2,1,0:T(8,128)(2,1)S(1)} collective-permute-done((bf16[2,128,2048]{2,1,0:T(8,128)(2,1)S(1)}, bf16[2,128,2048]{2,1,0:T(8,128)(2,1)S(1)}, u32[]{:S(2)}, u32[]{:S(2)}) %collective-permute-start.22) | collective-permute-done | bytes 1048608 | tf_op jit(solution)/shard_map/ppermute | solution.py:136
  149.8 1.6 collective-permute-start.23
  151.4 14.8 %collective-permute-done.16 = bf16[2,128,2048]{2,1,0:T(8,128)(2,1)S(1)} collective-permute-done((bf16[2,128,2048]{2,1,0:T(8,128)(2,1)S(1)}, bf16[2,128,2048]{2,1,0:T(8,128)(2,1)S(1)}, u32[]{:S(2)}, u32[]{:S(2)}) %collective-permute-start.16) | collective-permute-done | bytes 1048608 | tf_op jit(solution)/shard_map/ppermute | solution.py:136
  166.6 1.6 collective-permute-start.17
  169.2 6.7 %collective-permute-done.17 = bf16[128,2048]{1,0:T(8,128)(2,1)S(1)} collective-permute-done((bf16[128,2048]{1,0:T(8,128)(2,1)S(1)}, bf16[128,2048]{1,0:T(8,128)(2,1)S(1)}, u32[]{:S(2)}, u32[]{:S(2)}) %collective-permute-start.17) | collective-permute-done | bytes 524320 | tf_op jit(solution)/shard_map/ppermute | solution.py:136
  (117 shorter events, 33.0 us)
Async XLA Ops:
  1.7 10.1 %copy-start = (bf16[128,2048]{1,0:T(8,128)(2,1)S(1)}, bf16[128,2048]{1,0:T(8,128)(2,1)}, u32[]{:S(2)}) copy-start(bf16[128,2048]{1,0:T(8,128)(2,1)} %param.13) | copy-start | bytes 1572868
  1.7 11.6 %copy-start.2 = (bf16[8,64,896]{2,1,0:T(8,128)(2,1)S(1)}, bf16[8,64,896]{2,1,0:T(8,128)(2,1)}, u32[]{:S(2)}) copy-start(bf16[8,64,896]{2,1,0:T(8,128)(2,1)} %param.14) | copy-start | bytes 2752516
  2.4 11.2 %copy-start.3 = (bf16[896,512]{1,0:T(8,128)(2,1)}, bf16[896,512]{1,0:T(8,128)(2,1)S(1)}, u32[]{:S(2)}) copy-start(bf16[896,512]{1,0:T(8,128)(2,1)S(1)} %get-tuple-element.34) | copy-start | bytes 2752516
  2.4 11.0 %copy-start.7 = (f32[896]{0:T(1024)S(1)}, f32[896]{0:T(1024)}, u32[]{:S(2)}) copy-start(f32[896]{0:T(1024)} %param.15) | copy-start | bytes 10756
  2.5 34.4 %collective-permute-start.9 = (bf16[224,512]{1,0:T(8,128)(2,1)}, bf16[224,512]{1,0:T(8,128)(2,1)}, u32[]{:S(2)}, u32[]{:S(2)}) collective-permute-start(bf16[224,512]{1,0:T(8,128)(2,1)} %get-tuple-element.33), channel_id=1, source_target_pairs={{0,4},{1,5},{2,6},{3,7},{4,12},{5,13},{6,14},{7,15},{8,0},{9,1},{1... | collective-permute-start | bytes 688136 | tf_op jit(solution)/shard_map/ppermute | solution.py:136
  5.5 34.7 %collective-permute-start.10 = (bf16[224,512]{1,0:T(8,128)(2,1)}, bf16[224,512]{1,0:T(8,128)(2,1)}, u32[]{:S(2)}, u32[]{:S(2)}) collective-permute-start(bf16[224,512]{1,0:T(8,128)(2,1)} %get-tuple-element.33), channel_id=1, source_target_pairs={{0,8},{1,9},{2,10},{3,11},{4,0},{5,1},{6,2},{7,3},{8,12},{9,13},{1... | collective-permute-start | bytes 688136 | tf_op jit(solution)/shard_map/ppermute | solution.py:136
  6.5 7.8 %copy-start.9 = (s32[2,4]{1,0:T(2,128)S(1)}, s32[2,4]{1,0:T(2,128)}, u32[]{:S(2)}) copy-start(s32[2,4]{1,0:T(2,128)} %param.21) | copy-start | bytes 100
  10.2 53.9 %collective-permute-start.12 = (bf16[256,1024]{1,0:T(8,128)(2,1)}, bf16[256,1024]{1,0:T(8,128)(2,1)}, u32[]{:S(2)}, u32[]{:S(2)}) collective-permute-start(bf16[256,1024]{1,0:T(8,128)(2,1)} %get-tuple-element.7), channel_id=1, source_target_pairs={{0,4},{1,5},{2,6},{3,7},{4,12},{5,13},{6,14},{7,15},{8,0},{9,1},{1... | collective-permute-start | bytes 1572872 | tf_op jit(solution)/shard_map/ppermute | solution.py:136
  11.8 49.6 %collective-permute-start.18 = (bf16[128,2048]{1,0:T(8,128)(2,1)S(1)}, bf16[128,2048]{1,0:T(8,128)(2,1)}, u32[]{:S(2)}, u32[]{:S(2)}) collective-permute-start(bf16[128,2048]{1,0:T(8,128)(2,1)S(1)} %copy-done), channel_id=1, source_target_pairs={{0,2},{1,17},{2,0},{3,19},{4,6},{5,21},{6,4},{7,23},{8,10},{9,25},... | collective-permute-start | bytes 1572872 | tf_op jit(solution)/shard_map/ppermute | solution.py:136
  13.7 29.5 %collective-permute-start.6 = (bf16[256,896]{1,0:T(8,128)(2,1)S(1)}, bf16[256,896]{1,0:T(8,128)(2,1)S(1)}, u32[]{:S(2)}, u32[]{:S(2)}) collective-permute-start(bf16[256,896]{1,0:T(8,128)(2,1)S(1)} %bitcast.60), channel_id=1, source_target_pairs={{0,2},{1,17},{2,0},{3,19},{4,6},{5,21},{6,4},{7,23},{8,10},{9,25},... | collective-permute-start | bytes 1376264 | tf_op jit(solution)/shard_map/ppermute | solution.py:136
  36.8 19.8 %copy-start.5 = (bf16[1024,256]{1,0:T(8,128)(2,1)S(1)}, bf16[1024,256]{1,0:T(8,128)(2,1)}, u32[]{:S(2)}) copy-start(bf16[1024,256]{1,0:T(8,128)(2,1)} %get-tuple-element.9) | copy-start | bytes 1572868
  36.8 24.6 %copy-start.1 = (bf16[128,2048]{1,0:T(8,128)(2,1)S(1)}, bf16[128,2048]{1,0:T(8,128)(2,1)}, u32[]{:S(2)}) copy-start(bf16[128,2048]{1,0:T(8,128)(2,1)} %param.12) | copy-start | bytes 1572868
  36.8 34.6 %collective-permute-start.13 = (bf16[256,1024]{1,0:T(8,128)(2,1)}, bf16[256,1024]{1,0:T(8,128)(2,1)S(1)}, u32[]{:S(2)}, u32[]{:S(2)}) collective-permute-start(bf16[256,1024]{1,0:T(8,128)(2,1)} %get-tuple-element.7), channel_id=1, source_target_pairs={{0,8},{1,9},{2,10},{3,11},{4,0},{5,1},{6,2},{7,3},{8,12},{9,13},{1... | collective-permute-start | bytes 1572872 | tf_op jit(solution)/shard_map/ppermute | solution.py:136
  40.2 16.4 %collective-permute-start.11 = (bf16[224,512]{1,0:T(8,128)(2,1)}, bf16[224,512]{1,0:T(8,128)(2,1)S(1)}, u32[]{:S(2)}, u32[]{:S(2)}) collective-permute-start(bf16[224,512]{1,0:T(8,128)(2,1)} %collective-permute-done.9), channel_id=1, source_target_pairs={{0,4},{1,5},{2,6},{3,7},{4,12},{5,13},{6,14},{7,15},{8,0},{9,1},{1... | collective-permute-start | bytes 688136 | tf_op jit(solution)/shard_map/ppermute | solution.py:136
  43.2 28.2 %collective-permute-start.2 = (bf16[1024,256]{1,0:T(8,128)(2,1)}, bf16[1024,256]{1,0:T(8,128)(2,1)S(1)}, u32[]{:S(2)}, u32[]{:S(2)}) collective-permute-start(bf16[1024,256]{1,0:T(8,128)(2,1)} %get-tuple-element.9), channel_id=1, source_target_pairs={{0,4},{1,5},{2,6},{3,7},{4,12},{5,13},{6,14},{7,15},{8,0},{9,1},{1... | collective-permute-start | bytes 1572872 | tf_op jit(solution)/shard_map/ppermute | solution.py:136
  56.6 25.9 %collective-permute-start.3 = (bf16[1024,256]{1,0:T(8,128)(2,1)S(1)}, bf16[1024,256]{1,0:T(8,128)(2,1)S(1)}, u32[]{:S(2)}, u32[]{:S(2)}) collective-permute-start(bf16[1024,256]{1,0:T(8,128)(2,1)S(1)} %copy-done.5), channel_id=1, source_target_pairs={{0,8},{1,9},{2,10},{3,11},{4,0},{5,1},{6,2},{7,3},{8,12},{9,13},{1... | collective-permute-start | bytes 1572872 | tf_op jit(solution)/shard_map/ppermute | solution.py:136
  61.4 14.9 %collective-permute-start = (bf16[128,2048]{1,0:T(8,128)(2,1)S(1)}, bf16[128,2048]{1,0:T(8,128)(2,1)S(1)}, u32[]{:S(2)}, u32[]{:S(2)}) collective-permute-start(bf16[128,2048]{1,0:T(8,128)(2,1)S(1)} %copy-done.1), channel_id=1, source_target_pairs={{0,2},{1,17},{2,0},{3,19},{4,6},{5,21},{6,4},{7,23},{8,10},{9,25},... | collective-permute-start | bytes 1572872 | tf_op jit(solution)/shard_map/ppermute | solution.py:136
  64.1 37.4 %collective-permute-start.7 = (bf16[2,256,896]{2,1,0:T(8,128)(2,1)S(1)}, bf16[2,256,896]{2,1,0:T(8,128)(2,1)S(1)}, u32[]{:S(2)}, u32[]{:S(2)}) collective-permute-start(bf16[2,256,896]{2,1,0:T(8,128)(2,1)S(1)} %pad_maximum_fusion.7), channel_id=1, source_target_pairs={{0,16},{1,3},{2,18},{3,1},{4,20},{5,7},{6,22},{7,5},{8,24},{9,11},... | collective-permute-start | bytes 2752520 | tf_op jit(solution)/shard_map/ppermute | solution.py:136
  71.4 19.2 %collective-permute-start.14 = (bf16[256,1024]{1,0:T(8,128)(2,1)}, bf16[256,1024]{1,0:T(8,128)(2,1)S(1)}, u32[]{:S(2)}, u32[]{:S(2)}) collective-permute-start(bf16[256,1024]{1,0:T(8,128)(2,1)} %collective-permute-done.12), channel_id=1, source_target_pairs={{0,4},{1,5},{2,6},{3,7},{4,12},{5,13},{6,14},{7,15},{8,0},{9,1},{1... | collective-permute-start | bytes 1572872 | tf_op jit(solution)/shard_map/ppermute | solution.py:136
  71.4 30.1 %collective-permute-start.4 = (bf16[1024,256]{1,0:T(8,128)(2,1)S(1)}, bf16[1024,256]{1,0:T(8,128)(2,1)S(1)}, u32[]{:S(2)}, u32[]{:S(2)}) collective-permute-start(bf16[1024,256]{1,0:T(8,128)(2,1)S(1)} %collective-permute-done.2), channel_id=1, source_target_pairs={{0,4},{1,5},{2,6},{3,7},{4,12},{5,13},{6,14},{7,15},{8,0},{9,1},{1... | collective-permute-start | bytes 1572872 | tf_op jit(solution)/shard_map/ppermute | solution.py:136
  76.3 25.9 %collective-permute-start.19 = (bf16[2,128,2048]{2,1,0:T(8,128)(2,1)S(1)}, bf16[2,128,2048]{2,1,0:T(8,128)(2,1)S(1)}, u32[]{:S(2)}, u32[]{:S(2)}) collective-permute-start(bf16[2,128,2048]{2,1,0:T(8,128)(2,1)S(1)} %pad_maximum_fusion.6), channel_id=1, source_target_pairs={{0,16},{1,3},{2,18},{3,1},{4,20},{5,7},{6,22},{7,5},{8,24},{9,11},... | collective-permute-start | bytes 3145736 | tf_op jit(solution)/shard_map/ppermute | solution.py:136
  77.8 23.7 %copy-start.6 = (bf16[8,256,896]{2,1,0:T(8,128)(2,1)S(1)}, bf16[8,256,896]{2,1,0:T(8,128)(2,1)}, u32[]{:S(2)}) copy-start(bf16[8,256,896]{2,1,0:T(8,128)(2,1)} %constant_dynamic-update-slice_fusion.3) | copy-start | bytes 11010052
  82.5 21.6 %collective-permute-start.1 = (bf16[2,128,2048]{2,1,0:T(8,128)(2,1)S(1)}, bf16[2,128,2048]{2,1,0:T(8,128)(2,1)S(1)}, u32[]{:S(2)}, u32[]{:S(2)}) collective-permute-start(bf16[2,128,2048]{2,1,0:T(8,128)(2,1)S(1)} %pad_maximum_fusion.5), channel_id=1, source_target_pairs={{0,16},{1,3},{2,18},{3,1},{4,20},{5,7},{6,22},{7,5},{8,24},{9,11},... | collective-permute-start | bytes 3145736 | tf_op jit(solution)/shard_map/ppermute | solution.py:136
  102.0 3.9 %collective-permute-start.8 = (bf16[4,256,896]{2,1,0:T(8,128)(2,1)S(1)}, bf16[4,256,896]{2,1,0:T(8,128)(2,1)S(1)}, u32[]{:S(2)}, u32[]{:S(2)}) collective-permute-start(bf16[4,256,896]{2,1,0:T(8,128)(2,1)S(1)} %pad_maximum_fusion.4), channel_id=1, source_target_pairs={{0,1},{1,0},{2,3},{3,2},{4,5},{5,4},{6,7},{7,6},{8,9},{9,8},{10,11... | collective-permute-start | bytes 5505032 | tf_op jit(solution)/shard_map/ppermute | solution.py:136
  103.6 5.2 %collective-permute-start.20 = (bf16[4,128,2048]{2,1,0:T(8,128)(2,1)S(1)}, bf16[4,128,2048]{2,1,0:T(8,128)(2,1)S(1)}, u32[]{:S(2)}, u32[]{:S(2)}) collective-permute-start(bf16[4,128,2048]{2,1,0:T(8,128)(2,1)S(1)} %pad_maximum_fusion.2), channel_id=1, source_target_pairs={{0,1},{1,0},{2,3},{3,2},{4,5},{5,4},{6,7},{7,6},{8,9},{9,8},{10,11... | collective-permute-start | bytes 6291464 | tf_op jit(solution)/shard_map/ppermute | solution.py:136
  104.5 8.7 %collective-permute-start.5 = (bf16[4,128,2048]{2,1,0:T(8,128)(2,1)S(1)}, bf16[4,128,2048]{2,1,0:T(8,128)(2,1)S(1)}, u32[]{:S(2)}, u32[]{:S(2)}) collective-permute-start(bf16[4,128,2048]{2,1,0:T(8,128)(2,1)S(1)} %pad_maximum_fusion), channel_id=1, source_target_pairs={{0,1},{1,0},{2,3},{3,2},{4,5},{5,4},{6,7},{7,6},{8,9},{9,8},{10,11... | collective-permute-start | bytes 6291464 | tf_op jit(solution)/shard_map/ppermute | solution.py:136
  128.4 5.3 %collective-permute-start.21 = (bf16[4,128,2048]{2,1,0:T(8,128)(2,1)S(1)}, bf16[4,128,2048]{2,1,0:T(8,128)(2,1)S(1)}, u32[]{:S(2)}, u32[]{:S(2)}) collective-permute-start(bf16[4,128,2048]{2,1,0:T(8,128)(2,1)S(1)} %bitcast.75), channel_id=1, source_target_pairs={{0,1},{1,0},{2,3},{3,2},{4,5},{5,4},{6,7},{7,6},{8,9},{9,8},{10,11... | collective-permute-start | bytes 6291464 | tf_op jit(solution)/shard_map/ppermute | solution.py:136
  130.5 5.5 %collective-permute-start.15 = (bf16[4,128,2048]{2,1,0:T(8,128)(2,1)S(1)}, bf16[4,128,2048]{2,1,0:T(8,128)(2,1)S(1)}, u32[]{:S(2)}, u32[]{:S(2)}) collective-permute-start(bf16[4,128,2048]{2,1,0:T(8,128)(2,1)S(1)} %bitcast.74), channel_id=1, source_target_pairs={{0,1},{1,0},{2,3},{3,2},{4,5},{5,4},{6,7},{7,6},{8,9},{9,8},{10,11... | collective-permute-start | bytes 6291464 | tf_op jit(solution)/shard_map/ppermute | solution.py:136
  134.5 14.9 %collective-permute-start.22 = (bf16[2,128,2048]{2,1,0:T(8,128)(2,1)S(1)}, bf16[2,128,2048]{2,1,0:T(8,128)(2,1)S(1)}, u32[]{:S(2)}, u32[]{:S(2)}) collective-permute-start(bf16[2,128,2048]{2,1,0:T(8,128)(2,1)S(1)} %slice.253), channel_id=1, source_target_pairs={{0,2},{1,17},{2,0},{3,19},{4,6},{5,21},{6,4},{7,23},{8,10},{9,25},... | collective-permute-start | bytes 3145736 | tf_op jit(solution)/shard_map/ppermute | solution.py:136
  137.0 29.2 %collective-permute-start.16 = (bf16[2,128,2048]{2,1,0:T(8,128)(2,1)S(1)}, bf16[2,128,2048]{2,1,0:T(8,128)(2,1)S(1)}, u32[]{:S(2)}, u32[]{:S(2)}) collective-permute-start(bf16[2,128,2048]{2,1,0:T(8,128)(2,1)S(1)} %slice.254), channel_id=1, source_target_pairs={{0,2},{1,17},{2,0},{3,19},{4,6},{5,21},{6,4},{7,23},{8,10},{9,25},... | collective-permute-start | bytes 3145736 | tf_op jit(solution)/shard_map/ppermute | solution.py:136
  149.8 18.4 %collective-permute-start.23 = (bf16[128,2048]{1,0:T(8,128)(2,1)S(1)}, bf16[128,2048]{1,0:T(8,128)(2,1)S(1)}, u32[]{:S(2)}, u32[]{:S(2)}) collective-permute-start(bf16[128,2048]{1,0:T(8,128)(2,1)S(1)} %fusion.24), channel_id=1, source_target_pairs={{0,16},{1,3},{2,18},{3,1},{4,20},{5,7},{6,22},{7,5},{8,24},{9,11},... | collective-permute-start | bytes 1572872 | tf_op jit(solution)/shard_map/ppermute | solution.py:136
  166.6 9.2 %collective-permute-start.17 = (bf16[128,2048]{1,0:T(8,128)(2,1)S(1)}, bf16[128,2048]{1,0:T(8,128)(2,1)S(1)}, u32[]{:S(2)}, u32[]{:S(2)}) collective-permute-start(bf16[128,2048]{1,0:T(8,128)(2,1)S(1)} %fusion.23), channel_id=1, source_target_pairs={{0,16},{1,3},{2,18},{3,1},{4,20},{5,7},{6,22},{7,5},{8,24},{9,11},... | collective-permute-start | bytes 1572872 | tf_op jit(solution)/shard_map/ppermute | solution.py:136
  (4 other events, 16.4 us)

commit v2 on v0

--- a/solution.py
+++ b/solution.py
@@ -3,6 +3,8 @@
 import jax
 import jax.numpy as jnp
 from jax import lax
+from jax.experimental import pallas as pl
+from jax.experimental.pallas import tpu as pltpu
 from jax.sharding import PartitionSpec as P
 
 HD = 128
@@ -10,15 +12,497 @@
 BLOCK = 64
 UPC = 4
 UNITS = 8
+AXES = ("groups", "dp", "nbr", "mp")
+F32 = jnp.float32
+BF16 = jnp.bfloat16
 
 
 def encode_rows(states, enc_gain):
-    widened = states.astype(jnp.float32)
+    widened = states.astype(F32)
     inverse = lax.rsqrt(jnp.mean(widened * widened, axis=-1, keepdims=True) + 1e-06)
-    return (widened * inverse * enc_gain).astype(jnp.bfloat16)
-
-
-def local(
+    return (widened * inverse * enc_gain).astype(BF16)
+
+
+def dot(a, b):
+    return jnp.dot(a, b, preferred_element_type=F32)
+
+
+def dot_t(a, b):
+    return lax.dot_general(a, b, (((1,), (1,)), ((), ())), preferred_element_type=F32)
+
+
+CROSSED = (0, 2, 1, 3)
+TILE = 16
+SCALE = 1.0 / math.sqrt(HD)
+LONG = pl.CostEstimate(flops=10**11, bytes_accessed=1024, transcendentals=0)
+
+
+def shape_of(shape, dtype=BF16):
+    return jax.ShapeDtypeStruct(shape, dtype)
+
+
+def kernel_call(body, name, scalars, operands, out_shapes, in_specs):
+    whole = lambda a: pl.BlockSpec(a.shape, lambda i, *_, n=len(a.shape): (0,) * n)
+    return pl.pallas_call(
+        body,
+        grid_spec=pltpu.PrefetchScalarGridSpec(
+            num_scalar_prefetch=len(scalars),
+            grid=(1,),
+            in_specs=[sp or whole(a) for sp, a in zip(in_specs, operands)],
+            out_specs=[whole(a) for a in out_shapes],
+        ),
+        out_shape=tuple(out_shapes),
+        compiler_params=pltpu.CompilerParams(vmem_limit_bytes=56 << 20),
+        cost_estimate=LONG,
+        name=name,
+    )(*scalars, *operands)
+
+
+class Copies:
+    def __init__(self, sems):
+        self.sems, self.used, self.open = sems, 0, {}
+
+    def start(self, name, source, target):
+        copy = pltpu.make_async_copy(source, target, self.sems.at[self.used])
+        self.used += 1
+        copy.start()
+        self.open.setdefault(name, []).append(copy)
+
+    def wait(self, *names):
+        for name in names:
+            for copy in self.open.pop(name):
+                copy.wait()
+
+
+def copy_call(body, name, scalars, operands, out_shapes, scratch, copies):
+    anywhere = pl.BlockSpec(memory_space=pl.ANY)
+    smem = pl.BlockSpec(memory_space=pltpu.SMEM)
+    need = sum(math.prod(a.shape) * jnp.dtype(a.dtype).itemsize for a in scratch)
+    return pl.pallas_call(
+        body,
+        in_specs=[smem] * len(scalars) + [anywhere] * len(operands),
+        out_specs=[anywhere] * len(out_shapes),
+        out_shape=tuple(out_shapes),
+        scratch_shapes=[pltpu.VMEM(a.shape, a.dtype) for a in scratch] + [pltpu.SemaphoreType.DMA((copies,))],
+        compiler_params=pltpu.CompilerParams(vmem_limit_bytes=need + (10 << 20)),
+        cost_estimate=LONG,
+        name=name,
+    )(*scalars, *operands)
+
+
+def slices_kernel(place, q, k, v, o, out):
+    depth, width = q.shape
+    rank = k.shape[0]
+    out[:rank] = k[...]
+    out[rank : 2 * rank] = v[...]
+    out[2 * rank : 2 * rank + depth] = q[...]
+    for c in range(depth // width):
+        at = 2 * rank + depth + c * width
+        out[at : at + width] = o[:, c * width : (c + 1) * width]
+
+
+def projection_slices(chip, qw, kw, vw, ow):
+    depth, width, rank = qw.shape[0], qw.shape[1] // 4, kw.shape[0]
+    column = lambda i, place: (0, place[0])
+    return kernel_call(
+        slices_kernel,
+        "projection_slices",
+        (chip.reshape(1),),
+        (qw, kw, vw, ow),
+        (shape_of((2 * rank + 2 * depth, width)),),
+        [
+            pl.BlockSpec((depth, width), column),
+            pl.BlockSpec((rank, width), column),
+            pl.BlockSpec((rank, width), column),
+            pl.BlockSpec((width, depth), lambda i, place: (place[0], 0)),
+        ],
+    )[0]
+
+
+def prepare_kernel(core, owners, ids, hid, db, gain, near, far):
+    rows, half = hid.shape
+    blocks, e = db.shape[0] // 2, db.shape[2]
+    per = rows // BLOCK
+    near[:, :half] = hid[...]
+    for ref, which, start in ((near, core[0], half), (far, 1 - core[0], 0)):
+        for part in range(blocks // per):
+            states = db[pl.ds(which * blocks + part * per, per)].reshape(rows, e)
+            ref[:, start + part * e : start + (part + 1) * e] = encode_rows(states, gain[...])
+    lane = lax.broadcasted_iota(jnp.int32, (rows, near.shape[1] - half - blocks // per * e), 1)
+    row = jnp.zeros(lane.shape, jnp.int32)
+    for u in range(UNITS):
+        at = divmod(u, UPC)
+        row = jnp.where(lane == u, owners[at] * 2 * blocks + ids[at], row)
+    near[:, near.shape[1] - lane.shape[1] :] = row.astype(F32).astype(BF16)
+
+
+def prepare(core, owners, ids, hidden, db, gain):
+    rows, half = hidden.shape
+    wide = db.shape[0] // 2 * BLOCK // rows * db.shape[2]
+    return kernel_call(
+        prepare_kernel,
+        "prepare",
+        (core.reshape(1), owners, ids),
+        (hidden, db, gain),
+        (shape_of((rows, half + wide + 128)), shape_of((rows, wide))),
+        [None] * 3,
+    )
+
+
+def rows_of(ref, first, count):
+    return ref.at[pl.ds(first, count)]
+
+
+def take_blocks(idx, kv, span, cols):
+    parts = []
+    for u in range(UPC):
+        row = pl.multiple_of(idx[span, u] * TILE, TILE)
+        parts.append(kv[pl.ds(row, BLOCK), cols])
+    return jnp.concatenate(parts, axis=0)
+
+
+def head_cols(width, h):
+    return slice(h * HD, (h + 1) * HD), slice(width + h * HD, width + (h + 1) * HD)
+
+
+def stage_tokens(copies, name, arrays, target):
+    rows, half = arrays[0].shape[0], target.shape[1]
+    for slot, a in enumerate(arrays):
+        source = a.at[:, pl.ds(0, half)] if a.shape[1] > half else a
+        copies.start(name, source, rows_of(target, slot * rows, rows))
+
+
+def stage_output(copies, pos, parts, target):
+    depth, width = parts[3].shape
+    for r, part in enumerate(parts):
+        for c in range(depth // width):
+            at = part.shape[0] - depth + c * width
+            place = pl.multiple_of(pos[r] * depth + c * width, width)
+            copies.start("output", rows_of(part, at, width), target.at[:, pl.ds(place, width)])
+
+
+def forward_kernel(src, idx, pos, *refs):
+    banks, own, other, parts = refs[:8], refs[:4], refs[8:12], refs[12:16]
+    kv_out, mix_out, att_out = refs[16:19]
+    states, kvw, kv, near, far, weights, queries, mix, att, sems = refs[19:]
+    e, columns = kvw.shape
+    rank, rows, wide = e // 4, banks[0].shape[0], states.shape[1]
+    half, width = near.shape[1], weights.shape[1]
+    depth = weights.shape[0] // 4
+    spans = att.shape[0]
+    copies = Copies(sems)
+    for r, part in enumerate(parts):
+        place = pl.multiple_of(src[r] * rank, TILE)
+        for c in range(2):
+            target = kvw.at[pl.ds(place, rank), pl.ds(c * width, width)]
+            copies.start("kvw", rows_of(part, c * rank, rank), target)
+    for b, bank in enumerate(banks):
+        start = 0 if b == 4 else bank.shape[1] - 128 - wide
+        copies.start(b // 4, bank.at[:, pl.ds(start, wide)], rows_of(states, b * rows, rows))
+    for r, part in enumerate(parts):
+        place = pl.multiple_of(pos[r] * depth, depth)
+        copies.start("query", rows_of(part, 2 * rank, depth), rows_of(weights, place, depth))
+    stage_tokens(copies, "near", own, near)
+    stage_tokens(copies, "far", other, far)
+    copies.wait("kvw")
+    for side in range(2):
+        copies.wait(side)
+        for c in range(wide // e):
+            block = states[4 * side * rows : 4 * (side + 1) * rows, c * e : (c + 1) * e]
+            at = (8 * c + 4 * side) * rows
+            kv[at : at + 4 * rows] = dot(block, kvw[...]).astype(BF16)
+    copies.start("out", kv, kv_out)
+    copies.wait("query", "near")
+    total = dot(near[...], weights[:half])
+    copies.wait("far")
+    queries[...] = (total + dot(far[...], weights[half:])).astype(BF16)
+    for span in range(spans):
+        rows = slice(span * SPAN, (span + 1) * SPAN)
+        heads = range(width // HD)
+        cols = [head_cols(width, h) for h in heads]
+        scores = [dot_t(queries[rows, kc], take_blocks(idx, kv, span, kc)) * SCALE for kc, _ in cols]
+        scores = [jnp.exp(s - jnp.max(s, axis=-1, keepdims=True)) for s in scores]
+        scores = [s * (1.0 / jnp.sum(s, axis=-1, keepdims=True)) for s in scores]
+        for h in heads:
+            att[span, h] = scores[h]
+            kc, vc = cols[h]
+            mix[rows, kc] = dot(scores[h].astype(BF16), take_blocks(idx, kv, span, vc)).astype(BF16)
+        if span % 2:
+            copies.start("out", rows_of(att, span - 1, 2), rows_of(att_out, span - 1, 2))
+    copies.start("out", mix, mix_out)
+    copies.wait("out")
+
+
+def forward(src, idx, pos, own, far_states, other, parts, half, e, depth):
+    rows, width = own[0].shape[0], parts[0].shape[1]
+    tokens = 4 * rows
+    spans = tokens // SPAN
+    wide = far_states.shape[1]
+    kv = shape_of((8 * wide // e * rows, 2 * width))
+    mix = shape_of((tokens, width))
+    att = shape_of((spans, width // HD, SPAN, UPC * BLOCK), F32)
+    side = shape_of((tokens, half))
+    return copy_call(
+        forward_kernel,
+        "forward",
+        (src, idx, pos),
+        (*own, far_states, *other[1:], *other, *parts),
+        (kv, mix, att),
+        (
+            shape_of((8 * rows, wide)),
+            shape_of((e, 2 * width)),
+            kv,
+            side,
+            side,
+            shape_of((4 * depth, width)),
+            mix,
+            mix,
+            att,
+        ),
+        30 + spans // 2,
+    )
+
+
+def output_kernel(pos, *refs):
+    mix_in, parts = refs[0], refs[1:5]
+    theirs_out, mine_out, mix, weights, theirs, mine, sems = refs[5:]
+    tokens, half = mine.shape
+    rows = tokens // 4
+    copies = Copies(sems)
+    copies.start("mix", mix_in, mix)
+    stage_output(copies, pos, parts, weights)
+    copies.wait("mix", "output")
+    crossed = jnp.concatenate([mix[CROSSED[s] * rows : (CROSSED[s] + 1) * rows] for s in range(4)])
+    for ref, out, tokens_of, first in ((theirs, theirs_out, crossed, half), (mine, mine_out, mix[...], 0)):
+        for c in range(4):
+            step = half // 4
+            cols = slice(c * step, (c + 1) * step)
+            ref[:, cols] = dot(tokens_of, weights[:, first + c * step : first + (c + 1) * step]).astype(BF16)
+        copies.start("out", ref, out)
+    copies.wait("out")
+
+
+def output_halves(pos, mix, parts):
+    tokens, width = mix.shape
+    depth = parts[3].shape[0]
+    half = shape_of((tokens, 2 * depth))
+    return copy_call(
+        output_kernel,
+        "output_halves",
+        (pos,),
+        (mix, *parts),
+        (half, half),
+        (mix, shape_of((width, 4 * depth)), half, half),
+        3 + 4 * depth // width,
+    )
+
+
+def cotangent_kernel(pos, *refs):
+    own, other, parts, gm_out = refs[:4], refs[4:8], refs[8:12], refs[12]
+    near, far, weights, gm, sems = refs[13:]
+    half = near.shape[1]
+    copies = Copies(sems)
+    stage_output(copies, pos, parts, weights)
+    stage_tokens(copies, "near", own, near)
+    stage_tokens(copies, "far", other, far)
+    copies.wait("output", "near")
+    total = dot_t(near[...], weights[:, :half])
+    copies.wait("far")
+    gm[...] = (total + dot_t(far[...], weights[:, half:])).astype(BF16)
+    copies.start("out", gm, gm_out)
+    copies.wait("out")
+
+
+def cotangent(pos, own, other, parts):
+    rows, half = own[0].shape
+    depth, width = parts[3].shape
+    side, gm = shape_of((4 * rows, half)), shape_of((4 * rows, width))
+    return copy_call(
+        cotangent_kernel,
+        "cotangent",
+        (pos,),
+        (*own, *other, *parts),
+        (gm,),
+        (side, side, shape_of((width, 4 * depth)), gm),
+        9 + 4 * depth // width,
+    )[0]
+
+
+def backward_kernel(idx, pos, *refs):
+    gm_in, kv_in, att_in, parts, results = refs[0], refs[1], refs[2], refs[3:7], refs[7:11]
+    gm, kv, att, wq, gq, crossed, buffers, sems = refs[11:]
+    width, depth = wq.shape[1], wq.shape[0] // 4
+    spans = att.shape[0]
+    copies = Copies(sems)
+    copies.start("in", gm_in, gm)
+    copies.start("in", kv_in, kv)
+    copies.start("in", att_in, att)
+    for r, part in enumerate(parts):
+        place = pl.multiple_of(pos[r] * depth, depth)
+        first = part.shape[0] - 2 * depth if r < 3 else part.shape[0] - depth
+        copies.start("query", rows_of(part, first, depth), rows_of(wq, place, depth))
+    copies.wait("in")
+    for span in range(spans):
+        slot, rest = divmod(span, spans // 4)
+        rows = slice(span * SPAN, (span + 1) * SPAN)
+        there = (CROSSED[slot] * (spans // 4) + rest) * SPAN
+        heads = range(width // HD)
+        cols = [head_cols(width, h) for h in heads]
+        grads = [dot_t(gm[rows, kc], take_blocks(idx, kv, span, vc)) for kc, vc in cols]
+        inner = [jnp.sum(att[span, h] * grads[h], axis=-1, keepdims=True) for h in heads]
+        grads = [(att[span, h] * (grads[h] - inner[h]) * SCALE).astype(BF16) for h in heads]
+        for h in heads:
+            kc, _ = cols[h]
+            value = dot(grads[h], take_blocks(idx, kv, span, kc)).astype(BF16)
+            gq[rows, kc] = value
+            crossed[there : there + SPAN, kc] = value
+    copies.wait("query")
+    for n, (source, slice_of) in enumerate(((crossed, 2), (crossed, 3), (gq, 0), (gq, 1))):
+        for c in range(2):
+            step = depth // 2
+            at = slice_of * depth + c * step
+            buffers[n, :, c * step : (c + 1) * step] = dot_t(source[...], wq[at : at + step]).astype(BF16)
+        copies.start("out", buffers.at[n], results[n])
+    copies.wait("out")
+
+
+def backward(idx, pos, gm, kv, att, parts, depth):
+    tokens, width = gm.shape
+    chunk = shape_of((tokens, depth))
+    return copy_call(
+        backward_kernel,
+        "backward",
+        (idx, pos),
+        (gm, kv, att, *parts),
+        (chunk,) * 4,
+        (gm, kv, att, shape_of((4 * depth, width)), gm, gm, shape_of((4, tokens, depth))),
+        11,
+    )
+
+
+def flat(y, z, x, m):
+    return ((y * 4 + z) * 2 + x) * 2 + m
+
+
+def permutation(move):
+    pairs = []
+    for y in range(2):
+        for z in range(4):
+            for x in range(2):
+                for m in range(2):
+                    pairs.append((flat(y, z, x, m), flat(*move(y, z, x, m))))
+    return pairs
+
+
+RING = (0, 1, 3, 2)
+NEXT = {RING[i]: RING[(i + 1) % 4] for i in range(4)}
+PREV = {RING[i]: RING[(i + 3) % 4] for i in range(4)}
+FIRST = permutation(lambda y, z, x, m: (y, z, 1 - x, m) if m == 0 else (1 - y, z, x, m))
+SECOND = permutation(lambda y, z, x, m: (1 - y, z, x, m) if m == 0 else (y, z, 1 - x, m))
+DIAGONAL = permutation(lambda y, z, x, m: (1 - y, z, 1 - x, m))
+CORE = permutation(lambda y, z, x, m: (y, z, x, 1 - m))
+UP = permutation(lambda y, z, x, m: (y, NEXT[z], x, m))
+DOWN = permutation(lambda y, z, x, m: (y, PREV[z], x, m))
+
+
+def move(array, pairs):
+    return lax.ppermute(array, AXES, pairs)
+
+
+def after(array, *earlier):
+    return lax.optimization_barrier((array, *earlier))[0]
+
+
+def phase(*arrays):
+    return lax.optimization_barrier(arrays)
+
+
+def local_plane(
+    hidden,
+    grad_out,
+    database,
+    enc_gain,
+    query_weight,
+    key_weight,
+    value_weight,
+    out_weight,
+    block_ids,
+    owners,
+):
+    y, z, x, m = (lax.axis_index(a).astype(jnp.int32) for a in AXES)
+    depth, width = query_weight.shape[0], query_weight.shape[1] // 4
+    rank = key_weight.shape[0]
+    blocks, e = database.shape[0] // 2, database.shape[2]
+    rows, half = hidden.shape
+    nxt = lax.rem(2 * z + 1 - z // 2, 4)
+    sources = (z, 3 - nxt, nxt, 3 - z)
+    pos = jnp.stack([s ^ (2 * m) for s in sources])
+    sources = jnp.stack(sources)
+
+    weights = projection_slices(y * 2 + x, query_weight, key_weight, value_weight, out_weight)
+    up, down = move(weights, UP), move(weights, DOWN)
+    he, e_far = prepare(m, owners, block_ids, after(hidden, weights), database, enc_gain)
+    he_own = (he, move(he, SECOND), move(he, FIRST), move(he, DIAGONAL))
+    up, down, pos, sources, *he_own = phase(up, down, pos, sources, *he_own)
+
+    near_far = move(up[: 2 * rank + depth], UP)
+    h_zero = move(hidden, CORE)
+    he_other = (h_zero,) + tuple(move(he_own[CROSSED[i]], CORE) for i in (1, 2, 3))
+    o_far = move(after(up[2 * rank + depth :], *he_other), UP)
+    g = after(grad_out, *he_other)
+    g_own = (grad_out, move(g, SECOND), move(g, FIRST), move(g, DIAGONAL))
+
+    per = rows // BLOCK
+    codes = jnp.stack([after(a, *he_other)[0, a.shape[1] - 128 :][:UNITS] for a in he_own]).astype(jnp.int32)
+    own_of, id_of = codes // (2 * blocks), codes % (2 * blocks)
+    slot = jnp.arange(4, dtype=jnp.int32)
+    rel_x = own_of ^ x
+    rel_y = jnp.where(m == 0, slot % 2, slot // 2)[:, None]
+    bank = jnp.where(m == 0, rel_x * 2 + rel_y, rel_y * 2 + rel_x)
+    holder, block = id_of // blocks, id_of % blocks
+    idx = (block // per * 8 + (holder ^ m) * 4 + bank) * per + block % per
+    idx = (idx * (BLOCK // TILE)).reshape(-1, UPC).astype(jnp.int32)
+
+    parts = (weights, up, down, near_far)
+    kv, mixture, attention = forward(sources, idx, pos, he_own, e_far, he_other, parts, half, e, depth)
+    mixture, o_far, *g_own = phase(mixture, o_far, *g_own[1:])
+    g_own = (grad_out, *g_own)
+
+    def begin(mine, theirs):
+        return move((mine[2:].astype(F32) + theirs[2:].astype(F32)).astype(BF16), FIRST)
+
+    def carry_on(mine, theirs, first):
+        total = mine[1].astype(F32) + theirs[1].astype(F32) + first[1].astype(F32)
+        return move(total.astype(BF16), SECOND)
+
+    def finish(mine, theirs, first, second):
+        return sum(a.astype(F32) for a in (mine[0], theirs[0], first[0], second))
+
+    def slots(array):
+        return array.reshape(4, rows, -1)
+
+    g_other = tuple(move(g_own[CROSSED[i]], CORE) for i in range(4))
+    outs = (weights, up, down, o_far)
+    o_theirs, o_mine = output_halves(pos, mixture, outs)
+    o_theirs, o_mine = slots(move(o_theirs, CORE)), slots(o_mine)
+    gm = cotangent(pos, g_own, (g_other[0], after(g_other[1], o_mine), *g_other[2:]), outs)
+    o_theirs = after(o_theirs, gm)
+    o_first = begin(o_mine, o_theirs)
+    t0, t1, m0, m1 = backward(idx, pos, after(gm, o_theirs), kv, attention, parts, depth)
+    t0, t1 = after(t0, o_first), after(t1, o_first)
+    t0, t1 = slots(move(t0, CORE)), slots(move(t1, CORE))
+    m0, m1 = slots(m0), slots(m1)
+    first0, first1 = begin(m0, t0), begin(m1, t1)
+    o_second = carry_on(o_mine, o_theirs, o_first)
+    second0, second1 = carry_on(m0, t0, first0), carry_on(m1, t1, first1)
+    summed = finish(o_mine, o_theirs, o_first, o_second)
+    grad_sum = jnp.concatenate((finish(m0, t0, first0, second0), finish(m1, t1, first1, second1)), axis=1)
+    output = (hidden.astype(F32) + summed).astype(BF16)
+    grad_hidden = (grad_out.astype(F32) + grad_sum).astype(BF16)
+    return (output, grad_hidden)
+
+
+def local_any(
     hidden,
     grad_out,
     database,
@@ -121,4 +605,6 @@
         P(("groups", "dp", "nbr"), None),
     )
     out_specs = (P(("groups", "dp", "nbr"), "mp"), P(("groups", "dp", "nbr"), "mp"))
+    sizes = tuple(mesh.shape[a] for a in AXES)
+    local = local_plane if sizes == (2, 4, 2, 2) else local_any
     return jax.shard_map(local, mesh=mesh, in_specs=in_specs, out_specs=out_specs, check_vma=False)

time: 473 us -> 161 us (0.34)
  waiting for transfers between devices: 383 us -> 91.3 us
  matrix products: 44.2 us -> 0 us
  Pallas kernels: 0 us -> 30.8 us
  starting transfers between devices: 4.32 us -> 23.2 us
  between operations: 14.3 us -> 0.84 us
  blocking collectives: 7.74 us -> 0 us
    all_gather x6 -> x0, waiting for transfers between devices: 347 us -> none  [the longest x1 152 us: local(): lax.all_gather(out_weight, 'dp', axis=1, tiled=True)]
    ppermute x0 -> x27, waiting for transfers between devices: none -> 91.3 us  [move(): return lax.ppermute(array, AXES, pairs)]
    dot_general x10 -> x0, matrix products: 44.2 us -> none  [the longest x1 7.92 us: local(): jnp.einsum('chtj,cjhd->cthd', grad_scores, key_rows, preferred_element_ty...]
    pallas_call x0 -> x6, Pallas kernels: none -> 30.8 us  [the longest x4 24.9 us: copy_call(): pl.pallas_call(body, in_specs=[smem] * len(scalars) + [anywhere] * len(op...]
    all_to_all x1 -> x0, waiting for transfers between devices: 24 us -> none  [local(): lax.all_to_all(stacked, 'nbr', split_axis=0, concat_axis=0, tiled=True)]
    ppermute x0 -> x27, starting transfers between devices: none -> 23.2 us  [move(): return lax.ppermute(array, AXES, pairs)]
    reduce_scatter x2 -> x0, waiting for transfers between devices: 8.94 us -> none  [the longest x1 8.92 us: local(): lax.psum_scatter(partial_out, 'mp', scatter_dimension=1, tiled=True)]
    all_to_all x1 -> x0, blocking collectives: 7.74 us -> none  [local(): lax.all_to_all(requests, 'nbr', split_axis=0, concat_axis=0, tiled=True)]
  transfers between devices with their start and end apart: 9 -> 27, of which waited for: 7 -> 12; matrix products, arithmetic and copies ran while one was open for 7% -> 5% of each run, Pallas kernels for 0% -> 18%
where the time goes in v2:
time: 161 us
  waiting for transfers between devices  91.3 us (57%)
  Pallas kernels  30.8 us (19%)
  starting transfers between devices  23.2 us (14%)
  local copies, waits for them, and re-layouts  8.54 us (5%)
  other arithmetic  5.96 us (4%)
    ppermute x27, waiting for transfers between devices, move(): return lax.ppermute(array, AXES, pairs)  91.3 us
    pallas_call x4, Pallas kernels, copy_call(): pl.pallas_call(body, in_specs=[smem] * len(scalars) + [anywhere] * len(op...  24.9 us
    ppermute x27, starting transfers between devices, move(): return lax.ppermute(array, AXES, pairs)  23.2 us
    pallas_call x2, Pallas kernels, kernel_call(): pl.pallas_call(body, grid_spec=pltpu.PrefetchScalarGridSpec(num_scalar_pr...  5.95 us
    unnamed x14, local copies, waits for them, and re-layouts  3.6 us
  transfers between devices with their start and end apart: 27, of which 12 were waited for; matrix products, arithmetic and copies ran while one was open for 5% of the time, Pallas kernels for 18%

profile of v2, /device:TPU:0, one launch (start us, length us, event | category | flops | bytes accessed | tf_op | source)
XLA Modules:
  0.0 160.7 jit_solution(7664943820554386501)
XLA Ops:
  0.6 2.5 %projection_slices.1.refs_12_.refs_1_.refs_8_.refs_3_ = bf16[2496,256]{1,0:T(8,128)(2,1)} custom-call(s32[1]{0:T(128)} %bitcast.place, bf16[1024,1024]{1,0:T(8,128)(2,1)} %q.1, bf16[224,1024]{1,0:T(8,128)(2,1)} %k.1, bf16[224,1024]{1,0:T(8,128)(2,1)} %v.1, bf16[1024,1024]{1,0:T(8,128)(2,1)} %o.1), custom_call_target="tpu_custom_call" | custom-call | flops 99999997952 | bytes 1024 | tf_op jit(solution)/shard_map/projection_slices/pallas_call | solution.py:46
  3.1 4.0 %collective-permute-start.1 = (bf16[2496,256]{1,0:T(8,128)(2,1)}, bf16[2496,256]{1,0:T(8,128)(2,1)}, u32[]{:S(2)}, u32[]{:S(2)}) collective-permute-start(bf16[2496,256]{1,0:T(8,128)(2,1)} %projection_slices.1.refs_12_.refs_1_.refs_8_.refs_3_), channel_id=1, source_target_pairs={{0,8},{1,9},{2,10},{3,11},{4,0},{5,1},{6,2},{7,3},{8,12},{9,13},{1... | collective-permute-start | bytes 3833864 | tf_op jit(solution)/shard_map/ppermute | solution.py:409
  7.1 3.5 %prepare.1 = (bf16[128,3968]{1,0:T(8,128)(2,1)}, bf16[128,1792]{1,0:T(8,128)(2,1)}) custom-call(s32[1]{0:T(128)} %bitcast.9.core, s32[2,4]{1,0:T(2,128)} %owners.1, s32[2,4]{1,0:T(2,128)} %ids.1, bf16[128,2048]{1,0:T(8,128)(2,1)} %hid, bf16[8,64,896]{2,1,0:T(8,128)(2,1)} %db.1, f32[896]{0:T(1024)} %gain.1), custom_call_target="tpu_custom_call" | custom-call | flops 99999997952 | bytes 1024 | tf_op jit(solution)/shard_map/prepare/pallas_call | solution.py:46
  10.6 2.4 %collective-permute-start.4 = (bf16[128,3968]{1,0:T(8,128)(2,1)}, bf16[128,3968]{1,0:T(8,128)(2,1)}, u32[]{:S(2)}, u32[]{:S(2)}) collective-permute-start(bf16[128,3968]{1,0:T(8,128)(2,1)} %get-tuple-element.45.refs_0_), channel_id=1, source_target_pairs={{0,18},{1,19},{2,16},{3,17},{4,22},{5,23},{6,20},{7,21},{8,26},{9,... | collective-permute-start | bytes 3047432 | tf_op jit(solution)/shard_map/ppermute | solution.py:409
  14.2 23.1 %collective-permute-done.4.refs_3_ = bf16[128,3968]{1,0:T(8,128)(2,1)} collective-permute-done((bf16[128,3968]{1,0:T(8,128)(2,1)}, bf16[128,3968]{1,0:T(8,128)(2,1)}, u32[]{:S(2)}, u32[]{:S(2)}) %collective-permute-start.4) | collective-permute-done | bytes 1015840 | tf_op jit(solution)/shard_map/ppermute | solution.py:409
  37.3 20.4 %collective-permute-done.3.refs_2_ = bf16[128,3968]{1,0:T(8,128)(2,1)} collective-permute-done((bf16[128,3968]{1,0:T(8,128)(2,1)}, bf16[128,3968]{1,0:T(8,128)(2,1)}, u32[]{:S(2)}, u32[]{:S(2)}) %collective-permute-start.3) | collective-permute-done | bytes 1015840 | tf_op jit(solution)/shard_map/ppermute | solution.py:409
  57.6 6.2 %collective-permute-done.refs_13_.refs_2_.refs_9_.refs_4_ = bf16[2496,256]{1,0:T(8,128)(2,1)S(1)} collective-permute-done((bf16[2496,256]{1,0:T(8,128)(2,1)}, bf16[2496,256]{1,0:T(8,128)(2,1)S(1)}, u32[]{:S(2)}, u32[]{:S(2)}) %collective-permute-start) | collective-permute-done | bytes 1277984 | tf_op jit(solution)/shard_map/ppermute | solution.py:409
  64.9 1.0 slice.121
  65.9 0.7 collective-permute-start.9
  66.9 0.8 slice.122
  67.7 2.7 %collective-permute-done.5.refs_8_ = bf16[128,2048]{1,0:T(8,128)(2,1)} collective-permute-done((bf16[128,2048]{1,0:T(8,128)(2,1)}, bf16[128,2048]{1,0:T(8,128)(2,1)}, u32[]{:S(2)}, u32[]{:S(2)}) %collective-permute-start.5) | collective-permute-done | bytes 524320 | tf_op jit(solution)/shard_map/ppermute | solution.py:409
  70.6 2.5 %collective-permute-start.13 = (bf16[128,2048]{1,0:T(8,128)(2,1)}, bf16[128,2048]{1,0:T(8,128)(2,1)}, u32[]{:S(2)}, u32[]{:S(2)}) collective-permute-start(bf16[128,2048]{1,0:T(8,128)(2,1)} %refs_0_.1), channel_id=1, source_target_pairs={{0,18},{1,19},{2,16},{3,17},{4,22},{5,23},{6,20},{7,21},{8,26},{9,... | collective-permute-start | bytes 1572872 | tf_op jit(solution)/shard_map/ppermute | solution.py:409
  77.0 8.7 %collective-permute-done.9.refs_15_.refs_6_ = bf16[1472,256]{1,0:T(8,128)(2,1)S(1)} collective-permute-done((bf16[1472,256]{1,0:T(8,128)(2,1)}, bf16[1472,256]{1,0:T(8,128)(2,1)S(1)}, u32[]{:S(2)}, u32[]{:S(2)}) %collective-permute-start.9) | collective-permute-done | bytes 753696 | tf_op jit(solution)/shard_map/ppermute | solution.py:409
  85.8 1.2 copy-done.5
  87.0 1.0 copy-done.6
  88.0 11.6 %forward.1 = (bf16[2048,512]{1,0:T(8,128)(2,1)S(1)}, bf16[512,256]{1,0:T(8,128)(2,1)S(1)}, f32[8,2,64,256]{3,2,1,0:T(8,128)S(1)}) custom-call(s32[4]{0:T(128)S(1)} %get-tuple-element.40.src, s32[8,4]{1,0:T(8,128)S(1)} %fusion.15.idx, s32[4]{0:T(128)S(1)} %get-tuple-element.39.pos, bf16[128,3968]{1,0:T(8,128)(2,1)S(1)} %copy-done.5, ...), custom_call_target="tpu_custom_call" | custom-call | flops 99999997952 | bytes 1024 | tf_op jit(solution)/shard_map/forward/pallas_call | solution.py:81
  100.6 3.7 %output_halves.1 = (bf16[512,2048]{1,0:T(8,128)(2,1)S(1)}, bf16[512,2048]{1,0:T(8,128)(2,1)S(1)}) custom-call(s32[4]{0:T(128)S(1)} %get-tuple-element.39.pos, bf16[512,256]{1,0:T(8,128)(2,1)S(1)} %get-tuple-element.55.refs_0_, bf16[2496,256]{1,0:T(8,128)(2,1)S(1)} %copy-done.4, bf16[2496,256]{1,0:T(8,128)(2,1)S(1)} %collective-permute-done.refs_13_.refs_2_.refs_9_.refs_4_, ...), custom_call_target="tpu_custom_call" | custom-call | flops 99999997952 | bytes 1024 | tf_op jit(solution)/shard_map/output_halves/pallas_call | solution.py:81
  104.4 1.4 copy-done
  106.3 4.2 %cotangent.1.refs_0_ = bf16[512,256]{1,0:T(8,128)(2,1)S(1)} custom-call(s32[4]{0:T(128)S(1)} %get-tuple-element.39.pos, bf16[128,2048]{1,0:T(8,128)(2,1)} %refs_0_.1, bf16[128,2048]{1,0:T(8,128)(2,1)} %collective-permute-done.11.refs_1_, bf16[128,2048]{1,0:T(8,128)(2,1)} %collective-permute-done.12.refs_2_, ...), custom_call_target="tpu_custom_call" | custom-call | flops 99999997952 | bytes 1024 | tf_op jit(solution)/shard_map/cotangent/pallas_call | solution.py:81
  111.0 1.6 collective-permute-start.19
  112.5 5.3 %backward.1 = (bf16[512,1024]{1,0:T(8,128)(2,1)S(1)}, bf16[512,1024]{1,0:T(8,128)(2,1)S(1)}, bf16[512,1024]{1,0:T(8,128)(2,1)S(1)}, bf16[512,1024]{1,0:T(8,128)(2,1)S(1)}) custom-call(s32[8,4]{1,0:T(8,128)S(1)} %copy-done.3, s32[4]{0:T(128)S(1)} %get-tuple-element.39.pos, bf16[512,256]{1,0:T(8,128)(2,1)S(1)} %cotangent.1.refs_0_, ...), custom_call_target="tpu_custom_call" | custom-call | flops 99999997952 | bytes 1024 | tf_op jit(solution)/shard_map/backward/pallas_call | solution.py:81
  117.9 8.0 %collective-permute-done.19 = bf16[2,128,2048]{2,1,0:T(8,128)(2,1)S(1)} collective-permute-done((bf16[2,128,2048]{2,1,0:T(8,128)(2,1)S(1)}, bf16[2,128,2048]{2,1,0:T(8,128)(2,1)S(1)}, u32[]{:S(2)}, u32[]{:S(2)}) %collective-permute-start.19) | collective-permute-done | bytes 1048608 | tf_op jit(solution)/shard_map/ppermute | solution.py:409
  126.3 2.1 %collective-permute-done.21 = bf16[512,1024]{1,0:T(8,128)(2,1)S(1)} collective-permute-done((bf16[512,1024]{1,0:T(8,128)(2,1)S(1)}, bf16[512,1024]{1,0:T(8,128)(2,1)S(1)}, u32[]{:S(2)}, u32[]{:S(2)}) %collective-permute-start.21) | collective-permute-done | bytes 1048608 | tf_op jit(solution)/shard_map/ppermute | solution.py:409
  128.7 1.6 collective-permute-start.22
  130.5 1.6 collective-permute-start.20
  132.9 10.0 %collective-permute-done.22 = bf16[2,128,1024]{2,1,0:T(8,128)(2,1)S(1)} collective-permute-done((bf16[2,128,1024]{2,1,0:T(8,128)(2,1)S(1)}, bf16[2,128,1024]{2,1,0:T(8,128)(2,1)S(1)}, u32[]{:S(2)}, u32[]{:S(2)}) %collective-permute-start.22) | collective-permute-done | bytes 524320 | tf_op jit(solution)/shard_map/ppermute | solution.py:409
  143.0 2.0 %collective-permute-start.23 = (bf16[128,1024]{1,0:T(8,128)(2,1)S(1)}, bf16[128,1024]{1,0:T(8,128)(2,1)S(1)}, u32[]{:S(2)}, u32[]{:S(2)}) collective-permute-start(bf16[128,1024]{1,0:T(8,128)(2,1)S(1)} %fusion.8), channel_id=1, source_target_pairs={{0,16},{1,3},{2,18},{3,1},{4,20},{5,7},{6,22},{7,5},{8,24},{9,11},... | collective-permute-start | bytes 786440 | tf_op jit(solution)/shard_map/ppermute | solution.py:409
  145.4 2.3 %fusion.5 = bf16[128,2048]{1,0:T(8,128)(2,1)} fusion(bf16[128,2048]{1,0:T(8,128)(2,1)S(1)} %collective-permute-done.20, bf16[128,2048]{1,0:T(8,128)(2,1)} %hid, bf16[2,128,2048]{2,1,0:T(8,128)(2,1)S(1)} %collective-permute-done.19, bf16[4,128,2048]{2,1,0:T(8,128)(2,1)S(1)} %bitcast.54, bf16[512,2048]{1,0:T(8,128)(2,1)S(1)} %copy-done.1), kind=kLoop, calls=%fused_computation.10 | loop fusion | flops 2621440 | bytes 3145728 | tf_op jit(solution)/shard_map/convert_element_type | solution.py:500
  147.7 4.3 %collective-permute-done.25 = bf16[2,128,1024]{2,1,0:T(8,128)(2,1)S(1)} collective-permute-done((bf16[2,128,1024]{2,1,0:T(8,128)(2,1)S(1)}, bf16[2,128,1024]{2,1,0:T(8,128)(2,1)S(1)}, u32[]{:S(2)}, u32[]{:S(2)}) %collective-permute-start.25) | collective-permute-done | bytes 524320 | tf_op jit(solution)/shard_map/ppermute | solution.py:409
  152.1 1.3 collective-permute-start.26
  153.6 5.0 %collective-permute-done.26 = bf16[128,1024]{1,0:T(8,128)(2,1)S(1)} collective-permute-done((bf16[128,1024]{1,0:T(8,128)(2,1)S(1)}, bf16[128,1024]{1,0:T(8,128)(2,1)S(1)}, u32[]{:S(2)}, u32[]{:S(2)}) %collective-permute-start.26) | collective-permute-done | bytes 262176 | tf_op jit(solution)/shard_map/ppermute | solution.py:409
  158.7 1.9 %fusion.1 = bf16[128,2048]{1,0:T(8,128)(2,1)} fusion(f32[128,1024]{1,0:T(8,128)S(1)} %fusion.7, f32[128,1024]{1,0:T(8,128)S(1)} %fusion.9, bf16[128,2048]{1,0:T(8,128)(2,1)} %refs_0_.1), kind=kLoop, calls=%fused_computation.3 | loop fusion | flops 1048576 | bytes 2097152 | tf_op jit(solution)/shard_map/convert_element_type | solution.py:501
  (68 shorter events, 11.2 us)
Async XLA Ops:
  3.1 54.5 %collective-permute-start.1 = (bf16[2496,256]{1,0:T(8,128)(2,1)}, bf16[2496,256]{1,0:T(8,128)(2,1)}, u32[]{:S(2)}, u32[]{:S(2)}) collective-permute-start(bf16[2496,256]{1,0:T(8,128)(2,1)} %projection_slices.1.refs_12_.refs_1_.refs_8_.refs_3_), channel_id=1, source_target_pairs={{0,8},{1,9},{2,10},{3,11},{4,0},{5,1},{6,2},{7,3},{8,12},{9,13},{1... | collective-permute-start | bytes 3833864 | tf_op jit(solution)/shard_map/ppermute | solution.py:409
  7.1 56.7 %collective-permute-start = (bf16[2496,256]{1,0:T(8,128)(2,1)}, bf16[2496,256]{1,0:T(8,128)(2,1)S(1)}, u32[]{:S(2)}, u32[]{:S(2)}) collective-permute-start(bf16[2496,256]{1,0:T(8,128)(2,1)} %projection_slices.1.refs_12_.refs_1_.refs_8_.refs_3_), channel_id=1, source_target_pairs={{0,4},{1,5},{2,6},{3,7},{4,12},{5,13},{6,14},{7,15},{8,0},{9,1},{1... | collective-permute-start | bytes 3833864 | tf_op jit(solution)/shard_map/ppermute | solution.py:409
  10.6 75.1 %copy-start.4 = (bf16[2496,256]{1,0:T(8,128)(2,1)S(1)}, bf16[2496,256]{1,0:T(8,128)(2,1)}, u32[]{:S(2)}) copy-start(bf16[2496,256]{1,0:T(8,128)(2,1)} %projection_slices.1.refs_12_.refs_1_.refs_8_.refs_3_) | copy-start | bytes 3833860
  10.6 26.6 %collective-permute-start.4 = (bf16[128,3968]{1,0:T(8,128)(2,1)}, bf16[128,3968]{1,0:T(8,128)(2,1)}, u32[]{:S(2)}, u32[]{:S(2)}) collective-permute-start(bf16[128,3968]{1,0:T(8,128)(2,1)} %get-tuple-element.45.refs_0_), channel_id=1, source_target_pairs={{0,18},{1,19},{2,16},{3,17},{4,22},{5,23},{6,20},{7,21},{8,26},{9,... | collective-permute-start | bytes 3047432 | tf_op jit(solution)/shard_map/ppermute | solution.py:409
  13.1 44.6 %collective-permute-start.3 = (bf16[128,3968]{1,0:T(8,128)(2,1)}, bf16[128,3968]{1,0:T(8,128)(2,1)}, u32[]{:S(2)}, u32[]{:S(2)}) collective-permute-start(bf16[128,3968]{1,0:T(8,128)(2,1)} %get-tuple-element.45.refs_0_), channel_id=1, source_target_pairs={{0,2},{1,17},{2,0},{3,19},{4,6},{5,21},{6,4},{7,23},{8,10},{9,25},... | collective-permute-start | bytes 3047432 | tf_op jit(solution)/shard_map/ppermute | solution.py:409
  13.6 44.0 %collective-permute-start.2 = (bf16[128,3968]{1,0:T(8,128)(2,1)}, bf16[128,3968]{1,0:T(8,128)(2,1)}, u32[]{:S(2)}, u32[]{:S(2)}) collective-permute-start(bf16[128,3968]{1,0:T(8,128)(2,1)} %get-tuple-element.45.refs_0_), channel_id=1, source_target_pairs={{0,16},{1,3},{2,18},{3,1},{4,20},{5,7},{6,22},{7,5},{8,24},{9,11},... | collective-permute-start | bytes 3047432 | tf_op jit(solution)/shard_map/ppermute | solution.py:409
  63.9 6.8 %collective-permute-start.6 = (bf16[128,3968]{1,0:T(8,128)(2,1)}, bf16[128,3968]{1,0:T(8,128)(2,1)}, u32[]{:S(2)}, u32[]{:S(2)}) collective-permute-start(bf16[128,3968]{1,0:T(8,128)(2,1)} %collective-permute-done.3.refs_2_), channel_id=1, source_target_pairs={{0,1},{1,0},{2,3},{3,2},{4,5},{5,4},{6,7},{7,6},{8,9},{9,8},{10,11... | collective-permute-start | bytes 3047432 | tf_op jit(solution)/shard_map/ppermute | solution.py:409
  63.9 6.7 %collective-permute-start.7 = (bf16[128,3968]{1,0:T(8,128)(2,1)}, bf16[128,3968]{1,0:T(8,128)(2,1)}, u32[]{:S(2)}, u32[]{:S(2)}) collective-permute-start(bf16[128,3968]{1,0:T(8,128)(2,1)} %collective-permute-done.2.refs_1_), channel_id=1, source_target_pairs={{0,1},{1,0},{2,3},{3,2},{4,5},{5,4},{6,7},{7,6},{8,9},{9,8},{10,11... | collective-permute-start | bytes 3047432 | tf_op jit(solution)/shard_map/ppermute | solution.py:409
  64.4 6.2 %collective-permute-start.8 = (bf16[128,3968]{1,0:T(8,128)(2,1)}, bf16[128,3968]{1,0:T(8,128)(2,1)}, u32[]{:S(2)}, u32[]{:S(2)}) collective-permute-start(bf16[128,3968]{1,0:T(8,128)(2,1)} %collective-permute-done.4.refs_3_), channel_id=1, source_target_pairs={{0,1},{1,0},{2,3},{3,2},{4,5},{5,4},{6,7},{7,6},{8,9},{9,8},{10,11... | collective-permute-start | bytes 3047432 | tf_op jit(solution)/shard_map/ppermute | solution.py:409
  64.4 6.1 %collective-permute-start.5 = (bf16[128,2048]{1,0:T(8,128)(2,1)}, bf16[128,2048]{1,0:T(8,128)(2,1)}, u32[]{:S(2)}, u32[]{:S(2)}) collective-permute-start(bf16[128,2048]{1,0:T(8,128)(2,1)} %hid), channel_id=1, source_target_pairs={{0,1},{1,0},{2,3},{3,2},{4,5},{5,4},{6,7},{7,6},{8,9},{9,8},{10,11... | collective-permute-start | bytes 1572872 | tf_op jit(solution)/shard_map/ppermute | solution.py:409
  65.9 19.9 %collective-permute-start.9 = (bf16[1472,256]{1,0:T(8,128)(2,1)}, bf16[1472,256]{1,0:T(8,128)(2,1)S(1)}, u32[]{:S(2)}, u32[]{:S(2)}) collective-permute-start(bf16[1472,256]{1,0:T(8,128)(2,1)} %slice.121), channel_id=1, source_target_pairs={{0,4},{1,5},{2,6},{3,7},{4,12},{5,13},{6,14},{7,15},{8,0},{9,1},{1... | collective-permute-start | bytes 2261000 | tf_op jit(solution)/shard_map/ppermute | solution.py:409
  70.5 35.8 %collective-permute-start.15 = (bf16[128,2048]{1,0:T(8,128)(2,1)}, bf16[128,2048]{1,0:T(8,128)(2,1)}, u32[]{:S(2)}, u32[]{:S(2)}) collective-permute-start(bf16[128,2048]{1,0:T(8,128)(2,1)} %refs_0_.1), channel_id=1, source_target_pairs={{0,1},{1,0},{2,3},{3,2},{4,5},{5,4},{6,7},{7,6},{8,9},{9,8},{10,11... | collective-permute-start | bytes 1572872 | tf_op jit(solution)/shard_map/ppermute | solution.py:409
  70.6 29.3 %collective-permute-start.13 = (bf16[128,2048]{1,0:T(8,128)(2,1)}, bf16[128,2048]{1,0:T(8,128)(2,1)}, u32[]{:S(2)}, u32[]{:S(2)}) collective-permute-start(bf16[128,2048]{1,0:T(8,128)(2,1)} %refs_0_.1), channel_id=1, source_target_pairs={{0,18},{1,19},{2,16},{3,17},{4,22},{5,23},{6,20},{7,21},{8,26},{9,... | collective-permute-start | bytes 1572872 | tf_op jit(solution)/shard_map/ppermute | solution.py:409
  73.2 26.8 %collective-permute-start.12 = (bf16[128,2048]{1,0:T(8,128)(2,1)}, bf16[128,2048]{1,0:T(8,128)(2,1)}, u32[]{:S(2)}, u32[]{:S(2)}) collective-permute-start(bf16[128,2048]{1,0:T(8,128)(2,1)} %refs_0_.1), channel_id=1, source_target_pairs={{0,2},{1,17},{2,0},{3,19},{4,6},{5,21},{6,4},{7,23},{8,10},{9,25},... | collective-permute-start | bytes 1572872 | tf_op jit(solution)/shard_map/ppermute | solution.py:409
  73.7 26.3 %collective-permute-start.11 = (bf16[128,2048]{1,0:T(8,128)(2,1)}, bf16[128,2048]{1,0:T(8,128)(2,1)}, u32[]{:S(2)}, u32[]{:S(2)}) collective-permute-start(bf16[128,2048]{1,0:T(8,128)(2,1)} %refs_0_.1), channel_id=1, source_target_pairs={{0,16},{1,3},{2,18},{3,1},{4,20},{5,7},{6,22},{7,5},{8,24},{9,11},... | collective-permute-start | bytes 1572872 | tf_op jit(solution)/shard_map/ppermute | solution.py:409
  77.0 22.6 %copy-start.2 = (s32[8,4]{1,0:T(8,128)}, s32[8,4]{1,0:T(8,128)S(1)}, u32[]{:S(2)}) copy-start(s32[8,4]{1,0:T(8,128)S(1)} %fusion.15.idx) | copy-start | bytes 388
  85.7 14.2 %collective-permute-start.10 = (bf16[1024,256]{1,0:T(8,128)(2,1)}, bf16[1024,256]{1,0:T(8,128)(2,1)S(1)}, u32[]{:S(2)}, u32[]{:S(2)}) collective-permute-start(bf16[1024,256]{1,0:T(8,128)(2,1)} %slice.122), channel_id=1, source_target_pairs={{0,4},{1,5},{2,6},{3,7},{4,12},{5,13},{6,14},{7,15},{8,0},{9,1},{1... | collective-permute-start | bytes 1572872 | tf_op jit(solution)/shard_map/ppermute | solution.py:409
  100.0 6.4 %collective-permute-start.17 = (bf16[128,2048]{1,0:T(8,128)(2,1)}, bf16[128,2048]{1,0:T(8,128)(2,1)S(1)}, u32[]{:S(2)}, u32[]{:S(2)}) collective-permute-start(bf16[128,2048]{1,0:T(8,128)(2,1)} %collective-permute-done.11.refs_1_), channel_id=1, source_target_pairs={{0,1},{1,0},{2,3},{3,2},{4,5},{5,4},{6,7},{7,6},{8,9},{9,8},{10,11... | collective-permute-start | bytes 1572872 | tf_op jit(solution)/shard_map/ppermute | solution.py:409
  100.1 6.3 %collective-permute-start.16 = (bf16[128,2048]{1,0:T(8,128)(2,1)}, bf16[128,2048]{1,0:T(8,128)(2,1)S(1)}, u32[]{:S(2)}, u32[]{:S(2)}) collective-permute-start(bf16[128,2048]{1,0:T(8,128)(2,1)} %collective-permute-done.12.refs_2_), channel_id=1, source_target_pairs={{0,1},{1,0},{2,3},{3,2},{4,5},{5,4},{6,7},{7,6},{8,9},{9,8},{10,11... | collective-permute-start | bytes 1572872 | tf_op jit(solution)/shard_map/ppermute | solution.py:409
  100.5 5.8 %collective-permute-start.18 = (bf16[128,2048]{1,0:T(8,128)(2,1)}, bf16[128,2048]{1,0:T(8,128)(2,1)S(1)}, u32[]{:S(2)}, u32[]{:S(2)}) collective-permute-start(bf16[128,2048]{1,0:T(8,128)(2,1)} %collective-permute-done.13.refs_3_), channel_id=1, source_target_pairs={{0,1},{1,0},{2,3},{3,2},{4,5},{5,4},{6,7},{7,6},{8,9},{9,8},{10,11... | collective-permute-start | bytes 1572872 | tf_op jit(solution)/shard_map/ppermute | solution.py:409
  104.4 1.4 copy-start
  105.8 4.7 %collective-permute-start.14 = (bf16[512,2048]{1,0:T(8,128)(2,1)S(1)}, bf16[512,2048]{1,0:T(8,128)(2,1)S(1)}, u32[]{:S(2)}, u32[]{:S(2)}) collective-permute-start(bf16[512,2048]{1,0:T(8,128)(2,1)S(1)} %get-tuple-element.58), channel_id=1, source_target_pairs={{0,1},{1,0},{2,3},{3,2},{4,5},{5,4},{6,7},{7,6},{8,9},{9,8},{10,11... | collective-permute-start | bytes 6291464 | tf_op jit(solution)/shard_map/ppermute | solution.py:409
  110.6 2.0 %copy-start.3 = (s32[8,4]{1,0:T(8,128)S(1)}, s32[8,4]{1,0:T(8,128)}, u32[]{:S(2)}) copy-start(s32[8,4]{1,0:T(8,128)} %copy-done.2) | copy-start | bytes 388
  111.0 14.9 %collective-permute-start.19 = (bf16[2,128,2048]{2,1,0:T(8,128)(2,1)S(1)}, bf16[2,128,2048]{2,1,0:T(8,128)(2,1)S(1)}, u32[]{:S(2)}, u32[]{:S(2)}) collective-permute-start(bf16[2,128,2048]{2,1,0:T(8,128)(2,1)S(1)} %fusion), channel_id=1, source_target_pairs={{0,2},{1,17},{2,0},{3,19},{4,6},{5,21},{6,4},{7,23},{8,10},{9,25},... | collective-permute-start | bytes 3145736 | tf_op jit(solution)/shard_map/ppermute | solution.py:409
  112.5 17.7 %copy-start.1 = (bf16[512,2048]{1,0:T(8,128)(2,1)S(1)}, bf16[512,2048]{1,0:T(8,128)(2,1)}, u32[]{:S(2)}) copy-start(bf16[512,2048]{1,0:T(8,128)(2,1)} %copy-done) | copy-start | bytes 6291460
  125.8 2.7 %collective-permute-start.21 = (bf16[512,1024]{1,0:T(8,128)(2,1)S(1)}, bf16[512,1024]{1,0:T(8,128)(2,1)S(1)}, u32[]{:S(2)}, u32[]{:S(2)}) collective-permute-start(bf16[512,1024]{1,0:T(8,128)(2,1)S(1)} %get-tuple-element.68), channel_id=1, source_target_pairs={{0,1},{1,0},{2,3},{3,2},{4,5},{5,4},{6,7},{7,6},{8,9},{9,8},{10,11... | collective-permute-start | bytes 3145736 | tf_op jit(solution)/shard_map/ppermute | solution.py:409
  125.8 6.3 %collective-permute-start.24 = (bf16[512,1024]{1,0:T(8,128)(2,1)S(1)}, bf16[512,1024]{1,0:T(8,128)(2,1)S(1)}, u32[]{:S(2)}, u32[]{:S(2)}) collective-permute-start(bf16[512,1024]{1,0:T(8,128)(2,1)S(1)} %get-tuple-element.71), channel_id=1, source_target_pairs={{0,1},{1,0},{2,3},{3,2},{4,5},{5,4},{6,7},{7,6},{8,9},{9,8},{10,11... | collective-permute-start | bytes 3145736 | tf_op jit(solution)/shard_map/ppermute | solution.py:409
  128.7 14.2 %collective-permute-start.22 = (bf16[2,128,1024]{2,1,0:T(8,128)(2,1)S(1)}, bf16[2,128,1024]{2,1,0:T(8,128)(2,1)S(1)}, u32[]{:S(2)}, u32[]{:S(2)}) collective-permute-start(bf16[2,128,1024]{2,1,0:T(8,128)(2,1)S(1)} %bitcast.56), channel_id=1, source_target_pairs={{0,2},{1,17},{2,0},{3,19},{4,6},{5,21},{6,4},{7,23},{8,10},{9,25},... | collective-permute-start | bytes 1572872 | tf_op jit(solution)/shard_map/ppermute | solution.py:409
  130.5 14.9 %collective-permute-start.20 = (bf16[128,2048]{1,0:T(8,128)(2,1)S(1)}, bf16[128,2048]{1,0:T(8,128)(2,1)S(1)}, u32[]{:S(2)}, u32[]{:S(2)}) collective-permute-start(bf16[128,2048]{1,0:T(8,128)(2,1)S(1)} %fusion.2), channel_id=1, source_target_pairs={{0,16},{1,3},{2,18},{3,1},{4,20},{5,7},{6,22},{7,5},{8,24},{9,11},... | collective-permute-start | bytes 1572872 | tf_op jit(solution)/shard_map/ppermute | solution.py:409
  132.3 19.7 %collective-permute-start.25 = (bf16[2,128,1024]{2,1,0:T(8,128)(2,1)S(1)}, bf16[2,128,1024]{2,1,0:T(8,128)(2,1)S(1)}, u32[]{:S(2)}, u32[]{:S(2)}) collective-permute-start(bf16[2,128,1024]{2,1,0:T(8,128)(2,1)S(1)} %bitcast.55), channel_id=1, source_target_pairs={{0,2},{1,17},{2,0},{3,19},{4,6},{5,21},{6,4},{7,23},{8,10},{9,25},... | collective-permute-start | bytes 1572872 | tf_op jit(solution)/shard_map/ppermute | solution.py:409
  143.0 10.4 %collective-permute-start.23 = (bf16[128,1024]{1,0:T(8,128)(2,1)S(1)}, bf16[128,1024]{1,0:T(8,128)(2,1)S(1)}, u32[]{:S(2)}, u32[]{:S(2)}) collective-permute-start(bf16[128,1024]{1,0:T(8,128)(2,1)S(1)} %fusion.8), channel_id=1, source_target_pairs={{0,16},{1,3},{2,18},{3,1},{4,20},{5,7},{6,22},{7,5},{8,24},{9,11},... | collective-permute-start | bytes 786440 | tf_op jit(solution)/shard_map/ppermute | solution.py:409
  152.1 6.4 %collective-permute-start.26 = (bf16[128,1024]{1,0:T(8,128)(2,1)S(1)}, bf16[128,1024]{1,0:T(8,128)(2,1)S(1)}, u32[]{:S(2)}, u32[]{:S(2)}) collective-permute-start(bf16[128,1024]{1,0:T(8,128)(2,1)S(1)} %fusion.6), channel_id=1, source_target_pairs={{0,16},{1,3},{2,18},{3,1},{4,20},{5,7},{6,22},{7,5},{8,24},{9,11},... | collective-permute-start | bytes 786440 | tf_op jit(solution)/shard_map/ppermute | solution.py:409
  (2 other events, 2.2 us)

commit v3 on v2

--- a/solution.py
+++ b/solution.py
@@ -34,6 +34,7 @@
 CROSSED = (0, 2, 1, 3)
 TILE = 16
 SCALE = 1.0 / math.sqrt(HD)
+SHORT = pl.CostEstimate(flops=1024, bytes_accessed=1024, transcendentals=0)
 LONG = pl.CostEstimate(flops=10**11, bytes_accessed=1024, transcendentals=0)
 
 
@@ -74,31 +75,50 @@
                 copy.wait()
 
 
-def copy_call(body, name, scalars, operands, out_shapes, scratch, copies):
-    anywhere = pl.BlockSpec(memory_space=pl.ANY)
+def copy_call(body, name, scalars, operands, out_shapes, scratch, copies, cost=LONG, room=10, far=(), inputs=pl.ANY):
     smem = pl.BlockSpec(memory_space=pltpu.SMEM)
     need = sum(math.prod(a.shape) * jnp.dtype(a.dtype).itemsize for a in scratch)
     return pl.pallas_call(
         body,
-        in_specs=[smem] * len(scalars) + [anywhere] * len(operands),
-        out_specs=[anywhere] * len(out_shapes),
+        in_specs=[smem] * len(scalars) + [pl.BlockSpec(memory_space=inputs)] * len(operands),
+        out_specs=[pl.BlockSpec(memory_space=pltpu.HBM if n in far else pl.ANY) for n in range(len(out_shapes))],
         out_shape=tuple(out_shapes),
         scratch_shapes=[pltpu.VMEM(a.shape, a.dtype) for a in scratch] + [pltpu.SemaphoreType.DMA((copies,))],
-        compiler_params=pltpu.CompilerParams(vmem_limit_bytes=need + (10 << 20)),
-        cost_estimate=LONG,
+        compiler_params=pltpu.CompilerParams(vmem_limit_bytes=need + (room << 20)),
+        cost_estimate=cost,
         name=name,
     )(*scalars, *operands)
 
 
-def slices_kernel(place, q, k, v, o, out):
+def after(array, *earlier):
+    return lax.optimization_barrier((array, *earlier))[0]
+
+
+def step_kernel(before, now):
+    now[0] = before[0] + 1
+
+
+def step(*ready):
+    smem = pl.BlockSpec(memory_space=pltpu.SMEM)
+    return pl.pallas_call(
+        step_kernel,
+        in_specs=[smem],
+        out_specs=smem,
+        out_shape=shape_of((1,), jnp.int32),
+        compiler_params=pltpu.CompilerParams(has_side_effects=True),
+        cost_estimate=LONG,
+        name="step",
+    )(after(*ready))
+
+
+def slices_kernel(place, q, k, v, o, early, late):
     depth, width = q.shape
     rank = k.shape[0]
-    out[:rank] = k[...]
-    out[rank : 2 * rank] = v[...]
-    out[2 * rank : 2 * rank + depth] = q[...]
+    early[:rank] = k[...]
+    early[rank : 2 * rank] = v[...]
+    early[2 * rank :] = q[...]
     for c in range(depth // width):
-        at = 2 * rank + depth + c * width
-        out[at : at + width] = o[:, c * width : (c + 1) * width]
+        late[c * width : (c + 1) * width] = o[:, c * width : (c + 1) * width]
 
 
 def projection_slices(chip, qw, kw, vw, ow):
@@ -109,17 +129,17 @@
         "projection_slices",
         (chip.reshape(1),),
         (qw, kw, vw, ow),
-        (shape_of((2 * rank + 2 * depth, width)),),
+        (shape_of((2 * rank + depth, width)), shape_of((depth, width))),
         [
             pl.BlockSpec((depth, width), column),
             pl.BlockSpec((rank, width), column),
             pl.BlockSpec((rank, width), column),
             pl.BlockSpec((width, depth), lambda i, place: (place[0], 0)),
         ],
-    )[0]
-
-
-def prepare_kernel(core, owners, ids, hid, db, gain, near, far):
+    )
+
+
+def prepare_kernel(core, owners, ids, hid, db, gain, _, near, far):
     rows, half = hid.shape
     blocks, e = db.shape[0] // 2, db.shape[2]
     per = rows // BLOCK
@@ -136,16 +156,16 @@
     near[:, near.shape[1] - lane.shape[1] :] = row.astype(F32).astype(BF16)
 
 
-def prepare(core, owners, ids, hidden, db, gain):
+def prepare(core, owners, ids, hidden, db, gain, earlier):
     rows, half = hidden.shape
     wide = db.shape[0] // 2 * BLOCK // rows * db.shape[2]
     return kernel_call(
         prepare_kernel,
         "prepare",
         (core.reshape(1), owners, ids),
-        (hidden, db, gain),
+        (hidden, db, gain, earlier),
         (shape_of((rows, half + wide + 128)), shape_of((rows, wide))),
-        [None] * 3,
+        [None] * 3 + [pl.BlockSpec(memory_space=pl.ANY)],
     )
 
 
@@ -161,6 +181,10 @@
     return jnp.concatenate(parts, axis=0)
 
 
+def span_rows(n):
+    return slice(n * SPAN, (n + 1) * SPAN)
+
+
 def head_cols(width, h):
     return slice(h * HD, (h + 1) * HD), slice(width + h * HD, width + (h + 1) * HD)
 
@@ -172,13 +196,18 @@
         copies.start(name, source, rows_of(target, slot * rows, rows))
 
 
-def stage_output(copies, pos, parts, target):
-    depth, width = parts[3].shape
-    for r, part in enumerate(parts):
-        for c in range(depth // width):
-            at = part.shape[0] - depth + c * width
-            place = pl.multiple_of(pos[r] * depth + c * width, width)
-            copies.start("output", rows_of(part, at, width), target.at[:, pl.ds(place, width)])
+def stage_output(copies, name, part, target):
+    width = part.shape[1]
+    for c in range(part.shape[0] // width):
+        copies.start(name, rows_of(part, c * width, width), target.at[:, pl.ds(c * width, width)])
+
+
+def project(core, mix, weights, theirs, mine, columns):
+    sub, rows = weights.shape[1] // 2, mix.shape[0] // 4
+    crossed = jnp.concatenate([mix[s * rows : (s + 1) * rows] for s in CROSSED])
+    for ref, tokens, which in ((theirs, crossed, 1 - core), (mine, mix[...], core)):
+        cut = pl.ds(pl.multiple_of(which * sub, sub), sub)
+        ref[:, columns] = dot(tokens, weights[:, cut]).astype(BF16)
 
 
 def forward_kernel(src, idx, pos, *refs):
@@ -216,19 +245,15 @@
     total = dot(near[...], weights[:half])
     copies.wait("far")
     queries[...] = (total + dot(far[...], weights[half:])).astype(BF16)
-    for span in range(spans):
-        rows = slice(span * SPAN, (span + 1) * SPAN)
-        heads = range(width // HD)
-        cols = [head_cols(width, h) for h in heads]
-        scores = [dot_t(queries[rows, kc], take_blocks(idx, kv, span, kc)) * SCALE for kc, _ in cols]
-        scores = [jnp.exp(s - jnp.max(s, axis=-1, keepdims=True)) for s in scores]
-        scores = [s * (1.0 / jnp.sum(s, axis=-1, keepdims=True)) for s in scores]
-        for h in heads:
-            att[span, h] = scores[h]
-            kc, vc = cols[h]
-            mix[rows, kc] = dot(scores[h].astype(BF16), take_blocks(idx, kv, span, vc)).astype(BF16)
-        if span % 2:
-            copies.start("out", rows_of(att, span - 1, 2), rows_of(att_out, span - 1, 2))
+    todo = [(span_rows(n), n, h, *head_cols(width, h)) for n in range(spans) for h in range(width // HD)]
+    scores = [dot_t(queries[rows, kc], take_blocks(idx, kv, n, kc)) * SCALE for rows, n, _, kc, _ in todo]
+    scores = [jnp.exp(s - jnp.max(s, axis=-1, keepdims=True)) for s in scores]
+    scores = [s * (1.0 / jnp.sum(s, axis=-1, keepdims=True)) for s in scores]
+    for s, (_, n, h, _, _) in zip(scores, todo):
+        att[n, h] = s
+    copies.start("out", att, att_out)
+    for s, (rows, n, _, kc, vc) in zip(scores, todo):
+        mix[rows, kc] = dot(s.astype(BF16), take_blocks(idx, kv, n, vc)).astype(BF16)
     copies.start("out", mix, mix_out)
     copies.wait("out")
 
@@ -259,125 +284,188 @@
             mix,
             att,
         ),
-        30 + spans // 2,
-    )
-
-
-def output_kernel(pos, *refs):
-    mix_in, parts = refs[0], refs[1:5]
-    theirs_out, mine_out, mix, weights, theirs, mine, sems = refs[5:]
-    tokens, half = mine.shape
-    rows = tokens // 4
+        31,
+        SHORT,
+        42,
+    )
+
+
+def output_kernel(core, *refs):
+    mix_in, parts = refs[0], refs[1:4]
+    theirs_out, mine_out, mix, weights, theirs, mine, sems = refs[4:]
+    sub = weights.shape[2] // 2
     copies = Copies(sems)
     copies.start("mix", mix_in, mix)
-    stage_output(copies, pos, parts, weights)
-    copies.wait("mix", "output")
-    crossed = jnp.concatenate([mix[CROSSED[s] * rows : (CROSSED[s] + 1) * rows] for s in range(4)])
-    for ref, out, tokens_of, first in ((theirs, theirs_out, crossed, half), (mine, mine_out, mix[...], 0)):
-        for c in range(4):
-            step = half // 4
-            cols = slice(c * step, (c + 1) * step)
-            ref[:, cols] = dot(tokens_of, weights[:, first + c * step : first + (c + 1) * step]).astype(BF16)
-        copies.start("out", ref, out)
+    for r, part in enumerate(parts):
+        stage_output(copies, r, part, weights.at[r])
+    copies.wait("mix")
+    for r in range(3):
+        copies.wait(r)
+        project(core[0], mix, weights.at[r], theirs, mine, slice(r * sub, (r + 1) * sub))
+    copies.start("out", theirs, theirs_out)
+    copies.start("out", mine, mine_out)
     copies.wait("out")
 
 
-def output_halves(pos, mix, parts):
+def output_slices(core, mix, parts):
     tokens, width = mix.shape
-    depth = parts[3].shape[0]
-    half = shape_of((tokens, 2 * depth))
+    depth = parts[0].shape[0]
+    out = shape_of((tokens, 3 * depth // 2))
     return copy_call(
         output_kernel,
-        "output_halves",
-        (pos,),
+        "output_slices",
+        (core.reshape(1),),
         (mix, *parts),
-        (half, half),
-        (mix, shape_of((width, 4 * depth)), half, half),
-        3 + 4 * depth // width,
+        (out, out),
+        (mix, shape_of((3, width, depth)), out, out),
+        3 + 3 * (depth // width),
+        far=(0,),
     )
 
 
 def cotangent_kernel(pos, *refs):
-    own, other, parts, gm_out = refs[:4], refs[4:8], refs[8:12], refs[12]
-    near, far, weights, gm, sems = refs[13:]
-    half = near.shape[1]
+    own, other, parts, gm_out, rest_out = refs[:4], refs[4:8], refs[8:11], refs[11], refs[12]
+    grads, weights, gm, sems = refs[13:]
+    rows, depth = own[0].shape[0], grads.shape[2]
     copies = Copies(sems)
-    stage_output(copies, pos, parts, weights)
-    stage_tokens(copies, "near", own, near)
-    stage_tokens(copies, "far", other, far)
-    copies.wait("output", "near")
-    total = dot_t(near[...], weights[:, :half])
-    copies.wait("far")
-    gm[...] = (total + dot_t(far[...], weights[:, half:])).astype(BF16)
+    for r, part in enumerate(parts):
+        stage_output(copies, r, part, weights.at[r])
+    for side, arrays in enumerate((own, other)):
+        for slot, a in enumerate(arrays):
+            for c in range(2):
+                target = grads.at[2 * side + c, pl.ds(slot * rows, rows)]
+                copies.start("grads", a.at[:, pl.ds(c * depth, depth)], target)
+    copies.wait("grads")
+    copies.start("out", grads.at[pos[3]], rest_out)
+    copies.wait(0, 1, 2)
+    gm[...] = sum(dot_t(grads[pos[r]], weights[r]) for r in range(3))
     copies.start("out", gm, gm_out)
     copies.wait("out")
 
 
 def cotangent(pos, own, other, parts):
-    rows, half = own[0].shape
-    depth, width = parts[3].shape
-    side, gm = shape_of((4 * rows, half)), shape_of((4 * rows, width))
+    tokens, (depth, width) = 4 * own[0].shape[0], parts[0].shape
+    gm = shape_of((tokens, width), F32)
     return copy_call(
         cotangent_kernel,
         "cotangent",
         (pos,),
         (*own, *other, *parts),
-        (gm,),
-        (side, side, shape_of((width, 4 * depth)), gm),
-        9 + 4 * depth // width,
+        (gm, shape_of((tokens, depth))),
+        (shape_of((4, tokens, depth)), shape_of((3, width, depth)), gm),
+        3 * (depth // width) + 16 + 2,
+    )
+
+
+def late_kernel(core, idx, pos, *refs):
+    gm_in, rest_in, part, mix_in, kv_in, att_in, parts, results = *refs[:6], refs[6:10], refs[10:16]
+    gmf, rest, wo, mix, kv, att, wq, gm, gq, crossed, wide, narrow, sems = refs[16:]
+    width, depth = wq.shape[1], wq.shape[0] // 4
+    spans, sub = att.shape[0], depth // 2
+    copies = Copies(sems)
+    stage_output(copies, "in", part, wo)
+    copies.start("in", rest_in, rest)
+    copies.start("in", gm_in, gmf)
+    copies.start("kv", kv_in, kv)
+    copies.start("kv", att_in, att)
+    copies.start("mix", mix_in, mix)
+    for r, piece in enumerate(parts):
+        place = pl.multiple_of(pos[r] * depth, depth)
+        copies.start("query", rows_of(piece, piece.shape[0] - depth, depth), rows_of(wq, place, depth))
+    copies.wait("in")
+    gm[...] = (gmf[...] + dot_t(rest[...], wo[...])).astype(BF16)
+    copies.wait("kv")
+    todo = [(span_rows(n), n, h, *head_cols(width, h)) for n in range(spans) for h in range(width // HD)]
+    grads = [dot_t(gm[rows, kc], take_blocks(idx, kv, n, vc)) for rows, n, _, kc, vc in todo]
+    inner = [jnp.sum(att[n, h] * g, axis=-1, keepdims=True) for g, (_, n, h, _, _) in zip(grads, todo)]
+    grads = [(att[n, h] * (g - a) * SCALE).astype(BF16) for g, a, (_, n, h, _, _) in zip(grads, inner, todo)]
+    for g, (rows, n, _, kc, _) in zip(grads, todo):
+        slot, within = divmod(n, spans // 4)
+        value = dot(g, take_blocks(idx, kv, n, kc)).astype(BF16)
+        gq[rows, kc] = value
+        crossed[span_rows(CROSSED[slot] * (spans // 4) + within), kc] = value
+    copies.wait("mix", "query")
+    project(core[0], mix, wo, wide.at[0], wide.at[1], slice(0, sub))
+    first = wide.shape[2] - sub
+    for n, (source, chunk, side) in enumerate(((crossed, 0, 2), (crossed, 1, 2), (gq, 0, 0), (gq, 1, 0))):
+        buffer = (narrow if chunk else wide).at[n // 2]
+        start, place = side * depth + chunk * first, 0 if chunk else sub
+        for at in range(0, buffer.shape[1] - place, 256):
+            value = dot_t(source[...], wq[start + at : start + at + 256])
+            buffer[:, place + at : place + at + 256] = value.astype(BF16)
+        if n < 2:
+            copies.start("out", buffer, results[n])
+        else:
+            rows = buffer.shape[0] // 2
+            for half in range(2):
+                copies.start("out", rows_of(buffer, half * rows, rows), results[2 * n - 2 + half])
+    copies.wait("out")
+
+
+def late_slices(core, idx, pos, gm, rest, part, mix, kv, att, parts):
+    tokens, width = gm.shape
+    depth = part.shape[0]
+    wide = shape_of((tokens, depth // 2 + depth))
+    narrow = shape_of((tokens, depth))
+    heads = shape_of((tokens, width))
+    return copy_call(
+        late_kernel,
+        "late_slices",
+        (core.reshape(1), idx, pos),
+        (gm, rest, part, mix, kv, att, *parts),
+        (wide, narrow, *(shape_of((tokens // 2, a.shape[1])) for a in (wide, wide, narrow, narrow))),
+        (
+            gm,
+            rest,
+            shape_of((width, depth)),
+            mix,
+            kv,
+            att,
+            shape_of((4 * depth, width)),
+            heads,
+            heads,
+            heads,
+            shape_of((2, *wide.shape)),
+            shape_of((2, *narrow.shape)),
+        ),
+        depth // width + 5 + 4 + 6,
+        room=43,
+        far=(0, 1),
+    )
+
+
+def add_kernel(firsts, *refs):
+    n = len(firsts)
+    arrays, out, held, sems = refs[:n], refs[n], refs[n + 1], refs[n + 2]
+    rows = held.shape[1] // 2
+    copies = Copies(sems)
+    for part in range(2):
+        for k, array in enumerate(arrays):
+            copies.start(part, rows_of(array, firsts[k] + part * rows, rows), rows_of(held.at[k], part * rows, rows))
+    for part in range(2):
+        cut = slice(part * rows, (part + 1) * rows)
+        copies.wait(part)
+        held[0, cut] = sum(held[k, cut].astype(F32) for k in range(n)).astype(BF16)
+        copies.start("out", rows_of(held.at[0], part * rows, rows), rows_of(out, part * rows, rows))
+    copies.wait("out")
+
+
+def add_rows(rows, *terms):
+    arrays, firsts = zip(*terms)
+    shape = (rows, arrays[0].shape[1])
+    return copy_call(
+        lambda *refs: add_kernel(firsts, *refs),
+        "add_rows",
+        (),
+        arrays,
+        (shape_of(shape),),
+        (shape_of((len(arrays), *shape)),),
+        2 * len(arrays) + 2,
+        SHORT,
+        room=46,
+        far=(0,),
+        inputs=pltpu.HBM,
     )[0]
-
-
-def backward_kernel(idx, pos, *refs):
-    gm_in, kv_in, att_in, parts, results = refs[0], refs[1], refs[2], refs[3:7], refs[7:11]
-    gm, kv, att, wq, gq, crossed, buffers, sems = refs[11:]
-    width, depth = wq.shape[1], wq.shape[0] // 4
-    spans = att.shape[0]
-    copies = Copies(sems)
-    copies.start("in", gm_in, gm)
-    copies.start("in", kv_in, kv)
-    copies.start("in", att_in, att)
-    for r, part in enumerate(parts):
-        place = pl.multiple_of(pos[r] * depth, depth)
-        first = part.shape[0] - 2 * depth if r < 3 else part.shape[0] - depth
-        copies.start("query", rows_of(part, first, depth), rows_of(wq, place, depth))
-    copies.wait("in")
-    for span in range(spans):
-        slot, rest = divmod(span, spans // 4)
-        rows = slice(span * SPAN, (span + 1) * SPAN)
-        there = (CROSSED[slot] * (spans // 4) + rest) * SPAN
-        heads = range(width // HD)
-        cols = [head_cols(width, h) for h in heads]
-        grads = [dot_t(gm[rows, kc], take_blocks(idx, kv, span, vc)) for kc, vc in cols]
-        inner = [jnp.sum(att[span, h] * grads[h], axis=-1, keepdims=True) for h in heads]
-        grads = [(att[span, h] * (grads[h] - inner[h]) * SCALE).astype(BF16) for h in heads]
-        for h in heads:
-            kc, _ = cols[h]
-            value = dot(grads[h], take_blocks(idx, kv, span, kc)).astype(BF16)
-            gq[rows, kc] = value
-            crossed[there : there + SPAN, kc] = value
-    copies.wait("query")
-    for n, (source, slice_of) in enumerate(((crossed, 2), (crossed, 3), (gq, 0), (gq, 1))):
-        for c in range(2):
-            step = depth // 2
-            at = slice_of * depth + c * step
-            buffers[n, :, c * step : (c + 1) * step] = dot_t(source[...], wq[at : at + step]).astype(BF16)
-        copies.start("out", buffers.at[n], results[n])
-    copies.wait("out")
-
-
-def backward(idx, pos, gm, kv, att, parts, depth):
-    tokens, width = gm.shape
-    chunk = shape_of((tokens, depth))
-    return copy_call(
-        backward_kernel,
-        "backward",
-        (idx, pos),
-        (gm, kv, att, *parts),
-        (chunk,) * 4,
-        (gm, kv, att, shape_of((4 * depth, width)), gm, gm, shape_of((4, tokens, depth))),
-        11,
-    )
 
 
 def flat(y, z, x, m):
@@ -407,10 +495,6 @@
 
 def move(array, pairs):
     return lax.ppermute(array, AXES, pairs)
-
-
-def after(array, *earlier):
-    return lax.optimization_barrier((array, *earlier))[0]
 
 
 def phase(*arrays):
@@ -436,24 +520,31 @@
     rows, half = hidden.shape
     nxt = lax.rem(2 * z + 1 - z // 2, 4)
     sources = (z, 3 - nxt, nxt, 3 - z)
-    pos = jnp.stack([s ^ (2 * m) for s in sources])
-    sources = jnp.stack(sources)
-
-    weights = projection_slices(y * 2 + x, query_weight, key_weight, value_weight, out_weight)
-    up, down = move(weights, UP), move(weights, DOWN)
-    he, e_far = prepare(m, owners, block_ids, after(hidden, weights), database, enc_gain)
-    he_own = (he, move(he, SECOND), move(he, FIRST), move(he, DIAGONAL))
-    up, down, pos, sources, *he_own = phase(up, down, pos, sources, *he_own)
-
-    near_far = move(up[: 2 * rank + depth], UP)
+    def codes_of(array):
+        return array[0, array.shape[1] - 128 :][:UNITS].astype(jnp.int32)
+
+    early, late = projection_slices(y * 2 + x, query_weight, key_weight, value_weight, out_weight)
+    early_up, early_down = move(early, UP), move(early, DOWN)
+    he, e_far = prepare(m, owners, block_ids, hidden, database, enc_gain, early)
+    he_first, he_second = move(he, FIRST), move(he, SECOND)
+    g_first = move(grad_out, FIRST)
+    places = [s ^ (2 * m) for s in sources]
+    turn, zz = after(m, early_up, early_down), after(z, early_up, early_down)
+    nxt = lax.rem(2 * zz + 1 - zz // 2, 4)
+    sources = (zz, 3 - nxt, nxt, 3 - zz)
+    pos, sources = jnp.stack([s ^ (2 * turn) for s in sources]), jnp.stack(sources)
+    codes = codes_of(after(he, pos))
+    he_first, he_second, g_first, codes = phase(he_first, he_second, g_first, codes)
     h_zero = move(hidden, CORE)
-    he_other = (h_zero,) + tuple(move(he_own[CROSSED[i]], CORE) for i in (1, 2, 3))
-    o_far = move(after(up[2 * rank + depth :], *he_other), UP)
-    g = after(grad_out, *he_other)
-    g_own = (grad_out, move(g, SECOND), move(g, FIRST), move(g, DIAGONAL))
+    early_far = move(after(early_up, he_first, he_second), UP)
+    he_last = move(he_first, SECOND)
+    he_two, he_one = move(he_first, CORE), move(he_second, CORE)
+    codes_last = move(after(he, he_first)[:TILE, he.shape[1] - 128 :], DIAGONAL)
+    g_zero = move(grad_out, CORE)
+    codes = jnp.stack([codes] + [codes_of(a) for a in (he_second, he_first, codes_last)])
+    he_own = (he, he_second, he_first, he_last)
 
     per = rows // BLOCK
-    codes = jnp.stack([after(a, *he_other)[0, a.shape[1] - 128 :][:UNITS] for a in he_own]).astype(jnp.int32)
     own_of, id_of = codes // (2 * blocks), codes % (2 * blocks)
     slot = jnp.arange(4, dtype=jnp.int32)
     rel_x = own_of ^ x
@@ -463,42 +554,77 @@
     idx = (block // per * 8 + (holder ^ m) * 4 + bank) * per + block % per
     idx = (idx * (BLOCK // TILE)).reshape(-1, UPC).astype(jnp.int32)
 
-    parts = (weights, up, down, near_far)
-    kv, mixture, attention = forward(sources, idx, pos, he_own, e_far, he_other, parts, half, e, depth)
-    mixture, o_far, *g_own = phase(mixture, o_far, *g_own[1:])
-    g_own = (grad_out, *g_own)
+    he_two, he_one, idx = phase(he_two, he_one, idx)
+    early_far = after(early_far, he_two)
+    he_last = after(he_last, early_far)
+    he_three = move(he_last, CORE)
+    he_own = (*he_own[:3], he_last)
+    he_other = (h_zero, he_two, he_one, he_three)
+    g_second, g_last = move(grad_out, SECOND), move(g_first, SECOND)
+    late_up, late_down = move(after(late, idx), UP), move(after(late, idx), DOWN)
+    earlies = (early, early_up, early_down, early_far)
+    kv, mixture, attention = forward(sources, idx, pos, he_own, e_far, he_other, earlies, half, e, depth)
+    late_up, late_down, g_second, g_last, mixture = phase(late_up, late_down, g_second, g_last, mixture)
+
+    late_far = move(late_up, UP)
+    g_two, g_one, g_three = move(g_first, CORE), move(g_second, CORE), move(g_last, CORE)
+    lates = (late, late_up, late_down)
+    o_theirs, o_mine = output_slices(m, mixture, lates)
+    g_two, g_one, g_three, o_mine = phase(g_two, g_one, g_three, o_mine)
+
+    def slots(array):
+        return array.reshape(-1, rows, array.shape[1])
 
     def begin(mine, theirs):
-        return move((mine[2:].astype(F32) + theirs[2:].astype(F32)).astype(BF16), FIRST)
+        return (mine.astype(F32) + theirs[2:].astype(F32)).astype(BF16)
 
     def carry_on(mine, theirs, first):
-        total = mine[1].astype(F32) + theirs[1].astype(F32) + first[1].astype(F32)
-        return move(total.astype(BF16), SECOND)
+        return (mine[1].astype(F32) + theirs[1].astype(F32) + first[1].astype(F32)).astype(BF16)
 
     def finish(mine, theirs, first, second):
         return sum(a.astype(F32) for a in (mine[0], theirs[0], first[0], second))
 
-    def slots(array):
-        return array.reshape(4, rows, -1)
-
-    g_other = tuple(move(g_own[CROSSED[i]], CORE) for i in range(4))
-    outs = (weights, up, down, o_far)
-    o_theirs, o_mine = output_halves(pos, mixture, outs)
     o_theirs, o_mine = slots(move(o_theirs, CORE)), slots(o_mine)
-    gm = cotangent(pos, g_own, (g_other[0], after(g_other[1], o_mine), *g_other[2:]), outs)
+    g_other = (g_zero, g_two, g_one, g_three)
+    gm, rest = cotangent(pos, (grad_out, g_second, g_first, g_last), g_other, lates)
     o_theirs = after(o_theirs, gm)
-    o_first = begin(o_mine, o_theirs)
-    t0, t1, m0, m1 = backward(idx, pos, after(gm, o_theirs), kv, attention, parts, depth)
-    t0, t1 = after(t0, o_first), after(t1, o_first)
-    t0, t1 = slots(move(t0, CORE)), slots(move(t1, CORE))
-    m0, m1 = slots(m0), slots(m1)
-    first0, first1 = begin(m0, t0), begin(m1, t1)
-    o_second = carry_on(o_mine, o_theirs, o_first)
-    second0, second1 = carry_on(m0, t0, first0), carry_on(m1, t1, first1)
-    summed = finish(o_mine, o_theirs, o_first, o_second)
-    grad_sum = jnp.concatenate((finish(m0, t0, first0, second0), finish(m1, t1, first1, second1)), axis=1)
+    o_send = begin(o_mine[2:], o_theirs)
+    o_first = move(o_send, FIRST)
+    late_far = after(late_far, o_send)
+    t0, t1, m0, n0, m1, n1 = late_slices(m, idx, pos, gm, rest, late_far, mixture, kv, attention, earlies)
+    t0, t1, o_first = phase(t0, t1, o_first)
+    t0, t1 = move(t0, CORE), move(t1, CORE)
+    send0 = add_rows(2 * rows, (n0, 0), (t0, 2 * rows))
+    send1 = add_rows(2 * rows, (n1, 0), (after(t1, send0), 2 * rows))
+    t0, t1, m0, m1, send0, send1 = (slots(a) for a in (t0, t1, m0, m1, send0, send1))
+    first0, first1 = move(send0, FIRST), move(send1, FIRST)
+    o_next = carry_on(o_mine, o_theirs, after(o_first, send0))
+    o_second = move(o_next, SECOND)
+    first0 = after(first0, o_next)
+    next0 = carry_on(m0, t0, first0)
+    second0 = move(next0, SECOND)
+    first1 = after(first1, next0)
+    next1 = carry_on(m1, t1, first1)
+    second1 = move(next1, SECOND)
+    sub = depth // 2
+    o_sum = finish(o_mine, o_theirs, o_first, after(o_second, next1))
+    sum0 = finish(m0, t0, first0, after(second0, next1))
+
+    pieces = [o_sum[:, i * sub : (i + 1) * sub] for i in range(3)] + [sum0[:, :sub]]
+    whole = jnp.zeros((4,) + pieces[0].shape, F32)
+    for piece, place in zip(pieces, places):
+        whole = lax.dynamic_update_slice_in_dim(whole, piece[None], place, 0)
+    swapped = move(whole[2:].astype(BF16), CORE).astype(F32)
+    low = jnp.where(m == 0, whole[:2], swapped)
+    high = jnp.where(m == 0, swapped, whole[:2])
+    summed = jnp.concatenate((low[0], high[0], low[1], high[1]), axis=1)
     output = (hidden.astype(F32) + summed).astype(BF16)
-    grad_hidden = (grad_out.astype(F32) + grad_sum).astype(BF16)
+
+    edge = sum0.shape[1] - sub
+    rest1 = m1[0].astype(F32) + t1[0].astype(F32) + first1[0].astype(F32)
+    base = grad_out.astype(F32) + jnp.concatenate((sum0[:, sub:], rest1), axis=1)
+    second1 = after(second1, base, whole)
+    grad_hidden = (base + jnp.pad(second1.astype(F32), ((0, 0), (edge, 0)))).astype(BF16)
     return (output, grad_hidden)
 
 

time: 161 us -> 159 us (0.988)
  waiting for transfers between devices: 91.3 us -> 75.3 us
  starting transfers between devices: 23.2 us -> 32 us
  other arithmetic: 5.96 us -> 10.5 us
    ppermute x27 -> x31, waiting for transfers between devices: 91.3 us -> 75.3 us  [move(): return lax.ppermute(array, AXES, pairs)]
    ppermute x27 -> x31, starting transfers between devices: 23.2 us -> 32 us  [move(): return lax.ppermute(array, AXES, pairs)]
    slice x7 -> x4, local copies, waits for them, and re-layouts: 4.55 us -> 0.81 us  [the longest x1 0.69 us: local_plane(): codes_last = move(after(he, he_first)[:TILE, he.shape[1] - 128:], DIAGONAL)]
    unnamed x14 -> x42, local copies, waits for them, and re-layouts: 3.6 us -> 6.94 us
    add x2, other arithmetic: 0.31 us -> 2.36 us  [finish(): return sum((a.astype(F32) for a in (mine[0], theirs[0], first[0], second)))]
    convert_element_type x8 -> x7, other arithmetic: 3.21 us -> 4.85 us  [the longest x2 2.4 us: carry_on(): (mine[1].astype(F32) + theirs[1].astype(F32) + first[1].astype(F32)).asty...]
    pallas_call x4 -> x6, Pallas kernels: 24.9 us -> 25 us  [copy_call(): pl.pallas_call(body, in_specs=[smem] * len(scalars) + [pl.BlockSpec(memor...]
  transfers between devices with their start and end apart: 27 -> 31, of which waited for: 12 -> 12; matrix products, arithmetic and copies ran while one was open for 5% -> 7% of each run, Pallas kernels for 18% -> 18%
where the time goes in v3:
time: 159 us; the launch traced here: 158 us
  waiting for transfers between devices  75.3 us (47%)
  starting transfers between devices  32 us (20%)
  Pallas kernels  31 us (19%)
  other arithmetic  10.5 us (7%)
  local copies, waits for them, and re-layouts  8.43 us (5%)
    ppermute x31, waiting for transfers between devices, move(): return lax.ppermute(array, AXES, pairs)  75.3 us
    ppermute x31, starting transfers between devices, move(): return lax.ppermute(array, AXES, pairs)  32 us
    pallas_call x6, Pallas kernels, copy_call(): pl.pallas_call(body, in_specs=[smem] * len(scalars) + [pl.BlockSpec(memor...  25 us
    unnamed x42, local copies, waits for them, and re-layouts  6.94 us
    pallas_call x2, Pallas kernels, kernel_call(): pl.pallas_call(body, grid_spec=pltpu.PrefetchScalarGridSpec(num_scalar_pr...  6.02 us
  transfers between devices with their start and end apart: 31, of which 12 were waited for; matrix products, arithmetic and copies ran while one was open for 7% of the time, Pallas kernels for 18%

profile of v3, /device:TPU:0, one launch (start us, length us, event | category | flops | bytes accessed | tf_op | source)
XLA Modules:
  0.0 158.3 jit_solution(6988211045050226144)
XLA Ops:
  0.6 2.4 %projection_slices.1 = (bf16[1472,256]{1,0:T(8,128)(2,1)}, bf16[1024,256]{1,0:T(8,128)(2,1)}) custom-call(s32[1]{0:T(128)} %bitcast.1.place, bf16[1024,1024]{1,0:T(8,128)(2,1)} %q.1, bf16[224,1024]{1,0:T(8,128)(2,1)} %k.1, bf16[224,1024]{1,0:T(8,128)(2,1)} %v.1, bf16[1024,1024]{1,0:T(8,128)(2,1)} %o.1), custom_call_target="tpu_custom_call" | custom-call | flops 99999997952 | bytes 1024 | tf_op jit(solution)/shard_map/projection_slices/pallas_call | solution.py:47
  3.0 3.0 %collective-permute-start.3 = (bf16[1472,256]{1,0:T(8,128)(2,1)}, bf16[1472,256]{1,0:T(8,128)(2,1)S(1)}, u32[]{:S(2)}, u32[]{:S(2)}) collective-permute-start(bf16[1472,256]{1,0:T(8,128)(2,1)} %get-tuple-element.55._.refs_12_.refs_6_), channel_id=1, source_target_pairs={{0,4},{1,5},{2,6},{3,7},{4,12},{5,13},{6,14},{7,15},{8,0},{9,1},{1... | collective-permute-start | bytes 2261000 | tf_op jit(solution)/shard_map/ppermute | solution.py:497
  7.1 3.6 %prepare.1 = (bf16[128,3968]{1,0:T(8,128)(2,1)}, bf16[128,1792]{1,0:T(8,128)(2,1)}) custom-call(s32[1]{0:T(128)} %bitcast.core, s32[2,4]{1,0:T(2,128)} %owners.1, s32[2,4]{1,0:T(2,128)} %ids.1, bf16[128,2048]{1,0:T(8,128)(2,1)} %hid.1, bf16[8,64,896]{2,1,0:T(8,128)(2,1)} %db.1, f32[896]{0:T(1024)} %gain.1, bf16[1472,256]{1,0:T(8,128)(2,1)} %get-tuple-element.55._.refs_12_.refs_6_), custom_call_target="tpu_custom_call" | custom-call | flops 99999997952 | bytes 1024 | tf_op jit(solution)/shard_map/prepare/pallas_call | solution.py:47
  10.7 1.8 %collective-permute-start = (bf16[128,3968]{1,0:T(8,128)(2,1)}, bf16[128,3968]{1,0:T(8,128)(2,1)S(1)}, u32[]{:S(2)}, u32[]{:S(2)}) collective-permute-start(bf16[128,3968]{1,0:T(8,128)(2,1)} %get-tuple-element.65.refs_0_), channel_id=1, source_target_pairs={{0,2},{1,17},{2,0},{3,19},{4,6},{5,21},{6,4},{7,23},{8,10},{9,25},... | collective-permute-start | bytes 3047432 | tf_op jit(solution)/shard_map/ppermute | solution.py:497
  12.5 1.5 collective-permute-start.1
  14.6 9.7 %collective-permute-done.3.refs_13_.refs_7_ = bf16[1472,256]{1,0:T(8,128)(2,1)S(1)} collective-permute-done((bf16[1472,256]{1,0:T(8,128)(2,1)}, bf16[1472,256]{1,0:T(8,128)(2,1)S(1)}, u32[]{:S(2)}, u32[]{:S(2)}) %collective-permute-start.3) | collective-permute-done | bytes 753696 | tf_op jit(solution)/shard_map/ppermute | solution.py:497
  24.2 16.1 %collective-permute-done.4.refs_14_.refs_8_ = bf16[1472,256]{1,0:T(8,128)(2,1)} collective-permute-done((bf16[1472,256]{1,0:T(8,128)(2,1)}, bf16[1472,256]{1,0:T(8,128)(2,1)}, u32[]{:S(2)}, u32[]{:S(2)}) %collective-permute-start.4) | collective-permute-done | bytes 753696 | tf_op jit(solution)/shard_map/ppermute | solution.py:497
  43.2 1.5 collective-permute-start.13
  45.1 1.7 %collective-permute-start.14 = (bf16[1472,256]{1,0:T(8,128)(2,1)S(1)}, bf16[1472,256]{1,0:T(8,128)(2,1)}, u32[]{:S(2)}, u32[]{:S(2)}) collective-permute-start(bf16[1472,256]{1,0:T(8,128)(2,1)S(1)} %collective-permute-done.3.refs_13_.refs_7_), channel_id=1, source_target_pairs={{0,4},{1,5},{2,6},{3,7},{4,12},{5,13},{6,14},{7,15},{8,0},{9,1},{1... | collective-permute-start | bytes 2261000 | tf_op jit(solution)/shard_map/ppermute | solution.py:497
  47.5 1.4 collective-permute-start.8
  49.6 2.5 %collective-permute-done.8 = bf16[16,128]{1,0:T(8,128)(2,1)S(1)} collective-permute-done((bf16[16,128]{1,0:T(8,128)(2,1)S(1)}, bf16[16,128]{1,0:T(8,128)(2,1)S(1)}, u32[]{:S(2)}, u32[]{:S(2)}) %collective-permute-start.8) | collective-permute-done | bytes 4128 | tf_op jit(solution)/shard_map/ppermute | solution.py:497
  52.1 6.1 %collective-permute-start.16 = (bf16[128,2048]{1,0:T(8,128)(2,1)}, bf16[128,2048]{1,0:T(8,128)(2,1)}, u32[]{:S(2)}, u32[]{:S(2)}) collective-permute-start(bf16[128,2048]{1,0:T(8,128)(2,1)} %hid.1), channel_id=1, source_target_pairs={{0,1},{1,0},{2,3},{3,2},{4,5},{5,4},{6,7},{7,6},{8,9},{9,8},{10,11... | collective-permute-start | bytes 1572872 | tf_op jit(solution)/shard_map/ppermute | solution.py:497
  59.0 5.6 %collective-permute-done.14.refs_15_.refs_9_ = bf16[1472,256]{1,0:T(8,128)(2,1)} collective-permute-done((bf16[1472,256]{1,0:T(8,128)(2,1)S(1)}, bf16[1472,256]{1,0:T(8,128)(2,1)}, u32[]{:S(2)}, u32[]{:S(2)}) %collective-permute-start.14) | collective-permute-done | bytes 753696 | tf_op jit(solution)/shard_map/ppermute | solution.py:497
  64.6 1.5 collective-permute-start.11
  66.6 1.6 collective-permute-start.10
  70.2 10.4 %forward.1 = (bf16[2048,512]{1,0:T(8,128)(2,1)}, bf16[512,256]{1,0:T(8,128)(2,1)}, f32[8,2,64,256]{3,2,1,0:T(8,128)}) custom-call(s32[4]{0:T(128)} %pad_add_fusion.2.src, s32[8,4]{1,0:T(8,128)} %fusion.16.idx, s32[4]{0:T(128)} %pad_add_fusion.1.pos, bf16[128,3968]{1,0:T(8,128)(2,1)} %get-tuple-element.65.refs_0_, ...), custom_call_target="tpu_custom_call" | custom-call | flops 1024 | bytes 1024 | tf_op jit(solution)/shard_map/forward/pallas_call | solution.py:81
  80.7 12.9 %collective-permute-done.9.refs_2_.refs_9_ = bf16[1024,256]{1,0:T(8,128)(2,1)} collective-permute-done((bf16[1024,256]{1,0:T(8,128)(2,1)S(1)}, bf16[1024,256]{1,0:T(8,128)(2,1)}, u32[]{:S(2)}, u32[]{:S(2)}) %collective-permute-start.9) | collective-permute-done | bytes 524320 | tf_op jit(solution)/shard_map/ppermute | solution.py:497
  95.1 2.4 %output_slices.1 = (bf16[512,1536]{1,0:T(8,128)(2,1)S(1)}, bf16[512,1536]{1,0:T(8,128)(2,1)S(1)}) custom-call(s32[1]{0:T(128)} %bitcast.core, bf16[512,256]{1,0:T(8,128)(2,1)S(1)} %copy-done.8, bf16[1024,256]{1,0:T(8,128)(2,1)S(1)} %copy-done.7, bf16[1024,256]{1,0:T(8,128)(2,1)} %collective-permute-done.9.refs_2_.refs_9_, ...), custom_call_target="tpu_custom_call" | custom-call | flops 99999997952 | bytes 1024 | tf_op jit(solution)/shard_map/output_slices/pallas_call | solution.py:81
  97.6 3.0 %cotangent.1 = (f32[512,256]{1,0:T(8,128)S(1)}, bf16[512,1024]{1,0:T(8,128)(2,1)S(1)}) custom-call(s32[4]{0:T(128)S(1)} %copy-done.6, bf16[128,2048]{1,0:T(8,128)(2,1)S(1)} %copy-done.3, bf16[128,2048]{1,0:T(8,128)(2,1)S(1)} %collective-permute-done.11.refs_1_, bf16[128,2048]{1,0:T(8,128)(2,1)S(1)} %collective-permute-done.2.refs_2_, ...), custom_call_target="tpu_custom_call" | custom-call | flops 99999997952 | bytes 1024 | tf_op jit(solution)/shard_map/cotangent/pallas_call | solution.py:81
  102.4 6.8 %collective-permute-done.21.refs_2_ = bf16[1024,256]{1,0:T(8,128)(2,1)} collective-permute-done((bf16[1024,256]{1,0:T(8,128)(2,1)}, bf16[1024,256]{1,0:T(8,128)(2,1)}, u32[]{:S(2)}, u32[]{:S(2)}) %collective-permute-start.21) | collective-permute-done | bytes 524320 | tf_op jit(solution)/shard_map/ppermute | solution.py:497
  109.2 7.5 %late_slices.1 = (bf16[512,1536]{1,0:T(8,128)(2,1)}, bf16[512,1024]{1,0:T(8,128)(2,1)}, bf16[256,1536]{1,0:T(8,128)(2,1)}, bf16[256,1536]{1,0:T(8,128)(2,1)}, bf...) custom-call(s32[1]{0:T(128)} %bitcast.core, s32[8,4]{1,0:T(8,128)} %fusion.16.idx, s32[4]{0:T(128)} %pad_add_fusion.1.pos, ...), custom_call_target="tpu_custom_call" | custom-call | flops 99999997952 | bytes 1024 | tf_op jit(solution)/shard_map/late_slices/pallas_call | solution.py:81
  117.3 3.1 %collective-permute-done.23.refs_1_ = bf16[512,1536]{1,0:T(8,128)(2,1)S(1)} collective-permute-done((bf16[512,1536]{1,0:T(8,128)(2,1)}, bf16[512,1536]{1,0:T(8,128)(2,1)S(1)}, u32[]{:S(2)}, u32[]{:S(2)}) %collective-permute-start.23) | collective-permute-done | bytes 1572896 | tf_op jit(solution)/shard_map/ppermute | solution.py:497
  121.6 1.4 add_rows.2
  125.0 1.6 collective-permute-start.26
  126.6 1.3 fusion.4
  127.9 1.6 %collective-permute-start.24 = (bf16[128,1536]{1,0:T(8,128)(2,1)S(1)}, bf16[128,1536]{1,0:T(8,128)(2,1)S(1)}, u32[]{:S(2)}, u32[]{:S(2)}) collective-permute-start(bf16[128,1536]{1,0:T(8,128)(2,1)S(1)} %fusion.4), channel_id=1, source_target_pairs={{0,16},{1,3},{2,18},{3,1},{4,20},{5,7},{6,22},{7,5},{8,24},{9,11},... | collective-permute-start | bytes 1179656 | tf_op jit(solution)/shard_map/ppermute | solution.py:497
  129.4 9.9 %collective-permute-done.27 = bf16[2,128,1536]{2,1,0:T(8,128)(2,1)} collective-permute-done((bf16[2,128,1536]{2,1,0:T(8,128)(2,1)S(1)}, bf16[2,128,1536]{2,1,0:T(8,128)(2,1)}, u32[]{:S(2)}, u32[]{:S(2)}) %collective-permute-start.27) | collective-permute-done | bytes 786464 | tf_op jit(solution)/shard_map/ppermute | solution.py:497
  140.5 1.6 %collective-permute-start.28 = (bf16[128,1536]{1,0:T(8,128)(2,1)S(1)}, bf16[128,1536]{1,0:T(8,128)(2,1)S(1)}, u32[]{:S(2)}, u32[]{:S(2)}) collective-permute-start(bf16[128,1536]{1,0:T(8,128)(2,1)S(1)} %fusion.3), channel_id=1, source_target_pairs={{0,16},{1,3},{2,18},{3,1},{4,20},{5,7},{6,22},{7,5},{8,24},{9,11},... | collective-permute-start | bytes 1179656 | tf_op jit(solution)/shard_map/ppermute | solution.py:497
  142.1 6.7 %collective-permute-done.26 = bf16[2,128,1024]{2,1,0:T(8,128)(2,1)S(1)} collective-permute-done((bf16[2,128,1024]{2,1,0:T(8,128)(2,1)S(1)}, bf16[2,128,1024]{2,1,0:T(8,128)(2,1)S(1)}, u32[]{:S(2)}, u32[]{:S(2)}) %collective-permute-start.26) | collective-permute-done | bytes 524320 | tf_op jit(solution)/shard_map/ppermute | solution.py:497
  149.0 1.6 %collective-permute-start.30 = (bf16[128,1024]{1,0:T(8,128)(2,1)S(1)}, bf16[128,1024]{1,0:T(8,128)(2,1)S(1)}, u32[]{:S(2)}, u32[]{:S(2)}) collective-permute-start(bf16[128,1024]{1,0:T(8,128)(2,1)S(1)} %get-tuple-element.109), channel_id=1, source_target_pairs={{0,16},{1,3},{2,18},{3,1},{4,20},{5,7},{6,22},{7,5},{8,24},{9,11},... | collective-permute-start | bytes 786440 | tf_op jit(solution)/shard_map/ppermute | solution.py:497
  150.6 1.2 fusion.5
  152.0 1.2 fusion.2
  (114 shorter events, 23.1 us)
Async XLA Ops:
  3.0 21.2 %collective-permute-start.3 = (bf16[1472,256]{1,0:T(8,128)(2,1)}, bf16[1472,256]{1,0:T(8,128)(2,1)S(1)}, u32[]{:S(2)}, u32[]{:S(2)}) collective-permute-start(bf16[1472,256]{1,0:T(8,128)(2,1)} %get-tuple-element.55._.refs_12_.refs_6_), channel_id=1, source_target_pairs={{0,4},{1,5},{2,6},{3,7},{4,12},{5,13},{6,14},{7,15},{8,0},{9,1},{1... | collective-permute-start | bytes 2261000 | tf_op jit(solution)/shard_map/ppermute | solution.py:497
  6.1 34.3 %collective-permute-start.4 = (bf16[1472,256]{1,0:T(8,128)(2,1)}, bf16[1472,256]{1,0:T(8,128)(2,1)}, u32[]{:S(2)}, u32[]{:S(2)}) collective-permute-start(bf16[1472,256]{1,0:T(8,128)(2,1)} %get-tuple-element.55._.refs_12_.refs_6_), channel_id=1, source_target_pairs={{0,8},{1,9},{2,10},{3,11},{4,0},{5,1},{6,2},{7,3},{8,12},{9,13},{1... | collective-permute-start | bytes 2261000 | tf_op jit(solution)/shard_map/ppermute | solution.py:497
  7.1 59.5 %copy-start.7 = (bf16[1024,256]{1,0:T(8,128)(2,1)S(1)}, bf16[1024,256]{1,0:T(8,128)(2,1)}, u32[]{:S(2)}) copy-start(bf16[1024,256]{1,0:T(8,128)(2,1)} %get-tuple-element.67.refs_1_.refs_8_) | copy-start | bytes 1572868
  10.7 31.0 %collective-permute-start = (bf16[128,3968]{1,0:T(8,128)(2,1)}, bf16[128,3968]{1,0:T(8,128)(2,1)S(1)}, u32[]{:S(2)}, u32[]{:S(2)}) collective-permute-start(bf16[128,3968]{1,0:T(8,128)(2,1)} %get-tuple-element.65.refs_0_), channel_id=1, source_target_pairs={{0,2},{1,17},{2,0},{3,19},{4,6},{5,21},{6,4},{7,23},{8,10},{9,25},... | collective-permute-start | bytes 3047432 | tf_op jit(solution)/shard_map/ppermute | solution.py:497
  12.5 30.2 %collective-permute-start.1 = (bf16[128,3968]{1,0:T(8,128)(2,1)}, bf16[128,3968]{1,0:T(8,128)(2,1)}, u32[]{:S(2)}, u32[]{:S(2)}) collective-permute-start(bf16[128,3968]{1,0:T(8,128)(2,1)} %get-tuple-element.65.refs_0_), channel_id=1, source_target_pairs={{0,16},{1,3},{2,18},{3,1},{4,20},{5,7},{6,22},{7,5},{8,24},{9,11},... | collective-permute-start | bytes 3047432 | tf_op jit(solution)/shard_map/ppermute | solution.py:497
  14.0 27.7 %collective-permute-start.2 = (bf16[128,2048]{1,0:T(8,128)(2,1)S(1)}, bf16[128,2048]{1,0:T(8,128)(2,1)S(1)}, u32[]{:S(2)}, u32[]{:S(2)}) collective-permute-start(bf16[128,2048]{1,0:T(8,128)(2,1)S(1)} %copy-done.3), channel_id=1, source_target_pairs={{0,2},{1,17},{2,0},{3,19},{4,6},{5,21},{6,4},{7,23},{8,10},{9,25},... | collective-permute-start | bytes 1572872 | tf_op jit(solution)/shard_map/ppermute | solution.py:497
  42.7 16.3 %collective-permute-start.6 = (bf16[128,3968]{1,0:T(8,128)(2,1)}, bf16[128,3968]{1,0:T(8,128)(2,1)S(1)}, u32[]{:S(2)}, u32[]{:S(2)}) collective-permute-start(bf16[128,3968]{1,0:T(8,128)(2,1)} %copy-done.14), channel_id=1, source_target_pairs={{0,1},{1,0},{2,3},{3,2},{4,5},{5,4},{6,7},{7,6},{8,9},{9,8},{10,11... | collective-permute-start | bytes 3047432 | tf_op jit(solution)/shard_map/ppermute | solution.py:497
  42.7 16.3 %collective-permute-start.7 = (bf16[128,3968]{1,0:T(8,128)(2,1)}, bf16[128,3968]{1,0:T(8,128)(2,1)}, u32[]{:S(2)}, u32[]{:S(2)}) collective-permute-start(bf16[128,3968]{1,0:T(8,128)(2,1)} %collective-permute-done.1.refs_1_), channel_id=1, source_target_pairs={{0,1},{1,0},{2,3},{3,2},{4,5},{5,4},{6,7},{7,6},{8,9},{9,8},{10,11... | collective-permute-start | bytes 3047432 | tf_op jit(solution)/shard_map/ppermute | solution.py:497
  43.2 21.3 %collective-permute-start.13 = (bf16[128,3968]{1,0:T(8,128)(2,1)}, bf16[128,3968]{1,0:T(8,128)(2,1)}, u32[]{:S(2)}, u32[]{:S(2)}) collective-permute-start(bf16[128,3968]{1,0:T(8,128)(2,1)} %copy-done.14), channel_id=1, source_target_pairs={{0,16},{1,3},{2,18},{3,1},{4,20},{5,7},{6,22},{7,5},{8,24},{9,11},... | collective-permute-start | bytes 3047432 | tf_op jit(solution)/shard_map/ppermute | solution.py:497
  45.1 19.5 %collective-permute-start.14 = (bf16[1472,256]{1,0:T(8,128)(2,1)S(1)}, bf16[1472,256]{1,0:T(8,128)(2,1)}, u32[]{:S(2)}, u32[]{:S(2)}) collective-permute-start(bf16[1472,256]{1,0:T(8,128)(2,1)S(1)} %collective-permute-done.3.refs_13_.refs_7_), channel_id=1, source_target_pairs={{0,4},{1,5},{2,6},{3,7},{4,12},{5,13},{6,14},{7,15},{8,0},{9,1},{1... | collective-permute-start | bytes 2261000 | tf_op jit(solution)/shard_map/ppermute | solution.py:497
  47.5 4.6 %collective-permute-start.8 = (bf16[16,128]{1,0:T(8,128)(2,1)S(1)}, bf16[16,128]{1,0:T(8,128)(2,1)S(1)}, u32[]{:S(2)}, u32[]{:S(2)}) collective-permute-start(bf16[16,128]{1,0:T(8,128)(2,1)S(1)} %slice.136), channel_id=1, source_target_pairs={{0,18},{1,19},{2,16},{3,17},{4,22},{5,23},{6,20},{7,21},{8,26},{9,... | collective-permute-start | bytes 12296 | tf_op jit(solution)/shard_map/ppermute | solution.py:497
  52.1 16.1 %collective-permute-start.16 = (bf16[128,2048]{1,0:T(8,128)(2,1)}, bf16[128,2048]{1,0:T(8,128)(2,1)}, u32[]{:S(2)}, u32[]{:S(2)}) collective-permute-start(bf16[128,2048]{1,0:T(8,128)(2,1)} %hid.1), channel_id=1, source_target_pairs={{0,1},{1,0},{2,3},{3,2},{4,5},{5,4},{6,7},{7,6},{8,9},{9,8},{10,11... | collective-permute-start | bytes 1572872 | tf_op jit(solution)/shard_map/ppermute | solution.py:497
  64.6 4.7 %collective-permute-start.15 = (bf16[128,3968]{1,0:T(8,128)(2,1)}, bf16[128,3968]{1,0:T(8,128)(2,1)S(1)}, u32[]{:S(2)}, u32[]{:S(2)}) collective-permute-start(bf16[128,3968]{1,0:T(8,128)(2,1)} %collective-permute-done.13.refs_3_), channel_id=1, source_target_pairs={{0,1},{1,0},{2,3},{3,2},{4,5},{5,4},{6,7},{7,6},{8,9},{9,8},{10,11... | collective-permute-start | bytes 3047432 | tf_op jit(solution)/shard_map/ppermute | solution.py:497
  64.6 16.0 %collective-permute-start.11 = (bf16[128,2048]{1,0:T(8,128)(2,1)S(1)}, bf16[128,2048]{1,0:T(8,128)(2,1)S(1)}, u32[]{:S(2)}, u32[]{:S(2)}) collective-permute-start(bf16[128,2048]{1,0:T(8,128)(2,1)S(1)} %copy-done.3), channel_id=1, source_target_pairs={{0,16},{1,3},{2,18},{3,1},{4,20},{5,7},{6,22},{7,5},{8,24},{9,11},... | collective-permute-start | bytes 1572872 | tf_op jit(solution)/shard_map/ppermute | solution.py:497
  66.1 14.6 %collective-permute-start.12 = (bf16[128,2048]{1,0:T(8,128)(2,1)S(1)}, bf16[128,2048]{1,0:T(8,128)(2,1)S(1)}, u32[]{:S(2)}, u32[]{:S(2)}) collective-permute-start(bf16[128,2048]{1,0:T(8,128)(2,1)S(1)} %collective-permute-done.2.refs_2_), channel_id=1, source_target_pairs={{0,16},{1,3},{2,18},{3,1},{4,20},{5,7},{6,22},{7,5},{8,24},{9,11},... | collective-permute-start | bytes 1572872 | tf_op jit(solution)/shard_map/ppermute | solution.py:497
  66.6 14.1 %collective-permute-start.10 = (bf16[1024,256]{1,0:T(8,128)(2,1)S(1)}, bf16[1024,256]{1,0:T(8,128)(2,1)S(1)}, u32[]{:S(2)}, u32[]{:S(2)}) collective-permute-start(bf16[1024,256]{1,0:T(8,128)(2,1)S(1)} %copy-done.7), channel_id=1, source_target_pairs={{0,8},{1,9},{2,10},{3,11},{4,0},{5,1},{6,2},{7,3},{8,12},{9,13},{1... | collective-permute-start | bytes 1572872 | tf_op jit(solution)/shard_map/ppermute | solution.py:497
  68.2 25.4 %collective-permute-start.9 = (bf16[1024,256]{1,0:T(8,128)(2,1)S(1)}, bf16[1024,256]{1,0:T(8,128)(2,1)}, u32[]{:S(2)}, u32[]{:S(2)}) collective-permute-start(bf16[1024,256]{1,0:T(8,128)(2,1)S(1)} %copy-done.7), channel_id=1, source_target_pairs={{0,4},{1,5},{2,6},{3,7},{4,12},{5,13},{6,14},{7,15},{8,0},{9,1},{1... | collective-permute-start | bytes 1572872 | tf_op jit(solution)/shard_map/ppermute | solution.py:497
  69.2 28.4 %collective-permute-start.20 = (bf16[128,2048]{1,0:T(8,128)(2,1)S(1)}, bf16[128,2048]{1,0:T(8,128)(2,1)S(1)}, u32[]{:S(2)}, u32[]{:S(2)}) collective-permute-start(bf16[128,2048]{1,0:T(8,128)(2,1)S(1)} %copy-done.3), channel_id=1, source_target_pairs={{0,1},{1,0},{2,3},{3,2},{4,5},{5,4},{6,7},{7,6},{8,9},{9,8},{10,11... | collective-permute-start | bytes 1572872 | tf_op jit(solution)/shard_map/ppermute | solution.py:497
  80.6 16.9 %collective-permute-start.5 = (bf16[128,2048]{1,0:T(8,128)(2,1)S(1)}, bf16[128,2048]{1,0:T(8,128)(2,1)S(1)}, u32[]{:S(2)}, u32[]{:S(2)}) collective-permute-start(bf16[128,2048]{1,0:T(8,128)(2,1)S(1)} %collective-permute-done.2.refs_2_), channel_id=1, source_target_pairs={{0,1},{1,0},{2,3},{3,2},{4,5},{5,4},{6,7},{7,6},{8,9},{9,8},{10,11... | collective-permute-start | bytes 1572872 | tf_op jit(solution)/shard_map/ppermute | solution.py:497
  93.6 4.0 %collective-permute-start.17 = (bf16[128,2048]{1,0:T(8,128)(2,1)S(1)}, bf16[128,2048]{1,0:T(8,128)(2,1)S(1)}, u32[]{:S(2)}, u32[]{:S(2)}) collective-permute-start(bf16[128,2048]{1,0:T(8,128)(2,1)S(1)} %collective-permute-done.11.refs_1_), channel_id=1, source_target_pairs={{0,1},{1,0},{2,3},{3,2},{4,5},{5,4},{6,7},{7,6},{8,9},{9,8},{10,11... | collective-permute-start | bytes 1572872 | tf_op jit(solution)/shard_map/ppermute | solution.py:497
  93.6 4.0 %collective-permute-start.18 = (bf16[128,2048]{1,0:T(8,128)(2,1)S(1)}, bf16[128,2048]{1,0:T(8,128)(2,1)S(1)}, u32[]{:S(2)}, u32[]{:S(2)}) collective-permute-start(bf16[128,2048]{1,0:T(8,128)(2,1)S(1)} %collective-permute-done.12.refs_3_), channel_id=1, source_target_pairs={{0,1},{1,0},{2,3},{3,2},{4,5},{5,4},{6,7},{7,6},{8,9},{9,8},{10,11... | collective-permute-start | bytes 1572872 | tf_op jit(solution)/shard_map/ppermute | solution.py:497
  94.1 15.1 %collective-permute-start.21 = (bf16[1024,256]{1,0:T(8,128)(2,1)}, bf16[1024,256]{1,0:T(8,128)(2,1)}, u32[]{:S(2)}, u32[]{:S(2)}) collective-permute-start(bf16[1024,256]{1,0:T(8,128)(2,1)} %collective-permute-done.9.refs_2_.refs_9_), channel_id=1, source_target_pairs={{0,4},{1,5},{2,6},{3,7},{4,12},{5,13},{6,14},{7,15},{8,0},{9,1},{1... | collective-permute-start | bytes 1572872 | tf_op jit(solution)/shard_map/ppermute | solution.py:497
  97.5 3.5 %collective-permute-start.19 = (bf16[512,1536]{1,0:T(8,128)(2,1)S(1)}, bf16[512,1536]{1,0:T(8,128)(2,1)S(1)}, u32[]{:S(2)}, u32[]{:S(2)}) collective-permute-start(bf16[512,1536]{1,0:T(8,128)(2,1)S(1)} %get-tuple-element.82), channel_id=1, source_target_pairs={{0,1},{1,0},{2,3},{3,2},{4,5},{5,4},{6,7},{7,6},{8,9},{9,8},{10,11... | collective-permute-start | bytes 4718600 | tf_op jit(solution)/shard_map/ppermute | solution.py:497
  101.8 14.9 %collective-permute-start.22 = (bf16[2,128,1536]{2,1,0:T(8,128)(2,1)S(1)}, bf16[2,128,1536]{2,1,0:T(8,128)(2,1)S(1)}, u32[]{:S(2)}, u32[]{:S(2)}) collective-permute-start(bf16[2,128,1536]{2,1,0:T(8,128)(2,1)S(1)} %fusion), channel_id=1, source_target_pairs={{0,2},{1,17},{2,0},{3,19},{4,6},{5,21},{6,4},{7,23},{8,10},{9,25},... | collective-permute-start | bytes 2359304 | tf_op jit(solution)/shard_map/ppermute | solution.py:497
  116.8 3.7 %collective-permute-start.23 = (bf16[512,1536]{1,0:T(8,128)(2,1)}, bf16[512,1536]{1,0:T(8,128)(2,1)S(1)}, u32[]{:S(2)}, u32[]{:S(2)}) collective-permute-start(bf16[512,1536]{1,0:T(8,128)(2,1)} %get-tuple-element.96), channel_id=1, source_target_pairs={{0,1},{1,0},{2,3},{3,2},{4,5},{5,4},{6,7},{7,6},{8,9},{9,8},{10,11... | collective-permute-start | bytes 4718600 | tf_op jit(solution)/shard_map/ppermute | solution.py:497
  116.8 6.7 %collective-permute-start.25 = (bf16[512,1024]{1,0:T(8,128)(2,1)}, bf16[512,1024]{1,0:T(8,128)(2,1)S(1)}, u32[]{:S(2)}, u32[]{:S(2)}) collective-permute-start(bf16[512,1024]{1,0:T(8,128)(2,1)} %get-tuple-element.99), channel_id=1, source_target_pairs={{0,1},{1,0},{2,3},{3,2},{4,5},{5,4},{6,7},{7,6},{8,9},{9,8},{10,11... | collective-permute-start | bytes 3145736 | tf_op jit(solution)/shard_map/ppermute | solution.py:497
  122.9 16.4 %collective-permute-start.27 = (bf16[2,128,1536]{2,1,0:T(8,128)(2,1)S(1)}, bf16[2,128,1536]{2,1,0:T(8,128)(2,1)}, u32[]{:S(2)}, u32[]{:S(2)}) collective-permute-start(bf16[2,128,1536]{2,1,0:T(8,128)(2,1)S(1)} %bitcast.67), channel_id=1, source_target_pairs={{0,2},{1,17},{2,0},{3,19},{4,6},{5,21},{6,4},{7,23},{8,10},{9,25},... | collective-permute-start | bytes 2359304 | tf_op jit(solution)/shard_map/ppermute | solution.py:497
  125.0 23.7 %collective-permute-start.26 = (bf16[2,128,1024]{2,1,0:T(8,128)(2,1)S(1)}, bf16[2,128,1024]{2,1,0:T(8,128)(2,1)S(1)}, u32[]{:S(2)}, u32[]{:S(2)}) collective-permute-start(bf16[2,128,1024]{2,1,0:T(8,128)(2,1)S(1)} %bitcast.68), channel_id=1, source_target_pairs={{0,2},{1,17},{2,0},{3,19},{4,6},{5,21},{6,4},{7,23},{8,10},{9,25},... | collective-permute-start | bytes 1572872 | tf_op jit(solution)/shard_map/ppermute | solution.py:497
  127.9 22.8 %collective-permute-start.24 = (bf16[128,1536]{1,0:T(8,128)(2,1)S(1)}, bf16[128,1536]{1,0:T(8,128)(2,1)S(1)}, u32[]{:S(2)}, u32[]{:S(2)}) collective-permute-start(bf16[128,1536]{1,0:T(8,128)(2,1)S(1)} %fusion.4), channel_id=1, source_target_pairs={{0,16},{1,3},{2,18},{3,1},{4,20},{5,7},{6,22},{7,5},{8,24},{9,11},... | collective-permute-start | bytes 1179656 | tf_op jit(solution)/shard_map/ppermute | solution.py:497
  140.5 11.5 %collective-permute-start.28 = (bf16[128,1536]{1,0:T(8,128)(2,1)S(1)}, bf16[128,1536]{1,0:T(8,128)(2,1)S(1)}, u32[]{:S(2)}, u32[]{:S(2)}) collective-permute-start(bf16[128,1536]{1,0:T(8,128)(2,1)S(1)} %fusion.3), channel_id=1, source_target_pairs={{0,16},{1,3},{2,18},{3,1},{4,20},{5,7},{6,22},{7,5},{8,24},{9,11},... | collective-permute-start | bytes 1179656 | tf_op jit(solution)/shard_map/ppermute | solution.py:497
  149.0 6.4 %collective-permute-start.30 = (bf16[128,1024]{1,0:T(8,128)(2,1)S(1)}, bf16[128,1024]{1,0:T(8,128)(2,1)S(1)}, u32[]{:S(2)}, u32[]{:S(2)}) collective-permute-start(bf16[128,1024]{1,0:T(8,128)(2,1)S(1)} %get-tuple-element.109), channel_id=1, source_target_pairs={{0,16},{1,3},{2,18},{3,1},{4,20},{5,7},{6,22},{7,5},{8,24},{9,11},... | collective-permute-start | bytes 786440 | tf_op jit(solution)/shard_map/ppermute | solution.py:497
  155.5 1.5 collective-permute-start.29
  (20 other events, 137.9 us)

commit v4 on v3

--- a/solution.py
+++ b/solution.py
@@ -111,7 +111,7 @@
     )(after(*ready))
 
 
-def slices_kernel(place, q, k, v, o, early, late):
+def slices_kernel(place, q, k, v, o, early, late, both):
     depth, width = q.shape
     rank = k.shape[0]
     early[:rank] = k[...]
@@ -119,6 +119,8 @@
     early[2 * rank :] = q[...]
     for c in range(depth // width):
         late[c * width : (c + 1) * width] = o[:, c * width : (c + 1) * width]
+    both[: 2 * rank + depth] = early[...]
+    both[2 * rank + depth :] = late[...]
 
 
 def projection_slices(chip, qw, kw, vw, ow):
@@ -129,7 +131,7 @@
         "projection_slices",
         (chip.reshape(1),),
         (qw, kw, vw, ow),
-        (shape_of((2 * rank + depth, width)), shape_of((depth, width))),
+        tuple(shape_of((n, width)) for n in (2 * rank + depth, depth, 2 * rank + 2 * depth)),
         [
             pl.BlockSpec((depth, width), column),
             pl.BlockSpec((rank, width), column),
@@ -139,7 +141,7 @@
     )
 
 
-def prepare_kernel(core, owners, ids, hid, db, gain, _, near, far):
+def prepare_kernel(core, owners, ids, hid, grad, db, gain, _, near, far):
     rows, half = hid.shape
     blocks, e = db.shape[0] // 2, db.shape[2]
     per = rows // BLOCK
@@ -148,24 +150,25 @@
         for part in range(blocks // per):
             states = db[pl.ds(which * blocks + part * per, per)].reshape(rows, e)
             ref[:, start + part * e : start + (part + 1) * e] = encode_rows(states, gain[...])
-    lane = lax.broadcasted_iota(jnp.int32, (rows, near.shape[1] - half - blocks // per * e), 1)
+    near[:, near.shape[1] - half :] = grad[...]
+    lane = lax.broadcasted_iota(jnp.int32, (rows, 128), 1)
     row = jnp.zeros(lane.shape, jnp.int32)
     for u in range(UNITS):
         at = divmod(u, UPC)
         row = jnp.where(lane == u, owners[at] * 2 * blocks + ids[at], row)
-    near[:, near.shape[1] - lane.shape[1] :] = row.astype(F32).astype(BF16)
-
-
-def prepare(core, owners, ids, hidden, db, gain, earlier):
+    near[:, near.shape[1] - half - 128 : near.shape[1] - half] = row.astype(F32).astype(BF16)
+
+
+def prepare(core, owners, ids, hidden, grad, db, gain, earlier):
     rows, half = hidden.shape
     wide = db.shape[0] // 2 * BLOCK // rows * db.shape[2]
     return kernel_call(
         prepare_kernel,
         "prepare",
         (core.reshape(1), owners, ids),
-        (hidden, db, gain, earlier),
-        (shape_of((rows, half + wide + 128)), shape_of((rows, wide))),
-        [None] * 3 + [pl.BlockSpec(memory_space=pl.ANY)],
+        (hidden, grad, db, gain, earlier),
+        (shape_of((rows, half + wide + 128 + half)), shape_of((rows, wide))),
+        [None] * 4 + [pl.BlockSpec(memory_space=pl.ANY)],
     )
 
 
@@ -198,8 +201,10 @@
 
 def stage_output(copies, name, part, target):
     width = part.shape[1]
-    for c in range(part.shape[0] // width):
-        copies.start(name, rows_of(part, c * width, width), target.at[:, pl.ds(c * width, width)])
+    count = target.shape[1] // width
+    first = part.shape[0] - count * width
+    for c in range(count):
+        copies.start(name, rows_of(part, first + c * width, width), target.at[:, pl.ds(c * width, width)])
 
 
 def project(core, mix, weights, theirs, mine, columns):
@@ -226,7 +231,7 @@
             target = kvw.at[pl.ds(place, rank), pl.ds(c * width, width)]
             copies.start("kvw", rows_of(part, c * rank, rank), target)
     for b, bank in enumerate(banks):
-        start = 0 if b == 4 else bank.shape[1] - 128 - wide
+        start = 0 if b == 4 else half
         copies.start(b // 4, bank.at[:, pl.ds(start, wide)], rows_of(states, b * rows, rows))
     for r, part in enumerate(parts):
         place = pl.multiple_of(pos[r] * depth, depth)
@@ -334,7 +339,8 @@
         for slot, a in enumerate(arrays):
             for c in range(2):
                 target = grads.at[2 * side + c, pl.ds(slot * rows, rows)]
-                copies.start("grads", a.at[:, pl.ds(c * depth, depth)], target)
+                start = a.shape[1] - 2 * depth + c * depth
+                copies.start("grads", a.at[:, pl.ds(start, depth)], target)
     copies.wait("grads")
     copies.start("out", grads.at[pos[3]], rest_out)
     copies.wait(0, 1, 2)
@@ -371,7 +377,7 @@
     copies.start("mix", mix_in, mix)
     for r, piece in enumerate(parts):
         place = pl.multiple_of(pos[r] * depth, depth)
-        copies.start("query", rows_of(piece, piece.shape[0] - depth, depth), rows_of(wq, place, depth))
+        copies.start("query", rows_of(piece, parts[0].shape[0] - depth, depth), rows_of(wq, place, depth))
     copies.wait("in")
     gm[...] = (gmf[...] + dot_t(rest[...], wo[...])).astype(BF16)
     copies.wait("kv")
@@ -521,30 +527,36 @@
     nxt = lax.rem(2 * z + 1 - z // 2, 4)
     sources = (z, 3 - nxt, nxt, 3 - z)
     def codes_of(array):
-        return array[0, array.shape[1] - 128 :][:UNITS].astype(jnp.int32)
-
-    early, late = projection_slices(y * 2 + x, query_weight, key_weight, value_weight, out_weight)
-    early_up, early_down = move(early, UP), move(early, DOWN)
-    he, e_far = prepare(m, owners, block_ids, hidden, database, enc_gain, early)
+        start = array.shape[1] - half - 128 if array.shape[1] > 128 else 0
+        return array[0, start : start + UNITS].astype(jnp.int32)
+
+    early, late, both = projection_slices(y * 2 + x, query_weight, key_weight, value_weight, out_weight)
+    early_up, early_down = move(early, UP), move(both, DOWN)
+    he, e_far = prepare(m, owners, block_ids, hidden, grad_out, database, enc_gain, early)
     he_first, he_second = move(he, FIRST), move(he, SECOND)
-    g_first = move(grad_out, FIRST)
     places = [s ^ (2 * m) for s in sources]
     turn, zz = after(m, early_up, early_down), after(z, early_up, early_down)
     nxt = lax.rem(2 * zz + 1 - zz // 2, 4)
     sources = (zz, 3 - nxt, nxt, 3 - zz)
     pos, sources = jnp.stack([s ^ (2 * turn) for s in sources]), jnp.stack(sources)
     codes = codes_of(after(he, pos))
-    he_first, he_second, g_first, codes = phase(he_first, he_second, g_first, codes)
+    he_first, he_second, codes = phase(he_first, he_second, codes)
     h_zero = move(hidden, CORE)
     early_far = move(after(early_up, he_first, he_second), UP)
     he_last = move(he_first, SECOND)
     he_two, he_one = move(he_first, CORE), move(he_second, CORE)
-    codes_last = move(after(he, he_first)[:TILE, he.shape[1] - 128 :], DIAGONAL)
-    g_zero = move(grad_out, CORE)
-    codes = jnp.stack([codes] + [codes_of(a) for a in (he_second, he_first, codes_last)])
+    h_zero, g_zero = move(hidden, CORE), move(grad_out, CORE)
+    codes = jnp.stack([codes] + [codes_of(a) for a in (he_second, he_first)])
+    he_two, he_one, h_zero, g_zero, codes = phase(he_two, he_one, h_zero, g_zero, codes)
+    early_far = after(early_far, he_two)
+    he_last = after(he_last, early_far)
+    he_three = move(he_last, CORE)
+    late_up = move(after(late, early_far), UP)
     he_own = (he, he_second, he_first, he_last)
+    he_other = (h_zero, he_two, he_one, he_three)
 
     per = rows // BLOCK
+    codes = jnp.concatenate((codes, codes_of(he_last)[None]))
     own_of, id_of = codes // (2 * blocks), codes % (2 * blocks)
     slot = jnp.arange(4, dtype=jnp.int32)
     rel_x = own_of ^ x
@@ -554,23 +566,13 @@
     idx = (block // per * 8 + (holder ^ m) * 4 + bank) * per + block % per
     idx = (idx * (BLOCK // TILE)).reshape(-1, UPC).astype(jnp.int32)
 
-    he_two, he_one, idx = phase(he_two, he_one, idx)
-    early_far = after(early_far, he_two)
-    he_last = after(he_last, early_far)
-    he_three = move(he_last, CORE)
-    he_own = (*he_own[:3], he_last)
-    he_other = (h_zero, he_two, he_one, he_three)
-    g_second, g_last = move(grad_out, SECOND), move(g_first, SECOND)
-    late_up, late_down = move(after(late, idx), UP), move(after(late, idx), DOWN)
     earlies = (early, early_up, early_down, early_far)
     kv, mixture, attention = forward(sources, idx, pos, he_own, e_far, he_other, earlies, half, e, depth)
-    late_up, late_down, g_second, g_last, mixture = phase(late_up, late_down, g_second, g_last, mixture)
+    late_up, mixture = phase(late_up, mixture)
 
     late_far = move(late_up, UP)
-    g_two, g_one, g_three = move(g_first, CORE), move(g_second, CORE), move(g_last, CORE)
-    lates = (late, late_up, late_down)
+    lates = (late, late_up, early_down)
     o_theirs, o_mine = output_slices(m, mixture, lates)
-    g_two, g_one, g_three, o_mine = phase(g_two, g_one, g_three, o_mine)
 
     def slots(array):
         return array.reshape(-1, rows, array.shape[1])
@@ -585,8 +587,8 @@
         return sum(a.astype(F32) for a in (mine[0], theirs[0], first[0], second))
 
     o_theirs, o_mine = slots(move(o_theirs, CORE)), slots(o_mine)
-    g_other = (g_zero, g_two, g_one, g_three)
-    gm, rest = cotangent(pos, (grad_out, g_second, g_first, g_last), g_other, lates)
+    g_other = (after(g_zero, o_mine), *he_other[1:])
+    gm, rest = cotangent(pos, he_own, g_other, lates)
     o_theirs = after(o_theirs, gm)
     o_send = begin(o_mine[2:], o_theirs)
     o_first = move(o_send, FIRST)

time: 159 us -> 158 us (level)
  starting transfers between devices: 32 us -> 17.2 us
  waiting for transfers between devices: 75.3 us -> 87.6 us
  Pallas kernels: 31 us -> 33 us
    ppermute x31 -> x23, starting transfers between devices: 32 us -> 17.2 us  [move(): return lax.ppermute(array, AXES, pairs)]
    ppermute x31 -> x23, waiting for transfers between devices: 75.3 us -> 87.6 us  [move(): return lax.ppermute(array, AXES, pairs)]
    unnamed x42 -> x54, local copies, waits for them, and re-layouts: 6.94 us -> 6.75 us
  transfers between devices with their start and end apart: 31 -> 23, of which waited for: 12 -> 11; matrix products, arithmetic and copies ran while one was open for 7% -> 7% of each run, Pallas kernels for 18% -> 19%
where the time goes in v4:
time: 158 us
  waiting for transfers between devices  87.6 us (55%)
  Pallas kernels  33 us (21%)
  starting transfers between devices  17.2 us (11%)
  other arithmetic  11.1 us (7%)
  local copies, waits for them, and re-layouts  7.54 us (5%)
    ppermute x23, waiting for transfers between devices, move(): return lax.ppermute(array, AXES, pairs)  87.6 us
    pallas_call x6, Pallas kernels, copy_call(): pl.pallas_call(body, in_specs=[smem] * len(scalars) + [pl.BlockSpec(memor...  26.1 us
    ppermute x23, starting transfers between devices, move(): return lax.ppermute(array, AXES, pairs)  17.2 us
    pallas_call x2, Pallas kernels, kernel_call(): pl.pallas_call(body, grid_spec=pltpu.PrefetchScalarGridSpec(num_scalar_pr...  6.9 us
    unnamed x54, local copies, waits for them, and re-layouts  6.75 us
  transfers between devices with their start and end apart: 23, of which 11 were waited for; matrix products, arithmetic and copies ran while one was open for 7% of the time, Pallas kernels for 19%

profile of v4, /device:TPU:0, one launch (start us, length us, event | category | flops | bytes accessed | tf_op | source)
XLA Modules:
  0.0 157.5 jit_solution(13131991636108521715)
XLA Ops:
  0.6 2.9 %projection_slices.1 = (bf16[1472,256]{1,0:T(8,128)(2,1)}, bf16[1024,256]{1,0:T(8,128)(2,1)}, bf16[2496,256]{1,0:T(8,128)(2,1)}) custom-call(s32[1]{0:T(128)} %bitcast.1.place, bf16[1024,1024]{1,0:T(8,128)(2,1)} %q.1, bf16[224,1024]{1,0:T(8,128)(2,1)} %k.1, bf16[224,1024]{1,0:T(8,128)(2,1)} %v.1, bf16[1024,1024]{1,0:T(8,128)(2,1)} %o.1), custom_call_target="tpu_custom_call" | custom-call | flops 99999997952 | bytes 1024 | tf_op jit(solution)/shard_map/projection_slices/pallas_call | solution.py:47
  3.5 4.0 %collective-permute-start.3 = (bf16[2496,256]{1,0:T(8,128)(2,1)}, bf16[2496,256]{1,0:T(8,128)(2,1)S(1)}, u32[]{:S(2)}, u32[]{:S(2)}) collective-permute-start(bf16[2496,256]{1,0:T(8,128)(2,1)} %get-tuple-element.52), channel_id=1, source_target_pairs={{0,8},{1,9},{2,10},{3,11},{4,0},{5,1},{6,2},{7,3},{8,12},{9,13},{1... | collective-permute-start | bytes 3833864 | tf_op jit(solution)/shard_map/ppermute | solution.py:503
  7.5 4.1 %prepare.1 = (bf16[128,6016]{1,0:T(8,128)(2,1)}, bf16[128,1792]{1,0:T(8,128)(2,1)}) custom-call(s32[1]{0:T(128)} %bitcast.core, s32[2,4]{1,0:T(2,128)} %owners.1, s32[2,4]{1,0:T(2,128)} %ids.1, bf16[128,2048]{1,0:T(8,128)(2,1)} %hid.1, bf16[128,2048]{1,0:T(8,128)(2,1)} %grad.1, bf16[8,64,896]{2,1,0:T(8,128)(2,1)} %db.1, f32[896]{0:T(1024)} %gain.1, ...), custom_call_target="tpu_custom_call" | custom-call | flops 99999997952 | bytes 1024 | tf_op jit(solution)/shard_map/prepare/pallas_call | solution.py:47
  11.6 1.5 collective-permute-start.1
  13.1 1.5 collective-permute-start.2
  14.6 38.4 %collective-permute-done.refs_13_.refs_7_ = bf16[1472,256]{1,0:T(8,128)(2,1)S(1)} collective-permute-done((bf16[1472,256]{1,0:T(8,128)(2,1)S(1)}, bf16[1472,256]{1,0:T(8,128)(2,1)S(1)}, u32[]{:S(2)}, u32[]{:S(2)}) %collective-permute-start) | collective-permute-done | bytes 753696 | tf_op jit(solution)/shard_map/ppermute | solution.py:503
  55.0 1.5 collective-permute-start.10
  57.2 2.4 %collective-permute-done.7.refs_8_ = bf16[128,2048]{1,0:T(8,128)(2,1)} collective-permute-done((bf16[128,2048]{1,0:T(8,128)(2,1)}, bf16[128,2048]{1,0:T(8,128)(2,1)}, u32[]{:S(2)}, u32[]{:S(2)}) %collective-permute-start.7) | collective-permute-done | bytes 524320 | tf_op jit(solution)/shard_map/ppermute | solution.py:503
  60.5 1.3 collective-permute-done.8.refs_4_
  62.6 14.4 %collective-permute-done.4.refs_15_.refs_9_ = bf16[1472,256]{1,0:T(8,128)(2,1)} collective-permute-done((bf16[1472,256]{1,0:T(8,128)(2,1)}, bf16[1472,256]{1,0:T(8,128)(2,1)}, u32[]{:S(2)}, u32[]{:S(2)}) %collective-permute-start.4) | collective-permute-done | bytes 753696 | tf_op jit(solution)/shard_map/ppermute | solution.py:503
  79.3 1.4 collective-permute-done.11.refs_7_.refs_11_
  80.7 10.5 %forward.1 = (bf16[2048,512]{1,0:T(8,128)(2,1)}, bf16[512,256]{1,0:T(8,128)(2,1)}, f32[8,2,64,256]{3,2,1,0:T(8,128)}) custom-call(s32[4]{0:T(128)} %pad_add_fusion.3.src, s32[8,4]{1,0:T(8,128)} %fusion.16.idx, s32[4]{0:T(128)} %pad_add_fusion.2.pos, bf16[128,6016]{1,0:T(8,128)(2,1)} %get-tuple-element.55.refs_0_, ...), custom_call_target="tpu_custom_call" | custom-call | flops 1024 | bytes 1024 | tf_op jit(solution)/shard_map/forward/pallas_call | solution.py:81
  91.2 2.2 %collective-permute-done.9.refs_2_.refs_9_ = bf16[1024,256]{1,0:T(8,128)(2,1)} collective-permute-done((bf16[1024,256]{1,0:T(8,128)(2,1)}, bf16[1024,256]{1,0:T(8,128)(2,1)}, u32[]{:S(2)}, u32[]{:S(2)}) %collective-permute-start.9) | collective-permute-done | bytes 524320 | tf_op jit(solution)/shard_map/ppermute | solution.py:503
  93.7 1.1 copy-done.15
  94.8 2.6 %output_slices.1 = (bf16[512,1536]{1,0:T(8,128)(2,1)S(1)}, bf16[512,1536]{1,0:T(8,128)(2,1)S(1)}) custom-call(s32[1]{0:T(128)} %bitcast.core, bf16[512,256]{1,0:T(8,128)(2,1)S(1)} %copy-done.15, bf16[1024,256]{1,0:T(8,128)(2,1)S(1)} %copy-done.12, bf16[1024,256]{1,0:T(8,128)(2,1)} %collective-permute-done.9.refs_2_.refs_9_, bf16[2496,256]{1,0:T(8,128)(2,1)S(1)} %copy-done.8), custom_call_target="tpu_custom_call" | custom-call | flops 99999997952 | bytes 1024 | tf_op jit(solution)/shard_map/output_slices/pallas_call | solution.py:81
  97.5 3.8 %cotangent.1 = (f32[512,256]{1,0:T(8,128)S(1)}, bf16[512,1024]{1,0:T(8,128)(2,1)S(1)}) custom-call(s32[4]{0:T(128)S(1)} %copy-done.11, bf16[128,6016]{1,0:T(8,128)(2,1)S(1)} %copy-done.6, bf16[128,6016]{1,0:T(8,128)(2,1)} %collective-permute-done.2.refs_1_, bf16[128,6016]{1,0:T(8,128)(2,1)} %collective-permute-done.1.refs_2_, ...), custom_call_target="tpu_custom_call" | custom-call | flops 99999997952 | bytes 1024 | tf_op jit(solution)/shard_map/cotangent/pallas_call | solution.py:81
  102.5 1.5 collective-permute-start.14
  104.0 4.4 %collective-permute-done.13.refs_2_ = bf16[1024,256]{1,0:T(8,128)(2,1)} collective-permute-done((bf16[1024,256]{1,0:T(8,128)(2,1)}, bf16[1024,256]{1,0:T(8,128)(2,1)}, u32[]{:S(2)}, u32[]{:S(2)}) %collective-permute-start.13) | collective-permute-done | bytes 524320 | tf_op jit(solution)/shard_map/ppermute | solution.py:503
  108.5 7.5 %late_slices.1 = (bf16[512,1536]{1,0:T(8,128)(2,1)}, bf16[512,1024]{1,0:T(8,128)(2,1)}, bf16[256,1536]{1,0:T(8,128)(2,1)}, bf16[256,1536]{1,0:T(8,128)(2,1)}, bf...) custom-call(s32[1]{0:T(128)} %bitcast.core, s32[8,4]{1,0:T(8,128)} %fusion.16.idx, s32[4]{0:T(128)} %pad_add_fusion.2.pos, ...), custom_call_target="tpu_custom_call" | custom-call | flops 99999997952 | bytes 1024 | tf_op jit(solution)/shard_map/late_slices/pallas_call | solution.py:81
  116.6 3.1 %collective-permute-done.15.refs_1_ = bf16[512,1536]{1,0:T(8,128)(2,1)S(1)} collective-permute-done((bf16[512,1536]{1,0:T(8,128)(2,1)}, bf16[512,1536]{1,0:T(8,128)(2,1)S(1)}, u32[]{:S(2)}, u32[]{:S(2)}) %collective-permute-start.15) | collective-permute-done | bytes 1572896 | tf_op jit(solution)/shard_map/ppermute | solution.py:503
  119.7 1.1 copy-done.9
  120.8 1.4 add_rows.2
  122.2 1.6 collective-permute-start.19
  123.7 1.2 copy-done.10
  125.8 1.3 fusion.4
  127.9 10.6 %collective-permute-done.19 = bf16[2,128,1536]{2,1,0:T(8,128)(2,1)} collective-permute-done((bf16[2,128,1536]{2,1,0:T(8,128)(2,1)S(1)}, bf16[2,128,1536]{2,1,0:T(8,128)(2,1)}, u32[]{:S(2)}, u32[]{:S(2)}) %collective-permute-start.19) | collective-permute-done | bytes 786464 | tf_op jit(solution)/shard_map/ppermute | solution.py:503
  138.6 1.1 fusion.3
  140.6 7.4 %collective-permute-done.18 = bf16[2,128,1024]{2,1,0:T(8,128)(2,1)S(1)} collective-permute-done((bf16[2,128,1024]{2,1,0:T(8,128)(2,1)S(1)}, bf16[2,128,1024]{2,1,0:T(8,128)(2,1)S(1)}, u32[]{:S(2)}, u32[]{:S(2)}) %collective-permute-start.18) | collective-permute-done | bytes 524320 | tf_op jit(solution)/shard_map/ppermute | solution.py:503
  149.1 1.2 fusion.5
  150.5 1.2 fusion.2
  152.9 1.8 %collective-permute-done.22 = bf16[128,1024]{1,0:T(8,128)(2,1)S(1)} collective-permute-done((bf16[128,1024]{1,0:T(8,128)(2,1)S(1)}, bf16[128,1024]{1,0:T(8,128)(2,1)S(1)}, u32[]{:S(2)}, u32[]{:S(2)}) %collective-permute-start.22) | collective-permute-done | bytes 262176 | tf_op jit(solution)/shard_map/ppermute | solution.py:503
  156.6 0.9 fusion.1
  (110 shorter events, 15.5 us)
Async XLA Ops:
  3.5 49.5 %collective-permute-start.3 = (bf16[2496,256]{1,0:T(8,128)(2,1)}, bf16[2496,256]{1,0:T(8,128)(2,1)S(1)}, u32[]{:S(2)}, u32[]{:S(2)}) collective-permute-start(bf16[2496,256]{1,0:T(8,128)(2,1)} %get-tuple-element.52), channel_id=1, source_target_pairs={{0,8},{1,9},{2,10},{3,11},{4,0},{5,1},{6,2},{7,3},{8,12},{9,13},{1... | collective-permute-start | bytes 3833864 | tf_op jit(solution)/shard_map/ppermute | solution.py:503
  7.5 7.1 %copy-start.22 = (bf16[1472,256]{1,0:T(8,128)(2,1)S(1)}, bf16[1472,256]{1,0:T(8,128)(2,1)}, u32[]{:S(2)}) copy-start(bf16[1472,256]{1,0:T(8,128)(2,1)} %get-tuple-element.50._.refs_12_.refs_6_) | copy-start | bytes 2260996
  11.6 42.8 %collective-permute-start.1 = (bf16[128,6016]{1,0:T(8,128)(2,1)}, bf16[128,6016]{1,0:T(8,128)(2,1)}, u32[]{:S(2)}, u32[]{:S(2)}) collective-permute-start(bf16[128,6016]{1,0:T(8,128)(2,1)} %get-tuple-element.55.refs_0_), channel_id=1, source_target_pairs={{0,2},{1,17},{2,0},{3,19},{4,6},{5,21},{6,4},{7,23},{8,10},{9,25},... | collective-permute-start | bytes 4620296 | tf_op jit(solution)/shard_map/ppermute | solution.py:503
  13.1 41.3 %collective-permute-start.2 = (bf16[128,6016]{1,0:T(8,128)(2,1)}, bf16[128,6016]{1,0:T(8,128)(2,1)}, u32[]{:S(2)}, u32[]{:S(2)}) collective-permute-start(bf16[128,6016]{1,0:T(8,128)(2,1)} %get-tuple-element.55.refs_0_), channel_id=1, source_target_pairs={{0,16},{1,3},{2,18},{3,1},{4,20},{5,7},{6,22},{7,5},{8,24},{9,11},... | collective-permute-start | bytes 4620296 | tf_op jit(solution)/shard_map/ppermute | solution.py:503
  14.6 38.4 %collective-permute-start = (bf16[1472,256]{1,0:T(8,128)(2,1)S(1)}, bf16[1472,256]{1,0:T(8,128)(2,1)S(1)}, u32[]{:S(2)}, u32[]{:S(2)}) collective-permute-start(bf16[1472,256]{1,0:T(8,128)(2,1)S(1)} %copy-done.22), channel_id=1, source_target_pairs={{0,4},{1,5},{2,6},{3,7},{4,12},{5,13},{6,14},{7,15},{8,0},{9,1},{1... | collective-permute-start | bytes 2261000 | tf_op jit(solution)/shard_map/ppermute | solution.py:503
  54.4 8.2 %collective-permute-start.5 = (bf16[128,6016]{1,0:T(8,128)(2,1)}, bf16[128,6016]{1,0:T(8,128)(2,1)S(1)}, u32[]{:S(2)}, u32[]{:S(2)}) collective-permute-start(bf16[128,6016]{1,0:T(8,128)(2,1)} %collective-permute-done.1.refs_2_), channel_id=1, source_target_pairs={{0,1},{1,0},{2,3},{3,2},{4,5},{5,4},{6,7},{7,6},{8,9},{9,8},{10,11... | collective-permute-start | bytes 4620296 | tf_op jit(solution)/shard_map/ppermute | solution.py:503
  54.5 8.1 %collective-permute-start.6 = (bf16[128,6016]{1,0:T(8,128)(2,1)}, bf16[128,6016]{1,0:T(8,128)(2,1)S(1)}, u32[]{:S(2)}, u32[]{:S(2)}) collective-permute-start(bf16[128,6016]{1,0:T(8,128)(2,1)} %collective-permute-done.2.refs_1_), channel_id=1, source_target_pairs={{0,1},{1,0},{2,3},{3,2},{4,5},{5,4},{6,7},{7,6},{8,9},{9,8},{10,11... | collective-permute-start | bytes 4620296 | tf_op jit(solution)/shard_map/ppermute | solution.py:503
  55.0 22.0 %collective-permute-start.10 = (bf16[128,6016]{1,0:T(8,128)(2,1)}, bf16[128,6016]{1,0:T(8,128)(2,1)}, u32[]{:S(2)}, u32[]{:S(2)}) collective-permute-start(bf16[128,6016]{1,0:T(8,128)(2,1)} %collective-permute-done.1.refs_2_), channel_id=1, source_target_pairs={{0,16},{1,3},{2,18},{3,1},{4,20},{5,7},{6,22},{7,5},{8,24},{9,11},... | collective-permute-start | bytes 4620296 | tf_op jit(solution)/shard_map/ppermute | solution.py:503
  56.5 3.2 %collective-permute-start.7 = (bf16[128,2048]{1,0:T(8,128)(2,1)}, bf16[128,2048]{1,0:T(8,128)(2,1)}, u32[]{:S(2)}, u32[]{:S(2)}) collective-permute-start(bf16[128,2048]{1,0:T(8,128)(2,1)} %hid.1), channel_id=1, source_target_pairs={{0,1},{1,0},{2,3},{3,2},{4,5},{5,4},{6,7},{7,6},{8,9},{9,8},{10,11... | collective-permute-start | bytes 1572872 | tf_op jit(solution)/shard_map/ppermute | solution.py:503
  56.5 20.5 %collective-permute-start.4 = (bf16[1472,256]{1,0:T(8,128)(2,1)}, bf16[1472,256]{1,0:T(8,128)(2,1)}, u32[]{:S(2)}, u32[]{:S(2)}) collective-permute-start(bf16[1472,256]{1,0:T(8,128)(2,1)} %copy-done.23), channel_id=1, source_target_pairs={{0,4},{1,5},{2,6},{3,7},{4,12},{5,13},{6,14},{7,15},{8,0},{9,1},{1... | collective-permute-start | bytes 2261000 | tf_op jit(solution)/shard_map/ppermute | solution.py:503
  59.7 2.1 %collective-permute-start.8 = (bf16[128,2048]{1,0:T(8,128)(2,1)}, bf16[128,2048]{1,0:T(8,128)(2,1)S(1)}, u32[]{:S(2)}, u32[]{:S(2)}) collective-permute-start(bf16[128,2048]{1,0:T(8,128)(2,1)} %grad.1), channel_id=1, source_target_pairs={{0,1},{1,0},{2,3},{3,2},{4,5},{5,4},{6,7},{7,6},{8,9},{9,8},{10,11... | collective-permute-start | bytes 1572872 | tf_op jit(solution)/shard_map/ppermute | solution.py:503
  62.6 18.1 %copy-start = (bf16[128,6016]{1,0:T(8,128)(2,1)}, bf16[128,6016]{1,0:T(8,128)(2,1)S(1)}, u32[]{:S(2)}) copy-start(bf16[128,6016]{1,0:T(8,128)(2,1)S(1)} %collective-permute-done.5.refs_5_.refs_9_) | copy-start | bytes 4620292
  62.6 18.1 %copy-start.2 = (bf16[128,6016]{1,0:T(8,128)(2,1)}, bf16[128,6016]{1,0:T(8,128)(2,1)S(1)}, u32[]{:S(2)}) copy-start(bf16[128,6016]{1,0:T(8,128)(2,1)S(1)} %collective-permute-done.6.refs_6_.refs_10_) | copy-start | bytes 4620292
  77.0 3.7 %collective-permute-start.11 = (bf16[128,6016]{1,0:T(8,128)(2,1)}, bf16[128,6016]{1,0:T(8,128)(2,1)}, u32[]{:S(2)}, u32[]{:S(2)}) collective-permute-start(bf16[128,6016]{1,0:T(8,128)(2,1)} %collective-permute-done.10.refs_3_), channel_id=1, source_target_pairs={{0,1},{1,0},{2,3},{3,2},{4,5},{5,4},{6,7},{7,6},{8,9},{9,8},{10,11... | collective-permute-start | bytes 4620296 | tf_op jit(solution)/shard_map/ppermute | solution.py:503
  77.9 15.6 %collective-permute-start.9 = (bf16[1024,256]{1,0:T(8,128)(2,1)}, bf16[1024,256]{1,0:T(8,128)(2,1)}, u32[]{:S(2)}, u32[]{:S(2)}) collective-permute-start(bf16[1024,256]{1,0:T(8,128)(2,1)} %get-tuple-element.62.refs_1_.refs_8_), channel_id=1, source_target_pairs={{0,4},{1,5},{2,6},{3,7},{4,12},{5,13},{6,14},{7,15},{8,0},{9,1},{1... | collective-permute-start | bytes 1572872 | tf_op jit(solution)/shard_map/ppermute | solution.py:503
  80.7 13.0 %copy-start.8 = (bf16[2496,256]{1,0:T(8,128)(2,1)S(1)}, bf16[2496,256]{1,0:T(8,128)(2,1)}, u32[]{:S(2)}) copy-start(bf16[2496,256]{1,0:T(8,128)(2,1)} %copy-done.7) | copy-start | bytes 3833860
  80.7 13.0 %copy-start.12 = (bf16[1024,256]{1,0:T(8,128)(2,1)S(1)}, bf16[1024,256]{1,0:T(8,128)(2,1)}, u32[]{:S(2)}) copy-start(bf16[1024,256]{1,0:T(8,128)(2,1)} %get-tuple-element.62.refs_1_.refs_8_) | copy-start | bytes 1572868
  93.4 15.0 %collective-permute-start.13 = (bf16[1024,256]{1,0:T(8,128)(2,1)}, bf16[1024,256]{1,0:T(8,128)(2,1)}, u32[]{:S(2)}, u32[]{:S(2)}) collective-permute-start(bf16[1024,256]{1,0:T(8,128)(2,1)} %collective-permute-done.9.refs_2_.refs_9_), channel_id=1, source_target_pairs={{0,4},{1,5},{2,6},{3,7},{4,12},{5,13},{6,14},{7,15},{8,0},{9,1},{1... | collective-permute-start | bytes 1572872 | tf_op jit(solution)/shard_map/ppermute | solution.py:503
  97.4 4.1 %collective-permute-start.12 = (bf16[512,1536]{1,0:T(8,128)(2,1)S(1)}, bf16[512,1536]{1,0:T(8,128)(2,1)S(1)}, u32[]{:S(2)}, u32[]{:S(2)}) collective-permute-start(bf16[512,1536]{1,0:T(8,128)(2,1)S(1)} %get-tuple-element.72), channel_id=1, source_target_pairs={{0,1},{1,0},{2,3},{3,2},{4,5},{5,4},{6,7},{7,6},{8,9},{9,8},{10,11... | collective-permute-start | bytes 4718600 | tf_op jit(solution)/shard_map/ppermute | solution.py:503
  102.5 13.4 %collective-permute-start.14 = (bf16[2,128,1536]{2,1,0:T(8,128)(2,1)S(1)}, bf16[2,128,1536]{2,1,0:T(8,128)(2,1)S(1)}, u32[]{:S(2)}, u32[]{:S(2)}) collective-permute-start(bf16[2,128,1536]{2,1,0:T(8,128)(2,1)S(1)} %fusion), channel_id=1, source_target_pairs={{0,2},{1,17},{2,0},{3,19},{4,6},{5,21},{6,4},{7,23},{8,10},{9,25},... | collective-permute-start | bytes 2359304 | tf_op jit(solution)/shard_map/ppermute | solution.py:503
  116.0 6.2 %copy-start.20 = (bf16[2,128,1536]{2,1,0:T(8,128)(2,1)}, bf16[2,128,1536]{2,1,0:T(8,128)(2,1)S(1)}, u32[]{:S(2)}) copy-start(bf16[2,128,1536]{2,1,0:T(8,128)(2,1)S(1)} %collective-permute-done.14) | copy-start | bytes 2359300
  116.0 3.7 %collective-permute-start.15 = (bf16[512,1536]{1,0:T(8,128)(2,1)}, bf16[512,1536]{1,0:T(8,128)(2,1)S(1)}, u32[]{:S(2)}, u32[]{:S(2)}) collective-permute-start(bf16[512,1536]{1,0:T(8,128)(2,1)} %get-tuple-element.84), channel_id=1, source_target_pairs={{0,1},{1,0},{2,3},{3,2},{4,5},{5,4},{6,7},{7,6},{8,9},{9,8},{10,11... | collective-permute-start | bytes 4718600 | tf_op jit(solution)/shard_map/ppermute | solution.py:503
  116.1 7.7 %collective-permute-start.17 = (bf16[512,1024]{1,0:T(8,128)(2,1)}, bf16[512,1024]{1,0:T(8,128)(2,1)S(1)}, u32[]{:S(2)}, u32[]{:S(2)}) collective-permute-start(bf16[512,1024]{1,0:T(8,128)(2,1)} %get-tuple-element.87), channel_id=1, source_target_pairs={{0,1},{1,0},{2,3},{3,2},{4,5},{5,4},{6,7},{7,6},{8,9},{9,8},{10,11... | collective-permute-start | bytes 3145736 | tf_op jit(solution)/shard_map/ppermute | solution.py:503
  122.2 16.4 %collective-permute-start.19 = (bf16[2,128,1536]{2,1,0:T(8,128)(2,1)S(1)}, bf16[2,128,1536]{2,1,0:T(8,128)(2,1)}, u32[]{:S(2)}, u32[]{:S(2)}) collective-permute-start(bf16[2,128,1536]{2,1,0:T(8,128)(2,1)S(1)} %bitcast.67), channel_id=1, source_target_pairs={{0,2},{1,17},{2,0},{3,19},{4,6},{5,21},{6,4},{7,23},{8,10},{9,25},... | collective-permute-start | bytes 2359304 | tf_op jit(solution)/shard_map/ppermute | solution.py:503
  124.9 13.7 %copy-start.19 = (bf16[256,1536]{1,0:T(8,128)(2,1)S(1)}, bf16[256,1536]{1,0:T(8,128)(2,1)}, u32[]{:S(2)}) copy-start(bf16[256,1536]{1,0:T(8,128)(2,1)} %get-tuple-element.90) | copy-start | bytes 2359300
  125.2 22.8 %copy-start.26 = (bf16[256,1024]{1,0:T(8,128)(2,1)S(1)}, bf16[256,1024]{1,0:T(8,128)(2,1)}, u32[]{:S(2)}) copy-start(bf16[256,1024]{1,0:T(8,128)(2,1)} %get-tuple-element.86) | copy-start | bytes 1572868
  125.2 22.8 %collective-permute-start.18 = (bf16[2,128,1024]{2,1,0:T(8,128)(2,1)S(1)}, bf16[2,128,1024]{2,1,0:T(8,128)(2,1)S(1)}, u32[]{:S(2)}, u32[]{:S(2)}) collective-permute-start(bf16[2,128,1024]{2,1,0:T(8,128)(2,1)S(1)} %bitcast.68), channel_id=1, source_target_pairs={{0,2},{1,17},{2,0},{3,19},{4,6},{5,21},{6,4},{7,23},{8,10},{9,25},... | collective-permute-start | bytes 1572872 | tf_op jit(solution)/shard_map/ppermute | solution.py:503
  127.1 22.0 %collective-permute-start.16 = (bf16[128,1536]{1,0:T(8,128)(2,1)S(1)}, bf16[128,1536]{1,0:T(8,128)(2,1)S(1)}, u32[]{:S(2)}, u32[]{:S(2)}) collective-permute-start(bf16[128,1536]{1,0:T(8,128)(2,1)S(1)} %fusion.4), channel_id=1, source_target_pairs={{0,16},{1,3},{2,18},{3,1},{4,20},{5,7},{6,22},{7,5},{8,24},{9,11},... | collective-permute-start | bytes 1179656 | tf_op jit(solution)/shard_map/ppermute | solution.py:503
  139.7 9.4 %copy-start.21 = (bf16[2,128,1536]{2,1,0:T(8,128)(2,1)S(1)}, bf16[2,128,1536]{2,1,0:T(8,128)(2,1)}, u32[]{:S(2)}) copy-start(bf16[2,128,1536]{2,1,0:T(8,128)(2,1)} %copy-done.20) | copy-start | bytes 2359300
  139.7 10.8 %collective-permute-start.20 = (bf16[128,1536]{1,0:T(8,128)(2,1)S(1)}, bf16[128,1536]{1,0:T(8,128)(2,1)S(1)}, u32[]{:S(2)}, u32[]{:S(2)}) collective-permute-start(bf16[128,1536]{1,0:T(8,128)(2,1)S(1)} %fusion.3), channel_id=1, source_target_pairs={{0,16},{1,3},{2,18},{3,1},{4,20},{5,7},{6,22},{7,5},{8,24},{9,11},... | collective-permute-start | bytes 1179656 | tf_op jit(solution)/shard_map/ppermute | solution.py:503
  148.3 6.4 %collective-permute-start.22 = (bf16[128,1024]{1,0:T(8,128)(2,1)S(1)}, bf16[128,1024]{1,0:T(8,128)(2,1)S(1)}, u32[]{:S(2)}, u32[]{:S(2)}) collective-permute-start(bf16[128,1024]{1,0:T(8,128)(2,1)S(1)} %get-tuple-element.97), channel_id=1, source_target_pairs={{0,16},{1,3},{2,18},{3,1},{4,20},{5,7},{6,22},{7,5},{8,24},{9,11},... | collective-permute-start | bytes 786440 | tf_op jit(solution)/shard_map/ppermute | solution.py:503
  151.8 3.7 %collective-permute-start.21 = (bf16[2,128,512]{2,1,0:T(8,128)(2,1)S(1)}, bf16[2,128,512]{2,1,0:T(8,128)(2,1)S(1)}, u32[]{:S(2)}, u32[]{:S(2)}) collective-permute-start(bf16[2,128,512]{2,1,0:T(8,128)(2,1)S(1)} %slice.210), channel_id=1, source_target_pairs={{0,1},{1,0},{2,3},{3,2},{4,5},{5,4},{6,7},{7,6},{8,9},{9,8},{10,11... | collective-permute-start | bytes 786440 | tf_op jit(solution)/shard_map/ppermute | solution.py:503
  (18 other events, 40.2 us)

commit v5 on v4

--- a/solution.py
+++ b/solution.py
@@ -467,7 +467,6 @@
         (shape_of(shape),),
         (shape_of((len(arrays), *shape)),),
         2 * len(arrays) + 2,
-        SHORT,
         room=46,
         far=(0,),
         inputs=pltpu.HBM,
@@ -596,20 +595,21 @@
     t0, t1, m0, n0, m1, n1 = late_slices(m, idx, pos, gm, rest, late_far, mixture, kv, attention, earlies)
     t0, t1, o_first = phase(t0, t1, o_first)
     t0, t1 = move(t0, CORE), move(t1, CORE)
+    o_next = carry_on(o_mine, o_theirs, o_first)
+    o_second = move(o_next, SECOND)
+    t0 = after(t0, o_next)
     send0 = add_rows(2 * rows, (n0, 0), (t0, 2 * rows))
     send1 = add_rows(2 * rows, (n1, 0), (after(t1, send0), 2 * rows))
     t0, t1, m0, m1, send0, send1 = (slots(a) for a in (t0, t1, m0, m1, send0, send1))
     first0, first1 = move(send0, FIRST), move(send1, FIRST)
-    o_next = carry_on(o_mine, o_theirs, after(o_first, send0))
-    o_second = move(o_next, SECOND)
     first0 = after(first0, o_next)
     next0 = carry_on(m0, t0, first0)
     second0 = move(next0, SECOND)
-    first1 = after(first1, next0)
+    o_sum = finish(o_mine, o_theirs, o_first, after(o_second, next0))
+    first1 = after(first1, next0, o_sum)
     next1 = carry_on(m1, t1, first1)
     second1 = move(next1, SECOND)
     sub = depth // 2
-    o_sum = finish(o_mine, o_theirs, o_first, after(o_second, next1))
     sum0 = finish(m0, t0, first0, after(second0, next1))
 
     pieces = [o_sum[:, i * sub : (i + 1) * sub] for i in range(3)] + [sum0[:, :sub]]
@@ -625,7 +625,7 @@
     edge = sum0.shape[1] - sub
     rest1 = m1[0].astype(F32) + t1[0].astype(F32) + first1[0].astype(F32)
     base = grad_out.astype(F32) + jnp.concatenate((sum0[:, sub:], rest1), axis=1)
-    second1 = after(second1, base, whole)
+    second1 = after(second1, base, output)
     grad_hidden = (base + jnp.pad(second1.astype(F32), ((0, 0), (edge, 0)))).astype(BF16)
     return (output, grad_hidden)
 

time: 158 us -> 151 us (0.956)
  waiting for transfers between devices: 87.6 us -> 82 us
    ppermute x23, waiting for transfers between devices: 87.6 us -> 82 us  [move(): return lax.ppermute(array, AXES, pairs)]
  transfers between devices with their start and end apart: 23 -> 23, of which waited for: 11 -> 12; matrix products, arithmetic and copies ran while one was open for 7% -> 7% of each run, Pallas kernels for 19% -> 20%
where the time goes in v5:
time: 151 us; the launch traced here: 150 us
  waiting for transfers between devices  82 us (54%)
  Pallas kernels  32.9 us (22%)
  starting transfers between devices  17.4 us (12%)
  other arithmetic  10.2 us (7%)
  local copies, waits for them, and re-layouts  6.79 us (4%)
    ppermute x23, waiting for transfers between devices, move(): return lax.ppermute(array, AXES, pairs)  82 us
    pallas_call x6, Pallas kernels, copy_call(): pl.pallas_call(body, in_specs=[smem] * len(scalars) + [pl.BlockSpec(memor...  26 us
    ppermute x23, starting transfers between devices, move(): return lax.ppermute(array, AXES, pairs)  17.4 us
    pallas_call x2, Pallas kernels, kernel_call(): pl.pallas_call(body, grid_spec=pltpu.PrefetchScalarGridSpec(num_scalar_pr...  6.9 us
    unnamed x54, local copies, waits for them, and re-layouts  6 us
  transfers between devices with their start and end apart: 23, of which 12 were waited for; matrix products, arithmetic and copies ran while one was open for 7% of the time, Pallas kernels for 20%

profile of v5, /device:TPU:0, one launch (start us, length us, event | category | flops | bytes accessed | tf_op | source)
XLA Modules:
  0.0 150.3 jit_solution(7070476920976879381)
XLA Ops:
  0.6 2.9 %projection_slices.1 = (bf16[1472,256]{1,0:T(8,128)(2,1)}, bf16[1024,256]{1,0:T(8,128)(2,1)}, bf16[2496,256]{1,0:T(8,128)(2,1)}) custom-call(s32[1]{0:T(128)} %bitcast.1.place, bf16[1024,1024]{1,0:T(8,128)(2,1)} %q.1, bf16[224,1024]{1,0:T(8,128)(2,1)} %k.1, bf16[224,1024]{1,0:T(8,128)(2,1)} %v.1, bf16[1024,1024]{1,0:T(8,128)(2,1)} %o.1), custom_call_target="tpu_custom_call" | custom-call | flops 99999997952 | bytes 1024 | tf_op jit(solution)/shard_map/projection_slices/pallas_call | solution.py:47
  3.5 4.0 %collective-permute-start.3 = (bf16[2496,256]{1,0:T(8,128)(2,1)}, bf16[2496,256]{1,0:T(8,128)(2,1)S(1)}, u32[]{:S(2)}, u32[]{:S(2)}) collective-permute-start(bf16[2496,256]{1,0:T(8,128)(2,1)} %get-tuple-element.52), channel_id=1, source_target_pairs={{0,8},{1,9},{2,10},{3,11},{4,0},{5,1},{6,2},{7,3},{8,12},{9,13},{1... | collective-permute-start | bytes 3833864 | tf_op jit(solution)/shard_map/ppermute | solution.py:502
  7.5 4.1 %prepare.1 = (bf16[128,6016]{1,0:T(8,128)(2,1)}, bf16[128,1792]{1,0:T(8,128)(2,1)}) custom-call(s32[1]{0:T(128)} %bitcast.core, s32[2,4]{1,0:T(2,128)} %owners.1, s32[2,4]{1,0:T(2,128)} %ids.1, bf16[128,2048]{1,0:T(8,128)(2,1)} %hid.1, bf16[128,2048]{1,0:T(8,128)(2,1)} %grad.1, bf16[8,64,896]{2,1,0:T(8,128)(2,1)} %db.1, f32[896]{0:T(1024)} %gain.1, ...), custom_call_target="tpu_custom_call" | custom-call | flops 99999997952 | bytes 1024 | tf_op jit(solution)/shard_map/prepare/pallas_call | solution.py:47
  11.6 1.5 collective-permute-start.1
  13.1 1.5 %collective-permute-start.2 = (bf16[128,6016]{1,0:T(8,128)(2,1)}, bf16[128,6016]{1,0:T(8,128)(2,1)}, u32[]{:S(2)}, u32[]{:S(2)}) collective-permute-start(bf16[128,6016]{1,0:T(8,128)(2,1)} %get-tuple-element.55.refs_0_), channel_id=1, source_target_pairs={{0,16},{1,3},{2,18},{3,1},{4,20},{5,7},{6,22},{7,5},{8,24},{9,11},... | collective-permute-start | bytes 4620296 | tf_op jit(solution)/shard_map/ppermute | solution.py:502
  14.6 38.4 %collective-permute-done.refs_13_.refs_7_ = bf16[1472,256]{1,0:T(8,128)(2,1)S(1)} collective-permute-done((bf16[1472,256]{1,0:T(8,128)(2,1)S(1)}, bf16[1472,256]{1,0:T(8,128)(2,1)S(1)}, u32[]{:S(2)}, u32[]{:S(2)}) %collective-permute-start) | collective-permute-done | bytes 753696 | tf_op jit(solution)/shard_map/ppermute | solution.py:502
  55.0 1.5 %collective-permute-start.10 = (bf16[128,6016]{1,0:T(8,128)(2,1)}, bf16[128,6016]{1,0:T(8,128)(2,1)}, u32[]{:S(2)}, u32[]{:S(2)}) collective-permute-start(bf16[128,6016]{1,0:T(8,128)(2,1)} %collective-permute-done.1.refs_2_), channel_id=1, source_target_pairs={{0,16},{1,3},{2,18},{3,1},{4,20},{5,7},{6,22},{7,5},{8,24},{9,11},... | collective-permute-start | bytes 4620296 | tf_op jit(solution)/shard_map/ppermute | solution.py:502
  57.2 2.4 %collective-permute-done.7.refs_8_ = bf16[128,2048]{1,0:T(8,128)(2,1)} collective-permute-done((bf16[128,2048]{1,0:T(8,128)(2,1)}, bf16[128,2048]{1,0:T(8,128)(2,1)}, u32[]{:S(2)}, u32[]{:S(2)}) %collective-permute-start.7) | collective-permute-done | bytes 524320 | tf_op jit(solution)/shard_map/ppermute | solution.py:502
  60.5 1.3 collective-permute-done.8.refs_4_
  62.6 14.4 %collective-permute-done.4.refs_15_.refs_9_ = bf16[1472,256]{1,0:T(8,128)(2,1)} collective-permute-done((bf16[1472,256]{1,0:T(8,128)(2,1)}, bf16[1472,256]{1,0:T(8,128)(2,1)}, u32[]{:S(2)}, u32[]{:S(2)}) %collective-permute-start.4) | collective-permute-done | bytes 753696 | tf_op jit(solution)/shard_map/ppermute | solution.py:502
  79.3 1.4 collective-permute-done.11.refs_7_.refs_11_
  80.7 10.5 %forward.1 = (bf16[2048,512]{1,0:T(8,128)(2,1)}, bf16[512,256]{1,0:T(8,128)(2,1)}, f32[8,2,64,256]{3,2,1,0:T(8,128)}) custom-call(s32[4]{0:T(128)} %pad_add_fusion.3.src, s32[8,4]{1,0:T(8,128)} %fusion.16.idx, s32[4]{0:T(128)} %pad_add_fusion.2.pos, bf16[128,6016]{1,0:T(8,128)(2,1)} %get-tuple-element.55.refs_0_, ...), custom_call_target="tpu_custom_call" | custom-call | flops 1024 | bytes 1024 | tf_op jit(solution)/shard_map/forward/pallas_call | solution.py:81
  91.2 2.2 %collective-permute-done.9.refs_2_.refs_9_ = bf16[1024,256]{1,0:T(8,128)(2,1)} collective-permute-done((bf16[1024,256]{1,0:T(8,128)(2,1)}, bf16[1024,256]{1,0:T(8,128)(2,1)}, u32[]{:S(2)}, u32[]{:S(2)}) %collective-permute-start.9) | collective-permute-done | bytes 524320 | tf_op jit(solution)/shard_map/ppermute | solution.py:502
  93.7 1.2 copy-done.9
  94.9 1.0 copy-done.13
  95.9 2.5 %output_slices.1 = (bf16[512,1536]{1,0:T(8,128)(2,1)S(1)}, bf16[512,1536]{1,0:T(8,128)(2,1)S(1)}) custom-call(s32[1]{0:T(128)} %bitcast.core, bf16[512,256]{1,0:T(8,128)(2,1)S(1)} %copy-done.13, bf16[1024,256]{1,0:T(8,128)(2,1)S(1)} %copy-done.9, bf16[1024,256]{1,0:T(8,128)(2,1)} %collective-permute-done.9.refs_2_.refs_9_, bf16[2496,256]{1,0:T(8,128)(2,1)S(1)} %copy-done.7), custom_call_target="tpu_custom_call" | custom-call | flops 99999997952 | bytes 1024 | tf_op jit(solution)/shard_map/output_slices/pallas_call | solution.py:81
  98.6 3.8 %cotangent.1 = (f32[512,256]{1,0:T(8,128)S(1)}, bf16[512,1024]{1,0:T(8,128)(2,1)S(1)}) custom-call(s32[4]{0:T(128)S(1)} %copy-done.8, bf16[128,6016]{1,0:T(8,128)(2,1)S(1)} %copy-done.5, bf16[128,6016]{1,0:T(8,128)(2,1)} %collective-permute-done.2.refs_1_, bf16[128,6016]{1,0:T(8,128)(2,1)} %collective-permute-done.1.refs_2_, ...), custom_call_target="tpu_custom_call" | custom-call | flops 99999997952 | bytes 1024 | tf_op jit(solution)/shard_map/cotangent/pallas_call | solution.py:81
  103.6 1.5 collective-permute-start.14
  105.1 3.4 %collective-permute-done.13.refs_2_ = bf16[1024,256]{1,0:T(8,128)(2,1)} collective-permute-done((bf16[1024,256]{1,0:T(8,128)(2,1)}, bf16[1024,256]{1,0:T(8,128)(2,1)}, u32[]{:S(2)}, u32[]{:S(2)}) %collective-permute-start.13) | collective-permute-done | bytes 524320 | tf_op jit(solution)/shard_map/ppermute | solution.py:502
  108.4 7.5 %late_slices.1 = (bf16[512,1536]{1,0:T(8,128)(2,1)}, bf16[512,1024]{1,0:T(8,128)(2,1)}, bf16[256,1536]{1,0:T(8,128)(2,1)}, bf16[256,1536]{1,0:T(8,128)(2,1)}, bf...) custom-call(s32[1]{0:T(128)} %bitcast.core, s32[8,4]{1,0:T(8,128)} %fusion.16.idx, s32[4]{0:T(128)} %pad_add_fusion.2.pos, ...), custom_call_target="tpu_custom_call" | custom-call | flops 99999997952 | bytes 1024 | tf_op jit(solution)/shard_map/late_slices/pallas_call | solution.py:81
  116.0 1.0 copy-done.20
  116.9 2.1 %fusion.4 = bf16[128,1536]{1,0:T(8,128)(2,1)} fusion(bf16[2,128,1536]{2,1,0:T(8,128)(2,1)} %copy-done.20, bf16[4,128,1536]{2,1,0:T(8,128)(2,1)} %bitcast.71, bf16[512,1536]{1,0:T(8,128)(2,1)S(1)} %get-tuple-element.71), kind=kLoop, calls=%fused_computation.11 | loop fusion | flops 1179648 | bytes 1572864 | tf_op jit(solution)/shard_map/convert_element_type | solution.py:583
  119.8 0.9 collective-permute-start.19
  120.8 1.4 add_rows.2
  122.1 1.4 collective-permute-start.17
  124.6 10.4 %collective-permute-done.17 = bf16[2,128,1536]{2,1,0:T(8,128)(2,1)S(1)} collective-permute-done((bf16[2,128,1536]{2,1,0:T(8,128)(2,1)S(1)}, bf16[2,128,1536]{2,1,0:T(8,128)(2,1)S(1)}, u32[]{:S(2)}, u32[]{:S(2)}) %collective-permute-start.17) | collective-permute-done | bytes 786464 | tf_op jit(solution)/shard_map/ppermute | solution.py:502
  136.0 1.4 fusion.5
  137.4 5.3 %collective-permute-done.20 = bf16[2,128,1024]{2,1,0:T(8,128)(2,1)S(1)} collective-permute-done((bf16[2,128,1024]{2,1,0:T(8,128)(2,1)S(1)}, bf16[2,128,1024]{2,1,0:T(8,128)(2,1)S(1)}, u32[]{:S(2)}, u32[]{:S(2)}) %collective-permute-start.20) | collective-permute-done | bytes 524320 | tf_op jit(solution)/shard_map/ppermute | solution.py:502
  144.1 1.2 collective-permute-done.18
  147.7 0.9 fusion.1
  148.6 0.9 collective-permute-done.22
  149.4 0.9 add_convert_fusion
  (110 shorter events, 14.5 us)
Async XLA Ops:
  3.5 49.5 %collective-permute-start.3 = (bf16[2496,256]{1,0:T(8,128)(2,1)}, bf16[2496,256]{1,0:T(8,128)(2,1)S(1)}, u32[]{:S(2)}, u32[]{:S(2)}) collective-permute-start(bf16[2496,256]{1,0:T(8,128)(2,1)} %get-tuple-element.52), channel_id=1, source_target_pairs={{0,8},{1,9},{2,10},{3,11},{4,0},{5,1},{6,2},{7,3},{8,12},{9,13},{1... | collective-permute-start | bytes 3833864 | tf_op jit(solution)/shard_map/ppermute | solution.py:502
  7.5 7.1 %copy-start.22 = (bf16[1472,256]{1,0:T(8,128)(2,1)S(1)}, bf16[1472,256]{1,0:T(8,128)(2,1)}, u32[]{:S(2)}) copy-start(bf16[1472,256]{1,0:T(8,128)(2,1)} %get-tuple-element.50._.refs_12_.refs_6_) | copy-start | bytes 2260996
  11.6 42.8 %collective-permute-start.1 = (bf16[128,6016]{1,0:T(8,128)(2,1)}, bf16[128,6016]{1,0:T(8,128)(2,1)}, u32[]{:S(2)}, u32[]{:S(2)}) collective-permute-start(bf16[128,6016]{1,0:T(8,128)(2,1)} %get-tuple-element.55.refs_0_), channel_id=1, source_target_pairs={{0,2},{1,17},{2,0},{3,19},{4,6},{5,21},{6,4},{7,23},{8,10},{9,25},... | collective-permute-start | bytes 4620296 | tf_op jit(solution)/shard_map/ppermute | solution.py:502
  13.1 41.3 %collective-permute-start.2 = (bf16[128,6016]{1,0:T(8,128)(2,1)}, bf16[128,6016]{1,0:T(8,128)(2,1)}, u32[]{:S(2)}, u32[]{:S(2)}) collective-permute-start(bf16[128,6016]{1,0:T(8,128)(2,1)} %get-tuple-element.55.refs_0_), channel_id=1, source_target_pairs={{0,16},{1,3},{2,18},{3,1},{4,20},{5,7},{6,22},{7,5},{8,24},{9,11},... | collective-permute-start | bytes 4620296 | tf_op jit(solution)/shard_map/ppermute | solution.py:502
  14.6 38.4 %collective-permute-start = (bf16[1472,256]{1,0:T(8,128)(2,1)S(1)}, bf16[1472,256]{1,0:T(8,128)(2,1)S(1)}, u32[]{:S(2)}, u32[]{:S(2)}) collective-permute-start(bf16[1472,256]{1,0:T(8,128)(2,1)S(1)} %copy-done.22), channel_id=1, source_target_pairs={{0,4},{1,5},{2,6},{3,7},{4,12},{5,13},{6,14},{7,15},{8,0},{9,1},{1... | collective-permute-start | bytes 2261000 | tf_op jit(solution)/shard_map/ppermute | solution.py:502
  54.4 8.2 %collective-permute-start.5 = (bf16[128,6016]{1,0:T(8,128)(2,1)}, bf16[128,6016]{1,0:T(8,128)(2,1)S(1)}, u32[]{:S(2)}, u32[]{:S(2)}) collective-permute-start(bf16[128,6016]{1,0:T(8,128)(2,1)} %collective-permute-done.1.refs_2_), channel_id=1, source_target_pairs={{0,1},{1,0},{2,3},{3,2},{4,5},{5,4},{6,7},{7,6},{8,9},{9,8},{10,11... | collective-permute-start | bytes 4620296 | tf_op jit(solution)/shard_map/ppermute | solution.py:502
  54.5 8.1 %collective-permute-start.6 = (bf16[128,6016]{1,0:T(8,128)(2,1)}, bf16[128,6016]{1,0:T(8,128)(2,1)S(1)}, u32[]{:S(2)}, u32[]{:S(2)}) collective-permute-start(bf16[128,6016]{1,0:T(8,128)(2,1)} %collective-permute-done.2.refs_1_), channel_id=1, source_target_pairs={{0,1},{1,0},{2,3},{3,2},{4,5},{5,4},{6,7},{7,6},{8,9},{9,8},{10,11... | collective-permute-start | bytes 4620296 | tf_op jit(solution)/shard_map/ppermute | solution.py:502
  55.0 22.0 %collective-permute-start.10 = (bf16[128,6016]{1,0:T(8,128)(2,1)}, bf16[128,6016]{1,0:T(8,128)(2,1)}, u32[]{:S(2)}, u32[]{:S(2)}) collective-permute-start(bf16[128,6016]{1,0:T(8,128)(2,1)} %collective-permute-done.1.refs_2_), channel_id=1, source_target_pairs={{0,16},{1,3},{2,18},{3,1},{4,20},{5,7},{6,22},{7,5},{8,24},{9,11},... | collective-permute-start | bytes 4620296 | tf_op jit(solution)/shard_map/ppermute | solution.py:502
  56.5 3.2 %collective-permute-start.7 = (bf16[128,2048]{1,0:T(8,128)(2,1)}, bf16[128,2048]{1,0:T(8,128)(2,1)}, u32[]{:S(2)}, u32[]{:S(2)}) collective-permute-start(bf16[128,2048]{1,0:T(8,128)(2,1)} %hid.1), channel_id=1, source_target_pairs={{0,1},{1,0},{2,3},{3,2},{4,5},{5,4},{6,7},{7,6},{8,9},{9,8},{10,11... | collective-permute-start | bytes 1572872 | tf_op jit(solution)/shard_map/ppermute | solution.py:502
  56.5 20.5 %collective-permute-start.4 = (bf16[1472,256]{1,0:T(8,128)(2,1)}, bf16[1472,256]{1,0:T(8,128)(2,1)}, u32[]{:S(2)}, u32[]{:S(2)}) collective-permute-start(bf16[1472,256]{1,0:T(8,128)(2,1)} %copy-done.23), channel_id=1, source_target_pairs={{0,4},{1,5},{2,6},{3,7},{4,12},{5,13},{6,14},{7,15},{8,0},{9,1},{1... | collective-permute-start | bytes 2261000 | tf_op jit(solution)/shard_map/ppermute | solution.py:502
  59.7 2.1 %collective-permute-start.8 = (bf16[128,2048]{1,0:T(8,128)(2,1)}, bf16[128,2048]{1,0:T(8,128)(2,1)S(1)}, u32[]{:S(2)}, u32[]{:S(2)}) collective-permute-start(bf16[128,2048]{1,0:T(8,128)(2,1)} %grad.1), channel_id=1, source_target_pairs={{0,1},{1,0},{2,3},{3,2},{4,5},{5,4},{6,7},{7,6},{8,9},{9,8},{10,11... | collective-permute-start | bytes 1572872 | tf_op jit(solution)/shard_map/ppermute | solution.py:502
  62.6 18.1 %copy-start = (bf16[128,6016]{1,0:T(8,128)(2,1)}, bf16[128,6016]{1,0:T(8,128)(2,1)S(1)}, u32[]{:S(2)}) copy-start(bf16[128,6016]{1,0:T(8,128)(2,1)S(1)} %collective-permute-done.5.refs_5_.refs_9_) | copy-start | bytes 4620292
  62.6 18.1 %copy-start.2 = (bf16[128,6016]{1,0:T(8,128)(2,1)}, bf16[128,6016]{1,0:T(8,128)(2,1)S(1)}, u32[]{:S(2)}) copy-start(bf16[128,6016]{1,0:T(8,128)(2,1)S(1)} %collective-permute-done.6.refs_6_.refs_10_) | copy-start | bytes 4620292
  77.0 3.7 %collective-permute-start.11 = (bf16[128,6016]{1,0:T(8,128)(2,1)}, bf16[128,6016]{1,0:T(8,128)(2,1)}, u32[]{:S(2)}, u32[]{:S(2)}) collective-permute-start(bf16[128,6016]{1,0:T(8,128)(2,1)} %collective-permute-done.10.refs_3_), channel_id=1, source_target_pairs={{0,1},{1,0},{2,3},{3,2},{4,5},{5,4},{6,7},{7,6},{8,9},{9,8},{10,11... | collective-permute-start | bytes 4620296 | tf_op jit(solution)/shard_map/ppermute | solution.py:502
  77.9 15.6 %collective-permute-start.9 = (bf16[1024,256]{1,0:T(8,128)(2,1)}, bf16[1024,256]{1,0:T(8,128)(2,1)}, u32[]{:S(2)}, u32[]{:S(2)}) collective-permute-start(bf16[1024,256]{1,0:T(8,128)(2,1)} %get-tuple-element.62.refs_1_.refs_8_), channel_id=1, source_target_pairs={{0,4},{1,5},{2,6},{3,7},{4,12},{5,13},{6,14},{7,15},{8,0},{9,1},{1... | collective-permute-start | bytes 1572872 | tf_op jit(solution)/shard_map/ppermute | solution.py:502
  80.7 13.0 %copy-start.7 = (bf16[2496,256]{1,0:T(8,128)(2,1)S(1)}, bf16[2496,256]{1,0:T(8,128)(2,1)}, u32[]{:S(2)}) copy-start(bf16[2496,256]{1,0:T(8,128)(2,1)} %copy-done.6) | copy-start | bytes 3833860
  93.4 5.1 %copy-start.8 = (s32[4]{0:T(128)S(1)}, s32[4]{0:T(128)}, u32[]{:S(2)}) copy-start(s32[4]{0:T(128)} %pad_add_fusion.2.pos) | copy-start | bytes 52
  93.4 15.0 %collective-permute-start.13 = (bf16[1024,256]{1,0:T(8,128)(2,1)}, bf16[1024,256]{1,0:T(8,128)(2,1)}, u32[]{:S(2)}, u32[]{:S(2)}) collective-permute-start(bf16[1024,256]{1,0:T(8,128)(2,1)} %collective-permute-done.9.refs_2_.refs_9_), channel_id=1, source_target_pairs={{0,4},{1,5},{2,6},{3,7},{4,12},{5,13},{6,14},{7,15},{8,0},{9,1},{1... | collective-permute-start | bytes 1572872 | tf_op jit(solution)/shard_map/ppermute | solution.py:502
  98.4 18.5 %copy-start.4 = (bf16[512,1536]{1,0:T(8,128)(2,1)}, bf16[512,1536]{1,0:T(8,128)(2,1)S(1)}, u32[]{:S(2)}) copy-start(bf16[512,1536]{1,0:T(8,128)(2,1)S(1)} %get-tuple-element.71) | copy-start | bytes 4718596
  98.4 4.1 %collective-permute-start.12 = (bf16[512,1536]{1,0:T(8,128)(2,1)S(1)}, bf16[512,1536]{1,0:T(8,128)(2,1)S(1)}, u32[]{:S(2)}, u32[]{:S(2)}) collective-permute-start(bf16[512,1536]{1,0:T(8,128)(2,1)S(1)} %get-tuple-element.72), channel_id=1, source_target_pairs={{0,1},{1,0},{2,3},{3,2},{4,5},{5,4},{6,7},{7,6},{8,9},{9,8},{10,11... | collective-permute-start | bytes 4718600 | tf_op jit(solution)/shard_map/ppermute | solution.py:502
  103.6 12.4 %collective-permute-start.14 = (bf16[2,128,1536]{2,1,0:T(8,128)(2,1)S(1)}, bf16[2,128,1536]{2,1,0:T(8,128)(2,1)S(1)}, u32[]{:S(2)}, u32[]{:S(2)}) collective-permute-start(bf16[2,128,1536]{2,1,0:T(8,128)(2,1)S(1)} %fusion), channel_id=1, source_target_pairs={{0,2},{1,17},{2,0},{3,19},{4,6},{5,21},{6,4},{7,23},{8,10},{9,25},... | collective-permute-start | bytes 2359304 | tf_op jit(solution)/shard_map/ppermute | solution.py:502
  116.9 3.8 %collective-permute-start.16 = (bf16[512,1536]{1,0:T(8,128)(2,1)}, bf16[512,1536]{1,0:T(8,128)(2,1)S(1)}, u32[]{:S(2)}, u32[]{:S(2)}) collective-permute-start(bf16[512,1536]{1,0:T(8,128)(2,1)} %get-tuple-element.84), channel_id=1, source_target_pairs={{0,1},{1,0},{2,3},{3,2},{4,5},{5,4},{6,7},{7,6},{8,9},{9,8},{10,11... | collective-permute-start | bytes 4718600 | tf_op jit(solution)/shard_map/ppermute | solution.py:502
  119.0 17.0 %collective-permute-start.15 = (bf16[128,1536]{1,0:T(8,128)(2,1)}, bf16[128,1536]{1,0:T(8,128)(2,1)}, u32[]{:S(2)}, u32[]{:S(2)}) collective-permute-start(bf16[128,1536]{1,0:T(8,128)(2,1)} %fusion.4), channel_id=1, source_target_pairs={{0,16},{1,3},{2,18},{3,1},{4,20},{5,7},{6,22},{7,5},{8,24},{9,11},... | collective-permute-start | bytes 1179656 | tf_op jit(solution)/shard_map/ppermute | solution.py:502
  119.8 3.7 %collective-permute-start.19 = (bf16[512,1024]{1,0:T(8,128)(2,1)}, bf16[512,1024]{1,0:T(8,128)(2,1)S(1)}, u32[]{:S(2)}, u32[]{:S(2)}) collective-permute-start(bf16[512,1024]{1,0:T(8,128)(2,1)} %get-tuple-element.90), channel_id=1, source_target_pairs={{0,1},{1,0},{2,3},{3,2},{4,5},{5,4},{6,7},{7,6},{8,9},{9,8},{10,11... | collective-permute-start | bytes 3145736 | tf_op jit(solution)/shard_map/ppermute | solution.py:502
  122.1 12.9 %collective-permute-start.17 = (bf16[2,128,1536]{2,1,0:T(8,128)(2,1)S(1)}, bf16[2,128,1536]{2,1,0:T(8,128)(2,1)S(1)}, u32[]{:S(2)}, u32[]{:S(2)}) collective-permute-start(bf16[2,128,1536]{2,1,0:T(8,128)(2,1)S(1)} %bitcast.67), channel_id=1, source_target_pairs={{0,2},{1,17},{2,0},{3,19},{4,6},{5,21},{6,4},{7,23},{8,10},{9,25},... | collective-permute-start | bytes 2359304 | tf_op jit(solution)/shard_map/ppermute | solution.py:502
  123.5 11.5 %copy-start.19 = (bf16[256,1536]{1,0:T(8,128)(2,1)S(1)}, bf16[256,1536]{1,0:T(8,128)(2,1)}, u32[]{:S(2)}) copy-start(bf16[256,1536]{1,0:T(8,128)(2,1)} %get-tuple-element.83) | copy-start | bytes 2359300
  123.8 12.2 %copy-start.21 = (bf16[2,128,1536]{2,1,0:T(8,128)(2,1)S(1)}, bf16[2,128,1536]{2,1,0:T(8,128)(2,1)}, u32[]{:S(2)}) copy-start(bf16[2,128,1536]{2,1,0:T(8,128)(2,1)} %copy-done.20) | copy-start | bytes 2359300
  123.8 18.9 %collective-permute-start.20 = (bf16[2,128,1024]{2,1,0:T(8,128)(2,1)S(1)}, bf16[2,128,1024]{2,1,0:T(8,128)(2,1)S(1)}, u32[]{:S(2)}, u32[]{:S(2)}) collective-permute-start(bf16[2,128,1024]{2,1,0:T(8,128)(2,1)S(1)} %bitcast.68), channel_id=1, source_target_pairs={{0,2},{1,17},{2,0},{3,19},{4,6},{5,21},{6,4},{7,23},{8,10},{9,25},... | collective-permute-start | bytes 1572872 | tf_op jit(solution)/shard_map/ppermute | solution.py:502
  135.1 7.6 %copy-start.26 = (bf16[256,1024]{1,0:T(8,128)(2,1)S(1)}, bf16[256,1024]{1,0:T(8,128)(2,1)}, u32[]{:S(2)}) copy-start(bf16[256,1024]{1,0:T(8,128)(2,1)} %get-tuple-element.89) | copy-start | bytes 1572868
  135.1 10.1 %collective-permute-start.18 = (bf16[128,1536]{1,0:T(8,128)(2,1)S(1)}, bf16[128,1536]{1,0:T(8,128)(2,1)S(1)}, u32[]{:S(2)}, u32[]{:S(2)}) collective-permute-start(bf16[128,1536]{1,0:T(8,128)(2,1)S(1)} %fusion.3), channel_id=1, source_target_pairs={{0,16},{1,3},{2,18},{3,1},{4,20},{5,7},{6,22},{7,5},{8,24},{9,11},... | collective-permute-start | bytes 1179656 | tf_op jit(solution)/shard_map/ppermute | solution.py:502
  143.0 6.4 %collective-permute-start.22 = (bf16[128,1024]{1,0:T(8,128)(2,1)S(1)}, bf16[128,1024]{1,0:T(8,128)(2,1)S(1)}, u32[]{:S(2)}, u32[]{:S(2)}) collective-permute-start(bf16[128,1024]{1,0:T(8,128)(2,1)S(1)} %get-tuple-element.97), channel_id=1, source_target_pairs={{0,16},{1,3},{2,18},{3,1},{4,20},{5,7},{6,22},{7,5},{8,24},{9,11},... | collective-permute-start | bytes 786440 | tf_op jit(solution)/shard_map/ppermute | solution.py:502
  145.6 1.6 %collective-permute-start.21 = (bf16[2,128,512]{2,1,0:T(8,128)(2,1)S(1)}, bf16[2,128,512]{2,1,0:T(8,128)(2,1)S(1)}, u32[]{:S(2)}, u32[]{:S(2)}) collective-permute-start(bf16[2,128,512]{2,1,0:T(8,128)(2,1)S(1)} %slice.208), channel_id=1, source_target_pairs={{0,1},{1,0},{2,3},{3,2},{4,5},{5,4},{6,7},{7,6},{8,9},{9,8},{10,11... | collective-permute-start | bytes 786440 | tf_op jit(solution)/shard_map/ppermute | solution.py:502
  (18 other events, 40.7 us)

commit v6 on v5

--- a/solution.py
+++ b/solution.py
@@ -111,16 +111,15 @@
     )(after(*ready))
 
 
-def slices_kernel(place, q, k, v, o, early, late, both):
+def slices_kernel(place, q, k, v, o, out):
     depth, width = q.shape
     rank = k.shape[0]
-    early[:rank] = k[...]
-    early[rank : 2 * rank] = v[...]
-    early[2 * rank :] = q[...]
+    out[:rank] = k[...]
+    out[rank : 2 * rank] = v[...]
+    out[2 * rank : 2 * rank + depth] = q[...]
     for c in range(depth // width):
-        late[c * width : (c + 1) * width] = o[:, c * width : (c + 1) * width]
-    both[: 2 * rank + depth] = early[...]
-    both[2 * rank + depth :] = late[...]
+        at = 2 * rank + depth + c * width
+        out[at : at + width] = o[:, c * width : (c + 1) * width]
 
 
 def projection_slices(chip, qw, kw, vw, ow):
@@ -131,14 +130,14 @@
         "projection_slices",
         (chip.reshape(1),),
         (qw, kw, vw, ow),
-        tuple(shape_of((n, width)) for n in (2 * rank + depth, depth, 2 * rank + 2 * depth)),
+        (shape_of((2 * rank + 2 * depth, width)),),
         [
             pl.BlockSpec((depth, width), column),
             pl.BlockSpec((rank, width), column),
             pl.BlockSpec((rank, width), column),
             pl.BlockSpec((width, depth), lambda i, place: (place[0], 0)),
         ],
-    )
+    )[0]
 
 
 def prepare_kernel(core, owners, ids, hid, grad, db, gain, _, near, far):
@@ -492,7 +491,6 @@
 PREV = {RING[i]: RING[(i + 3) % 4] for i in range(4)}
 FIRST = permutation(lambda y, z, x, m: (y, z, 1 - x, m) if m == 0 else (1 - y, z, x, m))
 SECOND = permutation(lambda y, z, x, m: (1 - y, z, x, m) if m == 0 else (y, z, 1 - x, m))
-DIAGONAL = permutation(lambda y, z, x, m: (1 - y, z, 1 - x, m))
 CORE = permutation(lambda y, z, x, m: (y, z, x, 1 - m))
 UP = permutation(lambda y, z, x, m: (y, NEXT[z], x, m))
 DOWN = permutation(lambda y, z, x, m: (y, PREV[z], x, m))
@@ -525,13 +523,15 @@
     rows, half = hidden.shape
     nxt = lax.rem(2 * z + 1 - z // 2, 4)
     sources = (z, 3 - nxt, nxt, 3 - z)
+
     def codes_of(array):
         start = array.shape[1] - half - 128 if array.shape[1] > 128 else 0
         return array[0, start : start + UNITS].astype(jnp.int32)
 
-    early, late, both = projection_slices(y * 2 + x, query_weight, key_weight, value_weight, out_weight)
+    both = projection_slices(y * 2 + x, query_weight, key_weight, value_weight, out_weight)
+    early, late = both[: 2 * rank + depth], both[2 * rank + depth :]
     early_up, early_down = move(early, UP), move(both, DOWN)
-    he, e_far = prepare(m, owners, block_ids, hidden, grad_out, database, enc_gain, early)
+    he, e_far = prepare(m, owners, block_ids, hidden, grad_out, database, enc_gain, both)
     he_first, he_second = move(he, FIRST), move(he, SECOND)
     places = [s ^ (2 * m) for s in sources]
     turn, zz = after(m, early_up, early_down), after(z, early_up, early_down)
@@ -540,13 +540,14 @@
     pos, sources = jnp.stack([s ^ (2 * turn) for s in sources]), jnp.stack(sources)
     codes = codes_of(after(he, pos))
     he_first, he_second, codes = phase(he_first, he_second, codes)
-    h_zero = move(hidden, CORE)
     early_far = move(after(early_up, he_first, he_second), UP)
     he_last = move(he_first, SECOND)
     he_two, he_one = move(he_first, CORE), move(he_second, CORE)
     h_zero, g_zero = move(hidden, CORE), move(grad_out, CORE)
     codes = jnp.stack([codes] + [codes_of(a) for a in (he_second, he_first)])
-    he_two, he_one, h_zero, g_zero, codes = phase(he_two, he_one, h_zero, g_zero, codes)
+    he_two, he_one, h_zero, g_zero, codes, sources, late = phase(
+        he_two, he_one, h_zero, g_zero, codes, sources, late
+    )
     early_far = after(early_far, he_two)
     he_last = after(he_last, early_far)
     he_three = move(he_last, CORE)

time: 151 us -> 150 us (level)
  waiting for transfers between devices: 82 us -> 79.1 us
  local copies, waits for them, and re-layouts: 6.79 us -> 8.94 us
    ppermute x23, waiting for transfers between devices: 82 us -> 79.1 us  [move(): return lax.ppermute(array, AXES, pairs)]
    slice x0 -> x2, local copies, waits for them, and re-layouts: none -> 1.92 us  [local_plane(): early, late = (both[:2 * rank + depth], both[2 * rank + depth:])]
    unnamed x54 -> x56, local copies, waits for them, and re-layouts: 6 us -> 6.23 us
  transfers between devices with their start and end apart: 23 -> 23, of which waited for: 12 -> 11; matrix products, arithmetic and copies ran while one was open for 7% -> 8% of each run, Pallas kernels for 20% -> 20%
where the time goes in v6:
time: 150 us; the launch traced here: 149 us
  waiting for transfers between devices  79.1 us (53%)
  Pallas kernels  32.5 us (22%)
  starting transfers between devices  17.3 us (12%)
  other arithmetic  10.2 us (7%)
  local copies, waits for them, and re-layouts  8.94 us (6%)
    ppermute x23, waiting for transfers between devices, move(): return lax.ppermute(array, AXES, pairs)  79.1 us
    pallas_call x6, Pallas kernels, copy_call(): pl.pallas_call(body, in_specs=[smem] * len(scalars) + [pl.BlockSpec(memor...  26 us
    ppermute x23, starting transfers between devices, move(): return lax.ppermute(array, AXES, pairs)  17.3 us
    pallas_call x2, Pallas kernels, kernel_call(): pl.pallas_call(body, grid_spec=pltpu.PrefetchScalarGridSpec(num_scalar_pr...  6.53 us
    unnamed x56, local copies, waits for them, and re-layouts  6.23 us
  transfers between devices with their start and end apart: 23, of which 11 were waited for; matrix products, arithmetic and copies ran while one was open for 8% of the time, Pallas kernels for 20%

profile of v6, /device:TPU:0, one launch (start us, length us, event | category | flops | bytes accessed | tf_op | source)
XLA Modules:
  0.0 149.2 jit_solution(13256947354777835066)
XLA Ops:
  0.6 2.5 %projection_slices.1._ = bf16[2496,256]{1,0:T(8,128)(2,1)} custom-call(s32[1]{0:T(128)} %bitcast.1.place, bf16[1024,1024]{1,0:T(8,128)(2,1)} %q.1, bf16[224,1024]{1,0:T(8,128)(2,1)} %k.1, bf16[224,1024]{1,0:T(8,128)(2,1)} %v.1, bf16[1024,1024]{1,0:T(8,128)(2,1)} %o.1), custom_call_target="tpu_custom_call" | custom-call | flops 99999997952 | bytes 1024 | tf_op jit(solution)/shard_map/projection_slices/pallas_call | solution.py:47
  3.1 4.0 %collective-permute-start.3 = (bf16[2496,256]{1,0:T(8,128)(2,1)}, bf16[2496,256]{1,0:T(8,128)(2,1)S(1)}, u32[]{:S(2)}, u32[]{:S(2)}) collective-permute-start(bf16[2496,256]{1,0:T(8,128)(2,1)} %projection_slices.1._), channel_id=1, source_target_pairs={{0,8},{1,9},{2,10},{3,11},{4,0},{5,1},{6,2},{7,3},{8,12},{9,13},{1... | collective-permute-start | bytes 3833864 | tf_op jit(solution)/shard_map/ppermute | solution.py:500
  7.2 4.1 %prepare.1 = (bf16[128,6016]{1,0:T(8,128)(2,1)}, bf16[128,1792]{1,0:T(8,128)(2,1)}) custom-call(s32[1]{0:T(128)} %bitcast.core, s32[2,4]{1,0:T(2,128)} %owners.1, s32[2,4]{1,0:T(2,128)} %ids.1, bf16[128,2048]{1,0:T(8,128)(2,1)} %hid.1, bf16[128,2048]{1,0:T(8,128)(2,1)} %grad.1, bf16[8,64,896]{2,1,0:T(8,128)(2,1)} %db.1, f32[896]{0:T(1024)} %gain.1, ...), custom_call_target="tpu_custom_call" | custom-call | flops 99999997952 | bytes 1024 | tf_op jit(solution)/shard_map/prepare/pallas_call | solution.py:47
  11.2 1.5 collective-permute-start
  12.7 1.5 %collective-permute-start.1 = (bf16[128,6016]{1,0:T(8,128)(2,1)}, bf16[128,6016]{1,0:T(8,128)(2,1)}, u32[]{:S(2)}, u32[]{:S(2)}) collective-permute-start(bf16[128,6016]{1,0:T(8,128)(2,1)} %get-tuple-element.51.refs_0_), channel_id=1, source_target_pairs={{0,16},{1,3},{2,18},{3,1},{4,20},{5,7},{6,22},{7,5},{8,24},{9,11},... | collective-permute-start | bytes 4620296 | tf_op jit(solution)/shard_map/ppermute | solution.py:500
  14.4 38.3 %collective-permute-done.2.refs_13_.refs_7_ = bf16[1472,256]{1,0:T(8,128)(2,1)S(1)} collective-permute-done((bf16[1472,256]{1,0:T(8,128)(2,1)S(1)}, bf16[1472,256]{1,0:T(8,128)(2,1)S(1)}, u32[]{:S(2)}, u32[]{:S(2)}) %collective-permute-start.2) | collective-permute-done | bytes 753696 | tf_op jit(solution)/shard_map/ppermute | solution.py:500
  54.6 1.5 %collective-permute-start.10 = (bf16[128,6016]{1,0:T(8,128)(2,1)}, bf16[128,6016]{1,0:T(8,128)(2,1)}, u32[]{:S(2)}, u32[]{:S(2)}) collective-permute-start(bf16[128,6016]{1,0:T(8,128)(2,1)} %collective-permute-done.refs_2_), channel_id=1, source_target_pairs={{0,16},{1,3},{2,18},{3,1},{4,20},{5,7},{6,22},{7,5},{8,24},{9,11},... | collective-permute-start | bytes 4620296 | tf_op jit(solution)/shard_map/ppermute | solution.py:500
  56.9 2.4 %collective-permute-done.6.refs_8_ = bf16[128,2048]{1,0:T(8,128)(2,1)} collective-permute-done((bf16[128,2048]{1,0:T(8,128)(2,1)}, bf16[128,2048]{1,0:T(8,128)(2,1)}, u32[]{:S(2)}, u32[]{:S(2)}) %collective-permute-start.6) | collective-permute-done | bytes 524320 | tf_op jit(solution)/shard_map/ppermute | solution.py:500
  59.5 1.9 %slice.162.refs_1_.refs_8_ = bf16[1024,256]{1,0:T(8,128)(2,1)} slice(bf16[2496,256]{1,0:T(8,128)(2,1)} %projection_slices.1._), slice={[1472:2496], [0:256]} | slice | bytes 1048576 | tf_op jit(solution)/shard_map/slice | solution.py:532
  63.4 13.2 %collective-permute-done.8.refs_15_.refs_9_ = bf16[1472,256]{1,0:T(8,128)(2,1)} collective-permute-done((bf16[1472,256]{1,0:T(8,128)(2,1)}, bf16[1472,256]{1,0:T(8,128)(2,1)}, u32[]{:S(2)}, u32[]{:S(2)}) %collective-permute-start.8) | collective-permute-done | bytes 753696 | tf_op jit(solution)/shard_map/ppermute | solution.py:500
  78.3 2.0 %collective-permute-done.11.refs_7_.refs_11_ = bf16[128,6016]{1,0:T(8,128)(2,1)} collective-permute-done((bf16[128,6016]{1,0:T(8,128)(2,1)}, bf16[128,6016]{1,0:T(8,128)(2,1)}, u32[]{:S(2)}, u32[]{:S(2)}) %collective-permute-start.11) | collective-permute-done | bytes 1540128 | tf_op jit(solution)/shard_map/ppermute | solution.py:500
  80.3 10.5 %forward.1 = (bf16[2048,512]{1,0:T(8,128)(2,1)}, bf16[512,256]{1,0:T(8,128)(2,1)}, f32[8,2,64,256]{3,2,1,0:T(8,128)}) custom-call(s32[4]{0:T(128)} %pad_add_fusion.3.src, s32[8,4]{1,0:T(8,128)} %fusion.16.idx, s32[4]{0:T(128)} %pad_add_fusion.2.pos, bf16[128,6016]{1,0:T(8,128)(2,1)} %get-tuple-element.51.refs_0_, ...), custom_call_target="tpu_custom_call" | custom-call | flops 1024 | bytes 1024 | tf_op jit(solution)/shard_map/forward/pallas_call | solution.py:81
  90.8 1.7 %collective-permute-done.9.refs_2_.refs_9_ = bf16[1024,256]{1,0:T(8,128)(2,1)} collective-permute-done((bf16[1024,256]{1,0:T(8,128)(2,1)}, bf16[1024,256]{1,0:T(8,128)(2,1)}, u32[]{:S(2)}, u32[]{:S(2)}) %collective-permute-start.9) | collective-permute-done | bytes 524320 | tf_op jit(solution)/shard_map/ppermute | solution.py:500
  92.5 1.2 copy-done.8
  93.7 1.3 copy-done.13
  95.0 2.5 %output_slices.1 = (bf16[512,1536]{1,0:T(8,128)(2,1)S(1)}, bf16[512,1536]{1,0:T(8,128)(2,1)S(1)}) custom-call(s32[1]{0:T(128)} %bitcast.core, bf16[512,256]{1,0:T(8,128)(2,1)S(1)} %copy-done.13, bf16[1024,256]{1,0:T(8,128)(2,1)S(1)} %copy-done.8, bf16[1024,256]{1,0:T(8,128)(2,1)} %collective-permute-done.9.refs_2_.refs_9_, bf16[2496,256]{1,0:T(8,128)(2,1)S(1)} %copy-done.7), custom_call_target="tpu_custom_call" | custom-call | flops 99999997952 | bytes 1024 | tf_op jit(solution)/shard_map/output_slices/pallas_call | solution.py:81
  97.7 3.8 %cotangent.1 = (f32[512,256]{1,0:T(8,128)S(1)}, bf16[512,1024]{1,0:T(8,128)(2,1)S(1)}) custom-call(s32[4]{0:T(128)S(1)} %copy-done.10, bf16[128,6016]{1,0:T(8,128)(2,1)S(1)} %copy-done.5, bf16[128,6016]{1,0:T(8,128)(2,1)} %collective-permute-done.1.refs_1_, bf16[128,6016]{1,0:T(8,128)(2,1)} %collective-permute-done.refs_2_, ...), custom_call_target="tpu_custom_call" | custom-call | flops 99999997952 | bytes 1024 | tf_op jit(solution)/shard_map/cotangent/pallas_call | solution.py:81
  102.6 1.5 %collective-permute-start.14 = (bf16[2,128,1536]{2,1,0:T(8,128)(2,1)S(1)}, bf16[2,128,1536]{2,1,0:T(8,128)(2,1)S(1)}, u32[]{:S(2)}, u32[]{:S(2)}) collective-permute-start(bf16[2,128,1536]{2,1,0:T(8,128)(2,1)S(1)} %fusion), channel_id=1, source_target_pairs={{0,2},{1,17},{2,0},{3,19},{4,6},{5,21},{6,4},{7,23},{8,10},{9,25},... | collective-permute-start | bytes 2359304 | tf_op jit(solution)/shard_map/ppermute | solution.py:500
  104.1 3.1 %collective-permute-done.13.refs_2_ = bf16[1024,256]{1,0:T(8,128)(2,1)} collective-permute-done((bf16[1024,256]{1,0:T(8,128)(2,1)}, bf16[1024,256]{1,0:T(8,128)(2,1)}, u32[]{:S(2)}, u32[]{:S(2)}) %collective-permute-start.13) | collective-permute-done | bytes 524320 | tf_op jit(solution)/shard_map/ppermute | solution.py:500
  107.3 7.5 %late_slices.1 = (bf16[512,1536]{1,0:T(8,128)(2,1)}, bf16[512,1024]{1,0:T(8,128)(2,1)}, bf16[256,1536]{1,0:T(8,128)(2,1)}, bf16[256,1536]{1,0:T(8,128)(2,1)}, bf...) custom-call(s32[1]{0:T(128)} %bitcast.core, s32[8,4]{1,0:T(8,128)} %fusion.16.idx, s32[4]{0:T(128)} %pad_add_fusion.2.pos, ...), custom_call_target="tpu_custom_call" | custom-call | flops 99999997952 | bytes 1024 | tf_op jit(solution)/shard_map/late_slices/pallas_call | solution.py:81
  114.8 1.0 copy-done.22
  115.8 2.1 %fusion.4 = bf16[128,1536]{1,0:T(8,128)(2,1)} fusion(bf16[2,128,1536]{2,1,0:T(8,128)(2,1)} %copy-done.22, bf16[4,128,1536]{2,1,0:T(8,128)(2,1)} %bitcast.71, bf16[512,1536]{1,0:T(8,128)(2,1)S(1)} %get-tuple-element.69), kind=kLoop, calls=%fused_computation.11 | loop fusion | flops 1179648 | bytes 1572864 | tf_op jit(solution)/shard_map/convert_element_type | solution.py:584
  118.7 0.9 collective-permute-start.19
  119.6 1.4 add_rows.2
  121.0 1.4 collective-permute-start.17
  123.4 10.4 %collective-permute-done.17 = bf16[2,128,1536]{2,1,0:T(8,128)(2,1)S(1)} collective-permute-done((bf16[2,128,1536]{2,1,0:T(8,128)(2,1)S(1)}, bf16[2,128,1536]{2,1,0:T(8,128)(2,1)S(1)}, u32[]{:S(2)}, u32[]{:S(2)}) %collective-permute-start.17) | collective-permute-done | bytes 786464 | tf_op jit(solution)/shard_map/ppermute | solution.py:500
  134.8 1.4 fusion.5
  136.3 5.3 %collective-permute-done.20 = bf16[2,128,1024]{2,1,0:T(8,128)(2,1)S(1)} collective-permute-done((bf16[2,128,1024]{2,1,0:T(8,128)(2,1)S(1)}, bf16[2,128,1024]{2,1,0:T(8,128)(2,1)S(1)}, u32[]{:S(2)}, u32[]{:S(2)}) %collective-permute-start.20) | collective-permute-done | bytes 524320 | tf_op jit(solution)/shard_map/ppermute | solution.py:500
  142.9 1.2 collective-permute-done.18
  146.5 0.9 fusion.1
  147.4 0.9 collective-permute-done.22
  148.3 0.9 add_convert_fusion
  (114 shorter events, 14.4 us)
Async XLA Ops:
  3.1 49.5 %collective-permute-start.3 = (bf16[2496,256]{1,0:T(8,128)(2,1)}, bf16[2496,256]{1,0:T(8,128)(2,1)S(1)}, u32[]{:S(2)}, u32[]{:S(2)}) collective-permute-start(bf16[2496,256]{1,0:T(8,128)(2,1)} %projection_slices.1._), channel_id=1, source_target_pairs={{0,8},{1,9},{2,10},{3,11},{4,0},{5,1},{6,2},{7,3},{8,12},{9,13},{1... | collective-permute-start | bytes 3833864 | tf_op jit(solution)/shard_map/ppermute | solution.py:500
  7.2 7.1 %copy-start.20 = (bf16[2496,256]{1,0:T(8,128)(2,1)S(1)}, bf16[2496,256]{1,0:T(8,128)(2,1)}, u32[]{:S(2)}) copy-start(bf16[2496,256]{1,0:T(8,128)(2,1)} %projection_slices.1._) | copy-start | bytes 3833860
  11.2 42.8 %collective-permute-start = (bf16[128,6016]{1,0:T(8,128)(2,1)}, bf16[128,6016]{1,0:T(8,128)(2,1)}, u32[]{:S(2)}, u32[]{:S(2)}) collective-permute-start(bf16[128,6016]{1,0:T(8,128)(2,1)} %get-tuple-element.51.refs_0_), channel_id=1, source_target_pairs={{0,2},{1,17},{2,0},{3,19},{4,6},{5,21},{6,4},{7,23},{8,10},{9,25},... | collective-permute-start | bytes 4620296 | tf_op jit(solution)/shard_map/ppermute | solution.py:500
  12.7 41.3 %collective-permute-start.1 = (bf16[128,6016]{1,0:T(8,128)(2,1)}, bf16[128,6016]{1,0:T(8,128)(2,1)}, u32[]{:S(2)}, u32[]{:S(2)}) collective-permute-start(bf16[128,6016]{1,0:T(8,128)(2,1)} %get-tuple-element.51.refs_0_), channel_id=1, source_target_pairs={{0,16},{1,3},{2,18},{3,1},{4,20},{5,7},{6,22},{7,5},{8,24},{9,11},... | collective-permute-start | bytes 4620296 | tf_op jit(solution)/shard_map/ppermute | solution.py:500
  14.3 39.8 %copy-start.18 = (bf16[1472,256]{1,0:T(8,128)(2,1)}, bf16[1472,256]{1,0:T(8,128)(2,1)S(1)}, u32[]{:S(2)}) copy-start(bf16[1472,256]{1,0:T(8,128)(2,1)S(1)} %slice.161.refs_12_.refs_6_) | copy-start | bytes 2260996
  14.3 38.4 %collective-permute-start.2 = (bf16[1472,256]{1,0:T(8,128)(2,1)S(1)}, bf16[1472,256]{1,0:T(8,128)(2,1)S(1)}, u32[]{:S(2)}, u32[]{:S(2)}) collective-permute-start(bf16[1472,256]{1,0:T(8,128)(2,1)S(1)} %slice.161.refs_12_.refs_6_), channel_id=1, source_target_pairs={{0,4},{1,5},{2,6},{3,7},{4,12},{5,13},{6,14},{7,15},{8,0},{9,1},{1... | collective-permute-start | bytes 2261000 | tf_op jit(solution)/shard_map/ppermute | solution.py:500
  54.1 9.3 %collective-permute-start.4 = (bf16[128,6016]{1,0:T(8,128)(2,1)}, bf16[128,6016]{1,0:T(8,128)(2,1)S(1)}, u32[]{:S(2)}, u32[]{:S(2)}) collective-permute-start(bf16[128,6016]{1,0:T(8,128)(2,1)} %collective-permute-done.refs_2_), channel_id=1, source_target_pairs={{0,1},{1,0},{2,3},{3,2},{4,5},{5,4},{6,7},{7,6},{8,9},{9,8},{10,11... | collective-permute-start | bytes 4620296 | tf_op jit(solution)/shard_map/ppermute | solution.py:500
  54.1 9.2 %collective-permute-start.5 = (bf16[128,6016]{1,0:T(8,128)(2,1)}, bf16[128,6016]{1,0:T(8,128)(2,1)S(1)}, u32[]{:S(2)}, u32[]{:S(2)}) collective-permute-start(bf16[128,6016]{1,0:T(8,128)(2,1)} %collective-permute-done.1.refs_1_), channel_id=1, source_target_pairs={{0,1},{1,0},{2,3},{3,2},{4,5},{5,4},{6,7},{7,6},{8,9},{9,8},{10,11... | collective-permute-start | bytes 4620296 | tf_op jit(solution)/shard_map/ppermute | solution.py:500
  54.6 22.0 %collective-permute-start.10 = (bf16[128,6016]{1,0:T(8,128)(2,1)}, bf16[128,6016]{1,0:T(8,128)(2,1)}, u32[]{:S(2)}, u32[]{:S(2)}) collective-permute-start(bf16[128,6016]{1,0:T(8,128)(2,1)} %collective-permute-done.refs_2_), channel_id=1, source_target_pairs={{0,16},{1,3},{2,18},{3,1},{4,20},{5,7},{6,22},{7,5},{8,24},{9,11},... | collective-permute-start | bytes 4620296 | tf_op jit(solution)/shard_map/ppermute | solution.py:500
  56.2 3.2 %collective-permute-start.6 = (bf16[128,2048]{1,0:T(8,128)(2,1)}, bf16[128,2048]{1,0:T(8,128)(2,1)}, u32[]{:S(2)}, u32[]{:S(2)}) collective-permute-start(bf16[128,2048]{1,0:T(8,128)(2,1)} %hid.1), channel_id=1, source_target_pairs={{0,1},{1,0},{2,3},{3,2},{4,5},{5,4},{6,7},{7,6},{8,9},{9,8},{10,11... | collective-permute-start | bytes 1572872 | tf_op jit(solution)/shard_map/ppermute | solution.py:500
  56.2 20.5 %collective-permute-start.8 = (bf16[1472,256]{1,0:T(8,128)(2,1)}, bf16[1472,256]{1,0:T(8,128)(2,1)}, u32[]{:S(2)}, u32[]{:S(2)}) collective-permute-start(bf16[1472,256]{1,0:T(8,128)(2,1)} %copy-done.24), channel_id=1, source_target_pairs={{0,4},{1,5},{2,6},{3,7},{4,12},{5,13},{6,14},{7,15},{8,0},{9,1},{1... | collective-permute-start | bytes 2261000 | tf_op jit(solution)/shard_map/ppermute | solution.py:500
  59.3 3.2 %collective-permute-start.7 = (bf16[128,2048]{1,0:T(8,128)(2,1)}, bf16[128,2048]{1,0:T(8,128)(2,1)S(1)}, u32[]{:S(2)}, u32[]{:S(2)}) collective-permute-start(bf16[128,2048]{1,0:T(8,128)(2,1)} %grad.1), channel_id=1, source_target_pairs={{0,1},{1,0},{2,3},{3,2},{4,5},{5,4},{6,7},{7,6},{8,9},{9,8},{10,11... | collective-permute-start | bytes 1572872 | tf_op jit(solution)/shard_map/ppermute | solution.py:500
  63.4 17.0 %copy-start = (bf16[128,6016]{1,0:T(8,128)(2,1)}, bf16[128,6016]{1,0:T(8,128)(2,1)S(1)}, u32[]{:S(2)}) copy-start(bf16[128,6016]{1,0:T(8,128)(2,1)S(1)} %collective-permute-done.4.refs_5_.refs_9_) | copy-start | bytes 4620292
  63.4 16.9 %copy-start.2 = (bf16[128,6016]{1,0:T(8,128)(2,1)}, bf16[128,6016]{1,0:T(8,128)(2,1)S(1)}, u32[]{:S(2)}) copy-start(bf16[128,6016]{1,0:T(8,128)(2,1)S(1)} %collective-permute-done.5.refs_6_.refs_10_) | copy-start | bytes 4620292
  76.6 3.7 %collective-permute-start.11 = (bf16[128,6016]{1,0:T(8,128)(2,1)}, bf16[128,6016]{1,0:T(8,128)(2,1)}, u32[]{:S(2)}, u32[]{:S(2)}) collective-permute-start(bf16[128,6016]{1,0:T(8,128)(2,1)} %collective-permute-done.10.refs_3_), channel_id=1, source_target_pairs={{0,1},{1,0},{2,3},{3,2},{4,5},{5,4},{6,7},{7,6},{8,9},{9,8},{10,11... | collective-permute-start | bytes 4620296 | tf_op jit(solution)/shard_map/ppermute | solution.py:500
  77.0 15.6 %collective-permute-start.9 = (bf16[1024,256]{1,0:T(8,128)(2,1)}, bf16[1024,256]{1,0:T(8,128)(2,1)}, u32[]{:S(2)}, u32[]{:S(2)}) collective-permute-start(bf16[1024,256]{1,0:T(8,128)(2,1)} %slice.162.refs_1_.refs_8_), channel_id=1, source_target_pairs={{0,4},{1,5},{2,6},{3,7},{4,12},{5,13},{6,14},{7,15},{8,0},{9,1},{1... | collective-permute-start | bytes 1572872 | tf_op jit(solution)/shard_map/ppermute | solution.py:500
  80.3 12.2 %copy-start.7 = (bf16[2496,256]{1,0:T(8,128)(2,1)S(1)}, bf16[2496,256]{1,0:T(8,128)(2,1)}, u32[]{:S(2)}) copy-start(bf16[2496,256]{1,0:T(8,128)(2,1)} %copy-done.6) | copy-start | bytes 3833860
  92.5 14.8 %collective-permute-start.13 = (bf16[1024,256]{1,0:T(8,128)(2,1)}, bf16[1024,256]{1,0:T(8,128)(2,1)}, u32[]{:S(2)}, u32[]{:S(2)}) collective-permute-start(bf16[1024,256]{1,0:T(8,128)(2,1)} %collective-permute-done.9.refs_2_.refs_9_), channel_id=1, source_target_pairs={{0,4},{1,5},{2,6},{3,7},{4,12},{5,13},{6,14},{7,15},{8,0},{9,1},{1... | collective-permute-start | bytes 1572872 | tf_op jit(solution)/shard_map/ppermute | solution.py:500
  97.5 18.3 %copy-start.4 = (bf16[512,1536]{1,0:T(8,128)(2,1)}, bf16[512,1536]{1,0:T(8,128)(2,1)S(1)}, u32[]{:S(2)}) copy-start(bf16[512,1536]{1,0:T(8,128)(2,1)S(1)} %get-tuple-element.69) | copy-start | bytes 4718596
  97.5 4.1 %collective-permute-start.12 = (bf16[512,1536]{1,0:T(8,128)(2,1)S(1)}, bf16[512,1536]{1,0:T(8,128)(2,1)S(1)}, u32[]{:S(2)}, u32[]{:S(2)}) collective-permute-start(bf16[512,1536]{1,0:T(8,128)(2,1)S(1)} %get-tuple-element.70), channel_id=1, source_target_pairs={{0,1},{1,0},{2,3},{3,2},{4,5},{5,4},{6,7},{7,6},{8,9},{9,8},{10,11... | collective-permute-start | bytes 4718600 | tf_op jit(solution)/shard_map/ppermute | solution.py:500
  102.6 12.2 %collective-permute-start.14 = (bf16[2,128,1536]{2,1,0:T(8,128)(2,1)S(1)}, bf16[2,128,1536]{2,1,0:T(8,128)(2,1)S(1)}, u32[]{:S(2)}, u32[]{:S(2)}) collective-permute-start(bf16[2,128,1536]{2,1,0:T(8,128)(2,1)S(1)} %fusion), channel_id=1, source_target_pairs={{0,2},{1,17},{2,0},{3,19},{4,6},{5,21},{6,4},{7,23},{8,10},{9,25},... | collective-permute-start | bytes 2359304 | tf_op jit(solution)/shard_map/ppermute | solution.py:500
  115.8 3.8 %collective-permute-start.16 = (bf16[512,1536]{1,0:T(8,128)(2,1)}, bf16[512,1536]{1,0:T(8,128)(2,1)S(1)}, u32[]{:S(2)}, u32[]{:S(2)}) collective-permute-start(bf16[512,1536]{1,0:T(8,128)(2,1)} %get-tuple-element.82), channel_id=1, source_target_pairs={{0,1},{1,0},{2,3},{3,2},{4,5},{5,4},{6,7},{7,6},{8,9},{9,8},{10,11... | collective-permute-start | bytes 4718600 | tf_op jit(solution)/shard_map/ppermute | solution.py:500
  117.9 17.0 %collective-permute-start.15 = (bf16[128,1536]{1,0:T(8,128)(2,1)}, bf16[128,1536]{1,0:T(8,128)(2,1)}, u32[]{:S(2)}, u32[]{:S(2)}) collective-permute-start(bf16[128,1536]{1,0:T(8,128)(2,1)} %fusion.4), channel_id=1, source_target_pairs={{0,16},{1,3},{2,18},{3,1},{4,20},{5,7},{6,22},{7,5},{8,24},{9,11},... | collective-permute-start | bytes 1179656 | tf_op jit(solution)/shard_map/ppermute | solution.py:500
  118.7 3.7 %collective-permute-start.19 = (bf16[512,1024]{1,0:T(8,128)(2,1)}, bf16[512,1024]{1,0:T(8,128)(2,1)S(1)}, u32[]{:S(2)}, u32[]{:S(2)}) collective-permute-start(bf16[512,1024]{1,0:T(8,128)(2,1)} %get-tuple-element.88), channel_id=1, source_target_pairs={{0,1},{1,0},{2,3},{3,2},{4,5},{5,4},{6,7},{7,6},{8,9},{9,8},{10,11... | collective-permute-start | bytes 3145736 | tf_op jit(solution)/shard_map/ppermute | solution.py:500
  121.0 12.8 %collective-permute-start.17 = (bf16[2,128,1536]{2,1,0:T(8,128)(2,1)S(1)}, bf16[2,128,1536]{2,1,0:T(8,128)(2,1)S(1)}, u32[]{:S(2)}, u32[]{:S(2)}) collective-permute-start(bf16[2,128,1536]{2,1,0:T(8,128)(2,1)S(1)} %bitcast.67), channel_id=1, source_target_pairs={{0,2},{1,17},{2,0},{3,19},{4,6},{5,21},{6,4},{7,23},{8,10},{9,25},... | collective-permute-start | bytes 2359304 | tf_op jit(solution)/shard_map/ppermute | solution.py:500
  122.3 11.5 %copy-start.21 = (bf16[256,1536]{1,0:T(8,128)(2,1)S(1)}, bf16[256,1536]{1,0:T(8,128)(2,1)}, u32[]{:S(2)}) copy-start(bf16[256,1536]{1,0:T(8,128)(2,1)} %get-tuple-element.81) | copy-start | bytes 2359300
  122.6 12.2 %copy-start.23 = (bf16[2,128,1536]{2,1,0:T(8,128)(2,1)S(1)}, bf16[2,128,1536]{2,1,0:T(8,128)(2,1)}, u32[]{:S(2)}) copy-start(bf16[2,128,1536]{2,1,0:T(8,128)(2,1)} %copy-done.22) | copy-start | bytes 2359300
  122.7 18.9 %collective-permute-start.20 = (bf16[2,128,1024]{2,1,0:T(8,128)(2,1)S(1)}, bf16[2,128,1024]{2,1,0:T(8,128)(2,1)S(1)}, u32[]{:S(2)}, u32[]{:S(2)}) collective-permute-start(bf16[2,128,1024]{2,1,0:T(8,128)(2,1)S(1)} %bitcast.68), channel_id=1, source_target_pairs={{0,2},{1,17},{2,0},{3,19},{4,6},{5,21},{6,4},{7,23},{8,10},{9,25},... | collective-permute-start | bytes 1572872 | tf_op jit(solution)/shard_map/ppermute | solution.py:500
  134.0 7.6 %copy-start.27 = (bf16[256,1024]{1,0:T(8,128)(2,1)S(1)}, bf16[256,1024]{1,0:T(8,128)(2,1)}, u32[]{:S(2)}) copy-start(bf16[256,1024]{1,0:T(8,128)(2,1)} %get-tuple-element.87) | copy-start | bytes 1572868
  134.0 10.1 %collective-permute-start.18 = (bf16[128,1536]{1,0:T(8,128)(2,1)S(1)}, bf16[128,1536]{1,0:T(8,128)(2,1)S(1)}, u32[]{:S(2)}, u32[]{:S(2)}) collective-permute-start(bf16[128,1536]{1,0:T(8,128)(2,1)S(1)} %fusion.3), channel_id=1, source_target_pairs={{0,16},{1,3},{2,18},{3,1},{4,20},{5,7},{6,22},{7,5},{8,24},{9,11},... | collective-permute-start | bytes 1179656 | tf_op jit(solution)/shard_map/ppermute | solution.py:500
  141.8 6.4 %collective-permute-start.22 = (bf16[128,1024]{1,0:T(8,128)(2,1)S(1)}, bf16[128,1024]{1,0:T(8,128)(2,1)S(1)}, u32[]{:S(2)}, u32[]{:S(2)}) collective-permute-start(bf16[128,1024]{1,0:T(8,128)(2,1)S(1)} %get-tuple-element.95), channel_id=1, source_target_pairs={{0,16},{1,3},{2,18},{3,1},{4,20},{5,7},{6,22},{7,5},{8,24},{9,11},... | collective-permute-start | bytes 786440 | tf_op jit(solution)/shard_map/ppermute | solution.py:500
  144.4 1.6 %collective-permute-start.21 = (bf16[2,128,512]{2,1,0:T(8,128)(2,1)S(1)}, bf16[2,128,512]{2,1,0:T(8,128)(2,1)S(1)}, u32[]{:S(2)}, u32[]{:S(2)}) collective-permute-start(bf16[2,128,512]{2,1,0:T(8,128)(2,1)S(1)} %slice.218), channel_id=1, source_target_pairs={{0,1},{1,0},{2,3},{3,2},{4,5},{5,4},{6,7},{7,6},{8,9},{9,8},{10,11... | collective-permute-start | bytes 786440 | tf_op jit(solution)/shard_map/ppermute | solution.py:500
  (19 other events, 43.6 us)

commit v7 on v6

--- a/solution.py
+++ b/solution.py
@@ -410,8 +410,8 @@
 def late_slices(core, idx, pos, gm, rest, part, mix, kv, att, parts):
     tokens, width = gm.shape
     depth = part.shape[0]
-    wide = shape_of((tokens, depth // 2 + depth))
-    narrow = shape_of((tokens, depth))
+    wide = shape_of((tokens, depth // 2 + depth * 5 // 4))
+    narrow = shape_of((tokens, depth * 3 // 4))
     heads = shape_of((tokens, width))
     return copy_call(
         late_kernel,

time: 150 us -> 150 us (level)
  Pallas kernels: 32.5 us -> 34.6 us
  waiting for transfers between devices: 79.1 us -> 77 us
    pallas_call x6, Pallas kernels: 26 us -> 28.1 us  [copy_call(): pl.pallas_call(body, in_specs=[smem] * len(scalars) + [pl.BlockSpec(memor...]
    ppermute x23, waiting for transfers between devices: 79.1 us -> 77 us  [move(): return lax.ppermute(array, AXES, pairs)]
  transfers between devices with their start and end apart: 23 -> 23, of which waited for: 11 -> 11; matrix products, arithmetic and copies ran while one was open for 8% -> 8% of each run, Pallas kernels for 20% -> 22%
where the time goes in v7:
time: 150 us; the launch traced here: 149 us
  waiting for transfers between devices  77 us (51%)
  Pallas kernels  34.6 us (23%)
  starting transfers between devices  17.3 us (12%)
  other arithmetic  10.2 us (7%)
  local copies, waits for them, and re-layouts  8.94 us (6%)
    ppermute x23, waiting for transfers between devices, move(): return lax.ppermute(array, AXES, pairs)  77 us
    pallas_call x6, Pallas kernels, copy_call(): pl.pallas_call(body, in_specs=[smem] * len(scalars) + [pl.BlockSpec(memor...  28.1 us
    ppermute x23, starting transfers between devices, move(): return lax.ppermute(array, AXES, pairs)  17.3 us
    pallas_call x2, Pallas kernels, kernel_call(): pl.pallas_call(body, grid_spec=pltpu.PrefetchScalarGridSpec(num_scalar_pr...  6.52 us
    unnamed x56, local copies, waits for them, and re-layouts  6.22 us
  transfers between devices with their start and end apart: 23, of which 11 were waited for; matrix products, arithmetic and copies ran while one was open for 8% of the time, Pallas kernels for 22%

profile of v7, /device:TPU:0, one launch (start us, length us, event | category | flops | bytes accessed | tf_op | source)
XLA Modules:
  0.0 149.2 jit_solution(6719137359628470070)
XLA Ops:
  0.6 2.5 %projection_slices.1._ = bf16[2496,256]{1,0:T(8,128)(2,1)} custom-call(s32[1]{0:T(128)} %bitcast.1.place, bf16[1024,1024]{1,0:T(8,128)(2,1)} %q.1, bf16[224,1024]{1,0:T(8,128)(2,1)} %k.1, bf16[224,1024]{1,0:T(8,128)(2,1)} %v.1, bf16[1024,1024]{1,0:T(8,128)(2,1)} %o.1), custom_call_target="tpu_custom_call" | custom-call | flops 99999997952 | bytes 1024 | tf_op jit(solution)/shard_map/projection_slices/pallas_call | solution.py:47
  3.1 4.0 %collective-permute-start.3 = (bf16[2496,256]{1,0:T(8,128)(2,1)}, bf16[2496,256]{1,0:T(8,128)(2,1)S(1)}, u32[]{:S(2)}, u32[]{:S(2)}) collective-permute-start(bf16[2496,256]{1,0:T(8,128)(2,1)} %projection_slices.1._), channel_id=1, source_target_pairs={{0,8},{1,9},{2,10},{3,11},{4,0},{5,1},{6,2},{7,3},{8,12},{9,13},{1... | collective-permute-start | bytes 3833864 | tf_op jit(solution)/shard_map/ppermute | solution.py:500
  7.1 4.1 %prepare.1 = (bf16[128,6016]{1,0:T(8,128)(2,1)}, bf16[128,1792]{1,0:T(8,128)(2,1)}) custom-call(s32[1]{0:T(128)} %bitcast.core, s32[2,4]{1,0:T(2,128)} %owners.1, s32[2,4]{1,0:T(2,128)} %ids.1, bf16[128,2048]{1,0:T(8,128)(2,1)} %hid.1, bf16[128,2048]{1,0:T(8,128)(2,1)} %grad.1, bf16[8,64,896]{2,1,0:T(8,128)(2,1)} %db.1, f32[896]{0:T(1024)} %gain.1, ...), custom_call_target="tpu_custom_call" | custom-call | flops 99999997952 | bytes 1024 | tf_op jit(solution)/shard_map/prepare/pallas_call | solution.py:47
  11.2 1.5 collective-permute-start
  12.7 1.5 %collective-permute-start.1 = (bf16[128,6016]{1,0:T(8,128)(2,1)}, bf16[128,6016]{1,0:T(8,128)(2,1)}, u32[]{:S(2)}, u32[]{:S(2)}) collective-permute-start(bf16[128,6016]{1,0:T(8,128)(2,1)} %get-tuple-element.51.refs_0_), channel_id=1, source_target_pairs={{0,16},{1,3},{2,18},{3,1},{4,20},{5,7},{6,22},{7,5},{8,24},{9,11},... | collective-permute-start | bytes 4620296 | tf_op jit(solution)/shard_map/ppermute | solution.py:500
  14.3 38.3 %collective-permute-done.2.refs_13_.refs_7_ = bf16[1472,256]{1,0:T(8,128)(2,1)S(1)} collective-permute-done((bf16[1472,256]{1,0:T(8,128)(2,1)S(1)}, bf16[1472,256]{1,0:T(8,128)(2,1)S(1)}, u32[]{:S(2)}, u32[]{:S(2)}) %collective-permute-start.2) | collective-permute-done | bytes 753696 | tf_op jit(solution)/shard_map/ppermute | solution.py:500
  54.7 1.5 %collective-permute-start.10 = (bf16[128,6016]{1,0:T(8,128)(2,1)}, bf16[128,6016]{1,0:T(8,128)(2,1)}, u32[]{:S(2)}, u32[]{:S(2)}) collective-permute-start(bf16[128,6016]{1,0:T(8,128)(2,1)} %collective-permute-done.refs_2_), channel_id=1, source_target_pairs={{0,16},{1,3},{2,18},{3,1},{4,20},{5,7},{6,22},{7,5},{8,24},{9,11},... | collective-permute-start | bytes 4620296 | tf_op jit(solution)/shard_map/ppermute | solution.py:500
  56.9 2.4 %collective-permute-done.6.refs_8_ = bf16[128,2048]{1,0:T(8,128)(2,1)} collective-permute-done((bf16[128,2048]{1,0:T(8,128)(2,1)}, bf16[128,2048]{1,0:T(8,128)(2,1)}, u32[]{:S(2)}, u32[]{:S(2)}) %collective-permute-start.6) | collective-permute-done | bytes 524320 | tf_op jit(solution)/shard_map/ppermute | solution.py:500
  59.5 1.9 %slice.162.refs_1_.refs_8_ = bf16[1024,256]{1,0:T(8,128)(2,1)} slice(bf16[2496,256]{1,0:T(8,128)(2,1)} %projection_slices.1._), slice={[1472:2496], [0:256]} | slice | bytes 1048576 | tf_op jit(solution)/shard_map/slice | solution.py:532
  63.5 13.1 %collective-permute-done.8.refs_15_.refs_9_ = bf16[1472,256]{1,0:T(8,128)(2,1)} collective-permute-done((bf16[1472,256]{1,0:T(8,128)(2,1)}, bf16[1472,256]{1,0:T(8,128)(2,1)}, u32[]{:S(2)}, u32[]{:S(2)}) %collective-permute-start.8) | collective-permute-done | bytes 753696 | tf_op jit(solution)/shard_map/ppermute | solution.py:500
  78.4 2.0 %collective-permute-done.11.refs_7_.refs_11_ = bf16[128,6016]{1,0:T(8,128)(2,1)} collective-permute-done((bf16[128,6016]{1,0:T(8,128)(2,1)}, bf16[128,6016]{1,0:T(8,128)(2,1)}, u32[]{:S(2)}, u32[]{:S(2)}) %collective-permute-start.11) | collective-permute-done | bytes 1540128 | tf_op jit(solution)/shard_map/ppermute | solution.py:500
  80.4 10.6 %forward.1 = (bf16[2048,512]{1,0:T(8,128)(2,1)}, bf16[512,256]{1,0:T(8,128)(2,1)}, f32[8,2,64,256]{3,2,1,0:T(8,128)}) custom-call(s32[4]{0:T(128)} %pad_add_fusion.3.src, s32[8,4]{1,0:T(8,128)} %fusion.16.idx, s32[4]{0:T(128)} %pad_add_fusion.2.pos, bf16[128,6016]{1,0:T(8,128)(2,1)} %get-tuple-element.51.refs_0_, ...), custom_call_target="tpu_custom_call" | custom-call | flops 1024 | bytes 1024 | tf_op jit(solution)/shard_map/forward/pallas_call | solution.py:81
  91.0 1.6 %collective-permute-done.9.refs_2_.refs_9_ = bf16[1024,256]{1,0:T(8,128)(2,1)} collective-permute-done((bf16[1024,256]{1,0:T(8,128)(2,1)}, bf16[1024,256]{1,0:T(8,128)(2,1)}, u32[]{:S(2)}, u32[]{:S(2)}) %collective-permute-start.9) | collective-permute-done | bytes 524320 | tf_op jit(solution)/shard_map/ppermute | solution.py:500
  92.6 1.2 copy-done.8
  93.8 1.3 copy-done.13
  95.1 2.5 %output_slices.1 = (bf16[512,1536]{1,0:T(8,128)(2,1)S(1)}, bf16[512,1536]{1,0:T(8,128)(2,1)S(1)}) custom-call(s32[1]{0:T(128)} %bitcast.core, bf16[512,256]{1,0:T(8,128)(2,1)S(1)} %copy-done.13, bf16[1024,256]{1,0:T(8,128)(2,1)S(1)} %copy-done.8, bf16[1024,256]{1,0:T(8,128)(2,1)} %collective-permute-done.9.refs_2_.refs_9_, bf16[2496,256]{1,0:T(8,128)(2,1)S(1)} %copy-done.7), custom_call_target="tpu_custom_call" | custom-call | flops 99999997952 | bytes 1024 | tf_op jit(solution)/shard_map/output_slices/pallas_call | solution.py:81
  97.7 3.8 %cotangent.1 = (f32[512,256]{1,0:T(8,128)S(1)}, bf16[512,1024]{1,0:T(8,128)(2,1)S(1)}) custom-call(s32[4]{0:T(128)S(1)} %copy-done.10, bf16[128,6016]{1,0:T(8,128)(2,1)S(1)} %copy-done.5, bf16[128,6016]{1,0:T(8,128)(2,1)} %collective-permute-done.1.refs_1_, bf16[128,6016]{1,0:T(8,128)(2,1)} %collective-permute-done.refs_2_, ...), custom_call_target="tpu_custom_call" | custom-call | flops 99999997952 | bytes 1024 | tf_op jit(solution)/shard_map/cotangent/pallas_call | solution.py:81
  102.7 1.5 collective-permute-start.14
  104.2 3.2 %collective-permute-done.13.refs_2_ = bf16[1024,256]{1,0:T(8,128)(2,1)} collective-permute-done((bf16[1024,256]{1,0:T(8,128)(2,1)}, bf16[1024,256]{1,0:T(8,128)(2,1)}, u32[]{:S(2)}, u32[]{:S(2)}) %collective-permute-start.13) | collective-permute-done | bytes 524320 | tf_op jit(solution)/shard_map/ppermute | solution.py:500
  107.3 7.7 %late_slices.1 = (bf16[512,1792]{1,0:T(8,128)(2,1)}, bf16[512,768]{1,0:T(8,128)(2,1)}, bf16[256,1792]{1,0:T(8,128)(2,1)}, bf16[256,1792]{1,0:T(8,128)(2,1)}, bf1...) custom-call(s32[1]{0:T(128)} %bitcast.core, s32[8,4]{1,0:T(8,128)} %fusion.16.idx, s32[4]{0:T(128)} %pad_add_fusion.2.pos, ...), custom_call_target="tpu_custom_call" | custom-call | flops 99999997952 | bytes 1024 | tf_op jit(solution)/shard_map/late_slices/pallas_call | solution.py:81
  115.0 0.9 copy-done.22
  116.0 2.1 %fusion.4 = bf16[128,1536]{1,0:T(8,128)(2,1)} fusion(bf16[2,128,1536]{2,1,0:T(8,128)(2,1)} %copy-done.22, bf16[4,128,1536]{2,1,0:T(8,128)(2,1)} %bitcast.71, bf16[512,1536]{1,0:T(8,128)(2,1)S(1)} %get-tuple-element.69), kind=kLoop, calls=%fused_computation.11 | loop fusion | flops 1179648 | bytes 1572864 | tf_op jit(solution)/shard_map/convert_element_type | solution.py:584
  118.8 0.9 collective-permute-start.19
  120.0 1.9 %add_rows.2 = bf16[256,1792]{1,0:T(8,128)(2,1)S(1)} custom-call(bf16[256,1792]{1,0:T(8,128)(2,1)S(1)} %copy-done.15, bf16[512,1792]{1,0:T(8,128)(2,1)S(1)} %collective-permute-done.16.refs_1_), custom_call_target="tpu_custom_call" | custom-call | flops 99999997952 | bytes 1024 | tf_op jit(solution)/shard_map/add_rows/pallas_call | solution.py:81
  121.9 1.6 %collective-permute-start.17 = (bf16[2,128,1792]{2,1,0:T(8,128)(2,1)S(1)}, bf16[2,128,1792]{2,1,0:T(8,128)(2,1)S(1)}, u32[]{:S(2)}, u32[]{:S(2)}) collective-permute-start(bf16[2,128,1792]{2,1,0:T(8,128)(2,1)S(1)} %bitcast.67), channel_id=1, source_target_pairs={{0,2},{1,17},{2,0},{3,19},{4,6},{5,21},{6,4},{7,23},{8,10},{9,25},... | collective-permute-start | bytes 2752520 | tf_op jit(solution)/shard_map/ppermute | solution.py:500
  123.4 1.7 %add_rows.3 = bf16[256,768]{1,0:T(8,128)(2,1)S(1)} custom-call(bf16[256,768]{1,0:T(8,128)(2,1)S(1)} %copy-done.17, bf16[512,768]{1,0:T(8,128)(2,1)S(1)} %collective-permute-done.19.refs_1_), custom_call_target="tpu_custom_call" | custom-call | flops 99999997952 | bytes 1024 | tf_op jit(solution)/shard_map/add_rows/pallas_call | solution.py:81
  125.7 9.7 %collective-permute-done.17 = bf16[2,128,1792]{2,1,0:T(8,128)(2,1)S(1)} collective-permute-done((bf16[2,128,1792]{2,1,0:T(8,128)(2,1)S(1)}, bf16[2,128,1792]{2,1,0:T(8,128)(2,1)S(1)}, u32[]{:S(2)}, u32[]{:S(2)}) %collective-permute-start.17) | collective-permute-done | bytes 917536 | tf_op jit(solution)/shard_map/ppermute | solution.py:500
  136.5 1.4 fusion.5
  137.9 2.5 %collective-permute-done.20 = bf16[2,128,768]{2,1,0:T(8,128)(2,1)S(1)} collective-permute-done((bf16[2,128,768]{2,1,0:T(8,128)(2,1)S(1)}, bf16[2,128,768]{2,1,0:T(8,128)(2,1)S(1)}, u32[]{:S(2)}, u32[]{:S(2)}) %collective-permute-start.20) | collective-permute-done | bytes 393248 | tf_op jit(solution)/shard_map/ppermute | solution.py:500
  141.6 3.4 %collective-permute-done.18 = bf16[128,1792]{1,0:T(8,128)(2,1)S(1)} collective-permute-done((bf16[128,1792]{1,0:T(8,128)(2,1)S(1)}, bf16[128,1792]{1,0:T(8,128)(2,1)S(1)}, u32[]{:S(2)}, u32[]{:S(2)}) %collective-permute-start.18) | collective-permute-done | bytes 458784 | tf_op jit(solution)/shard_map/ppermute | solution.py:500
  147.4 0.9 fusion.1
  148.3 0.9 add_convert_fusion
  (114 shorter events, 14.2 us)
Async XLA Ops:
  3.1 49.5 %collective-permute-start.3 = (bf16[2496,256]{1,0:T(8,128)(2,1)}, bf16[2496,256]{1,0:T(8,128)(2,1)S(1)}, u32[]{:S(2)}, u32[]{:S(2)}) collective-permute-start(bf16[2496,256]{1,0:T(8,128)(2,1)} %projection_slices.1._), channel_id=1, source_target_pairs={{0,8},{1,9},{2,10},{3,11},{4,0},{5,1},{6,2},{7,3},{8,12},{9,13},{1... | collective-permute-start | bytes 3833864 | tf_op jit(solution)/shard_map/ppermute | solution.py:500
  7.1 7.1 %copy-start.20 = (bf16[2496,256]{1,0:T(8,128)(2,1)S(1)}, bf16[2496,256]{1,0:T(8,128)(2,1)}, u32[]{:S(2)}) copy-start(bf16[2496,256]{1,0:T(8,128)(2,1)} %projection_slices.1._) | copy-start | bytes 3833860
  11.2 42.9 %collective-permute-start = (bf16[128,6016]{1,0:T(8,128)(2,1)}, bf16[128,6016]{1,0:T(8,128)(2,1)}, u32[]{:S(2)}, u32[]{:S(2)}) collective-permute-start(bf16[128,6016]{1,0:T(8,128)(2,1)} %get-tuple-element.51.refs_0_), channel_id=1, source_target_pairs={{0,2},{1,17},{2,0},{3,19},{4,6},{5,21},{6,4},{7,23},{8,10},{9,25},... | collective-permute-start | bytes 4620296 | tf_op jit(solution)/shard_map/ppermute | solution.py:500
  12.7 41.4 %collective-permute-start.1 = (bf16[128,6016]{1,0:T(8,128)(2,1)}, bf16[128,6016]{1,0:T(8,128)(2,1)}, u32[]{:S(2)}, u32[]{:S(2)}) collective-permute-start(bf16[128,6016]{1,0:T(8,128)(2,1)} %get-tuple-element.51.refs_0_), channel_id=1, source_target_pairs={{0,16},{1,3},{2,18},{3,1},{4,20},{5,7},{6,22},{7,5},{8,24},{9,11},... | collective-permute-start | bytes 4620296 | tf_op jit(solution)/shard_map/ppermute | solution.py:500
  14.3 39.8 %copy-start.18 = (bf16[1472,256]{1,0:T(8,128)(2,1)}, bf16[1472,256]{1,0:T(8,128)(2,1)S(1)}, u32[]{:S(2)}) copy-start(bf16[1472,256]{1,0:T(8,128)(2,1)S(1)} %slice.161.refs_12_.refs_6_) | copy-start | bytes 2260996
  14.3 38.4 %collective-permute-start.2 = (bf16[1472,256]{1,0:T(8,128)(2,1)S(1)}, bf16[1472,256]{1,0:T(8,128)(2,1)S(1)}, u32[]{:S(2)}, u32[]{:S(2)}) collective-permute-start(bf16[1472,256]{1,0:T(8,128)(2,1)S(1)} %slice.161.refs_12_.refs_6_), channel_id=1, source_target_pairs={{0,4},{1,5},{2,6},{3,7},{4,12},{5,13},{6,14},{7,15},{8,0},{9,1},{1... | collective-permute-start | bytes 2261000 | tf_op jit(solution)/shard_map/ppermute | solution.py:500
  54.1 9.4 %collective-permute-start.4 = (bf16[128,6016]{1,0:T(8,128)(2,1)}, bf16[128,6016]{1,0:T(8,128)(2,1)S(1)}, u32[]{:S(2)}, u32[]{:S(2)}) collective-permute-start(bf16[128,6016]{1,0:T(8,128)(2,1)} %collective-permute-done.refs_2_), channel_id=1, source_target_pairs={{0,1},{1,0},{2,3},{3,2},{4,5},{5,4},{6,7},{7,6},{8,9},{9,8},{10,11... | collective-permute-start | bytes 4620296 | tf_op jit(solution)/shard_map/ppermute | solution.py:500
  54.2 9.3 %collective-permute-start.5 = (bf16[128,6016]{1,0:T(8,128)(2,1)}, bf16[128,6016]{1,0:T(8,128)(2,1)S(1)}, u32[]{:S(2)}, u32[]{:S(2)}) collective-permute-start(bf16[128,6016]{1,0:T(8,128)(2,1)} %collective-permute-done.1.refs_1_), channel_id=1, source_target_pairs={{0,1},{1,0},{2,3},{3,2},{4,5},{5,4},{6,7},{7,6},{8,9},{9,8},{10,11... | collective-permute-start | bytes 4620296 | tf_op jit(solution)/shard_map/ppermute | solution.py:500
  54.7 22.0 %collective-permute-start.10 = (bf16[128,6016]{1,0:T(8,128)(2,1)}, bf16[128,6016]{1,0:T(8,128)(2,1)}, u32[]{:S(2)}, u32[]{:S(2)}) collective-permute-start(bf16[128,6016]{1,0:T(8,128)(2,1)} %collective-permute-done.refs_2_), channel_id=1, source_target_pairs={{0,16},{1,3},{2,18},{3,1},{4,20},{5,7},{6,22},{7,5},{8,24},{9,11},... | collective-permute-start | bytes 4620296 | tf_op jit(solution)/shard_map/ppermute | solution.py:500
  56.2 3.2 %collective-permute-start.6 = (bf16[128,2048]{1,0:T(8,128)(2,1)}, bf16[128,2048]{1,0:T(8,128)(2,1)}, u32[]{:S(2)}, u32[]{:S(2)}) collective-permute-start(bf16[128,2048]{1,0:T(8,128)(2,1)} %hid.1), channel_id=1, source_target_pairs={{0,1},{1,0},{2,3},{3,2},{4,5},{5,4},{6,7},{7,6},{8,9},{9,8},{10,11... | collective-permute-start | bytes 1572872 | tf_op jit(solution)/shard_map/ppermute | solution.py:500
  56.2 20.5 %collective-permute-start.8 = (bf16[1472,256]{1,0:T(8,128)(2,1)}, bf16[1472,256]{1,0:T(8,128)(2,1)}, u32[]{:S(2)}, u32[]{:S(2)}) collective-permute-start(bf16[1472,256]{1,0:T(8,128)(2,1)} %copy-done.24), channel_id=1, source_target_pairs={{0,4},{1,5},{2,6},{3,7},{4,12},{5,13},{6,14},{7,15},{8,0},{9,1},{1... | collective-permute-start | bytes 2261000 | tf_op jit(solution)/shard_map/ppermute | solution.py:500
  59.4 3.3 %collective-permute-start.7 = (bf16[128,2048]{1,0:T(8,128)(2,1)}, bf16[128,2048]{1,0:T(8,128)(2,1)S(1)}, u32[]{:S(2)}, u32[]{:S(2)}) collective-permute-start(bf16[128,2048]{1,0:T(8,128)(2,1)} %grad.1), channel_id=1, source_target_pairs={{0,1},{1,0},{2,3},{3,2},{4,5},{5,4},{6,7},{7,6},{8,9},{9,8},{10,11... | collective-permute-start | bytes 1572872 | tf_op jit(solution)/shard_map/ppermute | solution.py:500
  63.5 16.9 %copy-start = (bf16[128,6016]{1,0:T(8,128)(2,1)}, bf16[128,6016]{1,0:T(8,128)(2,1)S(1)}, u32[]{:S(2)}) copy-start(bf16[128,6016]{1,0:T(8,128)(2,1)S(1)} %collective-permute-done.4.refs_5_.refs_9_) | copy-start | bytes 4620292
  63.5 16.9 %copy-start.2 = (bf16[128,6016]{1,0:T(8,128)(2,1)}, bf16[128,6016]{1,0:T(8,128)(2,1)S(1)}, u32[]{:S(2)}) copy-start(bf16[128,6016]{1,0:T(8,128)(2,1)S(1)} %collective-permute-done.5.refs_6_.refs_10_) | copy-start | bytes 4620292
  76.7 3.7 %collective-permute-start.11 = (bf16[128,6016]{1,0:T(8,128)(2,1)}, bf16[128,6016]{1,0:T(8,128)(2,1)}, u32[]{:S(2)}, u32[]{:S(2)}) collective-permute-start(bf16[128,6016]{1,0:T(8,128)(2,1)} %collective-permute-done.10.refs_3_), channel_id=1, source_target_pairs={{0,1},{1,0},{2,3},{3,2},{4,5},{5,4},{6,7},{7,6},{8,9},{9,8},{10,11... | collective-permute-start | bytes 4620296 | tf_op jit(solution)/shard_map/ppermute | solution.py:500
  77.0 15.6 %collective-permute-start.9 = (bf16[1024,256]{1,0:T(8,128)(2,1)}, bf16[1024,256]{1,0:T(8,128)(2,1)}, u32[]{:S(2)}, u32[]{:S(2)}) collective-permute-start(bf16[1024,256]{1,0:T(8,128)(2,1)} %slice.162.refs_1_.refs_8_), channel_id=1, source_target_pairs={{0,4},{1,5},{2,6},{3,7},{4,12},{5,13},{6,14},{7,15},{8,0},{9,1},{1... | collective-permute-start | bytes 1572872 | tf_op jit(solution)/shard_map/ppermute | solution.py:500
  80.4 12.2 %copy-start.7 = (bf16[2496,256]{1,0:T(8,128)(2,1)S(1)}, bf16[2496,256]{1,0:T(8,128)(2,1)}, u32[]{:S(2)}) copy-start(bf16[2496,256]{1,0:T(8,128)(2,1)} %copy-done.6) | copy-start | bytes 3833860
  92.6 5.1 %copy-start.5 = (bf16[128,6016]{1,0:T(8,128)(2,1)S(1)}, bf16[128,6016]{1,0:T(8,128)(2,1)}, u32[]{:S(2)}) copy-start(bf16[128,6016]{1,0:T(8,128)(2,1)} %get-tuple-element.51.refs_0_) | copy-start | bytes 4620292
  92.6 14.8 %collective-permute-start.13 = (bf16[1024,256]{1,0:T(8,128)(2,1)}, bf16[1024,256]{1,0:T(8,128)(2,1)}, u32[]{:S(2)}, u32[]{:S(2)}) collective-permute-start(bf16[1024,256]{1,0:T(8,128)(2,1)} %collective-permute-done.9.refs_2_.refs_9_), channel_id=1, source_target_pairs={{0,4},{1,5},{2,6},{3,7},{4,12},{5,13},{6,14},{7,15},{8,0},{9,1},{1... | collective-permute-start | bytes 1572872 | tf_op jit(solution)/shard_map/ppermute | solution.py:500
  97.6 18.4 %copy-start.4 = (bf16[512,1536]{1,0:T(8,128)(2,1)}, bf16[512,1536]{1,0:T(8,128)(2,1)S(1)}, u32[]{:S(2)}) copy-start(bf16[512,1536]{1,0:T(8,128)(2,1)S(1)} %get-tuple-element.69) | copy-start | bytes 4718596
  97.6 4.1 %collective-permute-start.12 = (bf16[512,1536]{1,0:T(8,128)(2,1)S(1)}, bf16[512,1536]{1,0:T(8,128)(2,1)S(1)}, u32[]{:S(2)}, u32[]{:S(2)}) collective-permute-start(bf16[512,1536]{1,0:T(8,128)(2,1)S(1)} %get-tuple-element.70), channel_id=1, source_target_pairs={{0,1},{1,0},{2,3},{3,2},{4,5},{5,4},{6,7},{7,6},{8,9},{9,8},{10,11... | collective-permute-start | bytes 4718600 | tf_op jit(solution)/shard_map/ppermute | solution.py:500
  102.7 12.3 %collective-permute-start.14 = (bf16[2,128,1536]{2,1,0:T(8,128)(2,1)S(1)}, bf16[2,128,1536]{2,1,0:T(8,128)(2,1)S(1)}, u32[]{:S(2)}, u32[]{:S(2)}) collective-permute-start(bf16[2,128,1536]{2,1,0:T(8,128)(2,1)S(1)} %fusion), channel_id=1, source_target_pairs={{0,2},{1,17},{2,0},{3,19},{4,6},{5,21},{6,4},{7,23},{8,10},{9,25},... | collective-permute-start | bytes 2359304 | tf_op jit(solution)/shard_map/ppermute | solution.py:500
  116.0 4.0 %collective-permute-start.16 = (bf16[512,1792]{1,0:T(8,128)(2,1)}, bf16[512,1792]{1,0:T(8,128)(2,1)S(1)}, u32[]{:S(2)}, u32[]{:S(2)}) collective-permute-start(bf16[512,1792]{1,0:T(8,128)(2,1)} %get-tuple-element.82), channel_id=1, source_target_pairs={{0,1},{1,0},{2,3},{3,2},{4,5},{5,4},{6,7},{7,6},{8,9},{9,8},{10,11... | collective-permute-start | bytes 5505032 | tf_op jit(solution)/shard_map/ppermute | solution.py:500
  118.1 18.4 %collective-permute-start.15 = (bf16[128,1536]{1,0:T(8,128)(2,1)}, bf16[128,1536]{1,0:T(8,128)(2,1)}, u32[]{:S(2)}, u32[]{:S(2)}) collective-permute-start(bf16[128,1536]{1,0:T(8,128)(2,1)} %fusion.4), channel_id=1, source_target_pairs={{0,16},{1,3},{2,18},{3,1},{4,20},{5,7},{6,22},{7,5},{8,24},{9,11},... | collective-permute-start | bytes 1179656 | tf_op jit(solution)/shard_map/ppermute | solution.py:500
  118.8 4.6 %collective-permute-start.19 = (bf16[512,768]{1,0:T(8,128)(2,1)}, bf16[512,768]{1,0:T(8,128)(2,1)S(1)}, u32[]{:S(2)}, u32[]{:S(2)}) collective-permute-start(bf16[512,768]{1,0:T(8,128)(2,1)} %get-tuple-element.88), channel_id=1, source_target_pairs={{0,1},{1,0},{2,3},{3,2},{4,5},{5,4},{6,7},{7,6},{8,9},{9,8},{10,11... | collective-permute-start | bytes 2359304 | tf_op jit(solution)/shard_map/ppermute | solution.py:500
  121.9 13.5 %collective-permute-start.17 = (bf16[2,128,1792]{2,1,0:T(8,128)(2,1)S(1)}, bf16[2,128,1792]{2,1,0:T(8,128)(2,1)S(1)}, u32[]{:S(2)}, u32[]{:S(2)}) collective-permute-start(bf16[2,128,1792]{2,1,0:T(8,128)(2,1)S(1)} %bitcast.67), channel_id=1, source_target_pairs={{0,2},{1,17},{2,0},{3,19},{4,6},{5,21},{6,4},{7,23},{8,10},{9,25},... | collective-permute-start | bytes 2752520 | tf_op jit(solution)/shard_map/ppermute | solution.py:500
  123.4 12.0 %copy-start.21 = (bf16[256,1792]{1,0:T(8,128)(2,1)S(1)}, bf16[256,1792]{1,0:T(8,128)(2,1)}, u32[]{:S(2)}) copy-start(bf16[256,1792]{1,0:T(8,128)(2,1)} %get-tuple-element.81) | copy-start | bytes 2752516
  125.1 11.4 %copy-start.23 = (bf16[2,128,1536]{2,1,0:T(8,128)(2,1)S(1)}, bf16[2,128,1536]{2,1,0:T(8,128)(2,1)}, u32[]{:S(2)}) copy-start(bf16[2,128,1536]{2,1,0:T(8,128)(2,1)} %copy-done.22) | copy-start | bytes 2359300
  125.1 15.2 %collective-permute-start.20 = (bf16[2,128,768]{2,1,0:T(8,128)(2,1)S(1)}, bf16[2,128,768]{2,1,0:T(8,128)(2,1)S(1)}, u32[]{:S(2)}, u32[]{:S(2)}) collective-permute-start(bf16[2,128,768]{2,1,0:T(8,128)(2,1)S(1)} %bitcast.68), channel_id=1, source_target_pairs={{0,2},{1,17},{2,0},{3,19},{4,6},{5,21},{6,4},{7,23},{8,10},{9,25},... | collective-permute-start | bytes 1179656 | tf_op jit(solution)/shard_map/ppermute | solution.py:500
  135.6 9.4 %collective-permute-start.18 = (bf16[128,1792]{1,0:T(8,128)(2,1)S(1)}, bf16[128,1792]{1,0:T(8,128)(2,1)S(1)}, u32[]{:S(2)}, u32[]{:S(2)}) collective-permute-start(bf16[128,1792]{1,0:T(8,128)(2,1)S(1)} %fusion.3), channel_id=1, source_target_pairs={{0,16},{1,3},{2,18},{3,1},{4,20},{5,7},{6,22},{7,5},{8,24},{9,11},... | collective-permute-start | bytes 1376264 | tf_op jit(solution)/shard_map/ppermute | solution.py:500
  140.5 7.8 %collective-permute-start.22 = (bf16[128,768]{1,0:T(8,128)(2,1)S(1)}, bf16[128,768]{1,0:T(8,128)(2,1)S(1)}, u32[]{:S(2)}, u32[]{:S(2)}) collective-permute-start(bf16[128,768]{1,0:T(8,128)(2,1)S(1)} %get-tuple-element.95), channel_id=1, source_target_pairs={{0,16},{1,3},{2,18},{3,1},{4,20},{5,7},{6,22},{7,5},{8,24},{9,11},... | collective-permute-start | bytes 589832 | tf_op jit(solution)/shard_map/ppermute | solution.py:500
  145.4 1.6 %collective-permute-start.21 = (bf16[2,128,512]{2,1,0:T(8,128)(2,1)S(1)}, bf16[2,128,512]{2,1,0:T(8,128)(2,1)S(1)}, u32[]{:S(2)}, u32[]{:S(2)}) collective-permute-start(bf16[2,128,512]{2,1,0:T(8,128)(2,1)S(1)} %slice.218), channel_id=1, source_target_pairs={{0,1},{1,0},{2,3},{3,2},{4,5},{5,4},{6,7},{7,6},{8,9},{9,8},{10,11... | collective-permute-start | bytes 786440 | tf_op jit(solution)/shard_map/ppermute | solution.py:500
  (19 other events, 44.2 us)

commit v8 on v6

--- a/solution.py
+++ b/solution.py
@@ -595,8 +595,10 @@
     late_far = after(late_far, o_send)
     t0, t1, m0, n0, m1, n1 = late_slices(m, idx, pos, gm, rest, late_far, mixture, kv, attention, earlies)
     t0, t1, o_first = phase(t0, t1, o_first)
-    t0, t1 = move(t0, CORE), move(t1, CORE)
-    o_next = carry_on(o_mine, o_theirs, o_first)
+    t0 = move(t0, CORE)
+    t1 = move(after(t1, t0), CORE)
+    merged = (a.reshape(-1, a.shape[2]) for a in (o_mine, o_theirs, o_first))
+    o_next = add_rows(rows, *((a, rows) for a in merged))
     o_second = move(o_next, SECOND)
     t0 = after(t0, o_next)
     send0 = add_rows(2 * rows, (n0, 0), (t0, 2 * rows))

time: 150 us -> 160 us (1.067)
  waiting for transfers between devices: 79.1 us -> 85.4 us
  Pallas kernels: 32.5 us -> 36.1 us
  local copies, waits for them, and re-layouts: 8.94 us -> 6.91 us
    ppermute x23, waiting for transfers between devices: 79.1 us -> 85.4 us  [move(): return lax.ppermute(array, AXES, pairs)]
    pallas_call x6 -> x7, Pallas kernels: 26 us -> 29.7 us  [copy_call(): pl.pallas_call(body, in_specs=[smem] * len(scalars) + [pl.BlockSpec(memor...]
    unnamed x56 -> x54, local copies, waits for them, and re-layouts: 6.23 us -> 4.2 us
  transfers between devices with their start and end apart: 23 -> 23, of which waited for: 11 -> 10; matrix products, arithmetic and copies ran while one was open for 8% -> 8% of each run, Pallas kernels for 20% -> 20%
where the time goes in v8:
time: 160 us; the launch traced here: 159 us
  waiting for transfers between devices  85.4 us (53%)
  Pallas kernels  36.1 us (23%)
  starting transfers between devices  18.7 us (12%)
  other arithmetic  10.4 us (6%)
  local copies, waits for them, and re-layouts  6.91 us (4%)
    ppermute x23, waiting for transfers between devices, move(): return lax.ppermute(array, AXES, pairs)  85.4 us
    pallas_call x7, Pallas kernels, copy_call(): pl.pallas_call(body, in_specs=[smem] * len(scalars) + [pl.BlockSpec(memor...  29.7 us
    ppermute x23, starting transfers between devices, move(): return lax.ppermute(array, AXES, pairs)  18.7 us
    pallas_call x2, Pallas kernels, kernel_call(): pl.pallas_call(body, grid_spec=pltpu.PrefetchScalarGridSpec(num_scalar_pr...  6.48 us
    unnamed x54, local copies, waits for them, and re-layouts  4.2 us
  transfers between devices with their start and end apart: 23, of which 10 were waited for; matrix products, arithmetic and copies ran while one was open for 8% of the time, Pallas kernels for 20%

profile of v8, /device:TPU:0, one launch (start us, length us, event | category | flops | bytes accessed | tf_op | source)
XLA Modules:
  0.0 158.8 jit_solution(5468998217988093792)
XLA Ops:
  0.6 2.5 %projection_slices.1._ = bf16[2496,256]{1,0:T(8,128)(2,1)} custom-call(s32[1]{0:T(128)} %bitcast.1.place, bf16[1024,1024]{1,0:T(8,128)(2,1)} %q.1, bf16[224,1024]{1,0:T(8,128)(2,1)} %k.1, bf16[224,1024]{1,0:T(8,128)(2,1)} %v.1, bf16[1024,1024]{1,0:T(8,128)(2,1)} %o.1), custom_call_target="tpu_custom_call" | custom-call | flops 99999997952 | bytes 1024 | tf_op jit(solution)/shard_map/projection_slices/pallas_call | solution.py:47
  3.1 4.0 %collective-permute-start.3 = (bf16[2496,256]{1,0:T(8,128)(2,1)}, bf16[2496,256]{1,0:T(8,128)(2,1)S(1)}, u32[]{:S(2)}, u32[]{:S(2)}) collective-permute-start(bf16[2496,256]{1,0:T(8,128)(2,1)} %projection_slices.1._), channel_id=1, source_target_pairs={{0,8},{1,9},{2,10},{3,11},{4,0},{5,1},{6,2},{7,3},{8,12},{9,13},{1... | collective-permute-start | bytes 3833864 | tf_op jit(solution)/shard_map/ppermute | solution.py:500
  7.2 4.0 %prepare.1 = (bf16[128,6016]{1,0:T(8,128)(2,1)}, bf16[128,1792]{1,0:T(8,128)(2,1)}) custom-call(s32[1]{0:T(128)} %bitcast.core, s32[2,4]{1,0:T(2,128)} %owners.1, s32[2,4]{1,0:T(2,128)} %ids.1, bf16[128,2048]{1,0:T(8,128)(2,1)} %hid.1, bf16[128,2048]{1,0:T(8,128)(2,1)} %grad.1, bf16[8,64,896]{2,1,0:T(8,128)(2,1)} %db.1, f32[896]{0:T(1024)} %gain.1, ...), custom_call_target="tpu_custom_call" | custom-call | flops 99999997952 | bytes 1024 | tf_op jit(solution)/shard_map/prepare/pallas_call | solution.py:47
  11.2 1.5 collective-permute-start
  12.7 1.5 collective-permute-start.1
  14.3 38.3 %collective-permute-done.2.refs_13_.refs_7_ = bf16[1472,256]{1,0:T(8,128)(2,1)S(1)} collective-permute-done((bf16[1472,256]{1,0:T(8,128)(2,1)S(1)}, bf16[1472,256]{1,0:T(8,128)(2,1)S(1)}, u32[]{:S(2)}, u32[]{:S(2)}) %collective-permute-start.2) | collective-permute-done | bytes 753696 | tf_op jit(solution)/shard_map/ppermute | solution.py:500
  54.6 1.5 collective-permute-start.10
  56.9 2.4 %collective-permute-done.6.refs_8_ = bf16[128,2048]{1,0:T(8,128)(2,1)} collective-permute-done((bf16[128,2048]{1,0:T(8,128)(2,1)}, bf16[128,2048]{1,0:T(8,128)(2,1)}, u32[]{:S(2)}, u32[]{:S(2)}) %collective-permute-start.6) | collective-permute-done | bytes 524320 | tf_op jit(solution)/shard_map/ppermute | solution.py:500
  59.5 1.9 %slice.149.refs_1_.refs_8_ = bf16[1024,256]{1,0:T(8,128)(2,1)} slice(bf16[2496,256]{1,0:T(8,128)(2,1)} %projection_slices.1._), slice={[1472:2496], [0:256]} | slice | bytes 1048576 | tf_op jit(solution)/shard_map/slice | solution.py:532
  63.5 13.1 %collective-permute-done.8.refs_15_.refs_9_ = bf16[1472,256]{1,0:T(8,128)(2,1)} collective-permute-done((bf16[1472,256]{1,0:T(8,128)(2,1)}, bf16[1472,256]{1,0:T(8,128)(2,1)}, u32[]{:S(2)}, u32[]{:S(2)}) %collective-permute-start.8) | collective-permute-done | bytes 753696 | tf_op jit(solution)/shard_map/ppermute | solution.py:500
  78.4 1.9 %collective-permute-done.11.refs_7_.refs_11_ = bf16[128,6016]{1,0:T(8,128)(2,1)} collective-permute-done((bf16[128,6016]{1,0:T(8,128)(2,1)}, bf16[128,6016]{1,0:T(8,128)(2,1)}, u32[]{:S(2)}, u32[]{:S(2)}) %collective-permute-start.11) | collective-permute-done | bytes 1540128 | tf_op jit(solution)/shard_map/ppermute | solution.py:500
  80.3 10.5 %forward.1 = (bf16[2048,512]{1,0:T(8,128)(2,1)}, bf16[512,256]{1,0:T(8,128)(2,1)}, f32[8,2,64,256]{3,2,1,0:T(8,128)}) custom-call(s32[4]{0:T(128)} %pad_add_fusion.3.src, s32[8,4]{1,0:T(8,128)} %fusion.15.idx, s32[4]{0:T(128)} %pad_add_fusion.2.pos, bf16[128,6016]{1,0:T(8,128)(2,1)} %get-tuple-element.52.refs_0_, ...), custom_call_target="tpu_custom_call" | custom-call | flops 1024 | bytes 1024 | tf_op jit(solution)/shard_map/forward/pallas_call | solution.py:81
  90.9 1.6 %collective-permute-done.9.refs_2_.refs_9_ = bf16[1024,256]{1,0:T(8,128)(2,1)} collective-permute-done((bf16[1024,256]{1,0:T(8,128)(2,1)}, bf16[1024,256]{1,0:T(8,128)(2,1)}, u32[]{:S(2)}, u32[]{:S(2)}) %collective-permute-start.9) | collective-permute-done | bytes 524320 | tf_op jit(solution)/shard_map/ppermute | solution.py:500
  92.5 1.2 copy-done.7
  93.7 1.3 copy-done.15
  95.0 2.5 %output_slices.1 = (bf16[512,1536]{1,0:T(8,128)(2,1)S(1)}, bf16[512,1536]{1,0:T(8,128)(2,1)S(1)}) custom-call(s32[1]{0:T(128)} %bitcast.core, bf16[512,256]{1,0:T(8,128)(2,1)S(1)} %copy-done.15, bf16[1024,256]{1,0:T(8,128)(2,1)S(1)} %copy-done.7, bf16[1024,256]{1,0:T(8,128)(2,1)} %collective-permute-done.9.refs_2_.refs_9_, bf16[2496,256]{1,0:T(8,128)(2,1)S(1)} %copy-done.6), custom_call_target="tpu_custom_call" | custom-call | flops 99999997952 | bytes 1024 | tf_op jit(solution)/shard_map/output_slices/pallas_call | solution.py:81
  97.6 3.8 %cotangent.1 = (f32[512,256]{1,0:T(8,128)S(1)}, bf16[512,1024]{1,0:T(8,128)(2,1)S(1)}) custom-call(s32[4]{0:T(128)S(1)} %copy-done.12, bf16[128,6016]{1,0:T(8,128)(2,1)S(1)} %copy-done.4, bf16[128,6016]{1,0:T(8,128)(2,1)} %collective-permute-done.1.refs_1_, bf16[128,6016]{1,0:T(8,128)(2,1)} %collective-permute-done.refs_2_, ...), custom_call_target="tpu_custom_call" | custom-call | flops 99999997952 | bytes 1024 | tf_op jit(solution)/shard_map/cotangent/pallas_call | solution.py:81
  102.6 1.5 collective-permute-start.14
  104.1 3.2 %collective-permute-done.13.refs_2_ = bf16[1024,256]{1,0:T(8,128)(2,1)} collective-permute-done((bf16[1024,256]{1,0:T(8,128)(2,1)}, bf16[1024,256]{1,0:T(8,128)(2,1)}, u32[]{:S(2)}, u32[]{:S(2)}) %collective-permute-start.13) | collective-permute-done | bytes 524320 | tf_op jit(solution)/shard_map/ppermute | solution.py:500
  107.3 7.6 %late_slices.1 = (bf16[512,1536]{1,0:T(8,128)(2,1)}, bf16[512,1024]{1,0:T(8,128)(2,1)}, bf16[256,1536]{1,0:T(8,128)(2,1)}, bf16[256,1536]{1,0:T(8,128)(2,1)}, bf...) custom-call(s32[1]{0:T(128)} %bitcast.core, s32[8,4]{1,0:T(8,128)} %fusion.15.idx, s32[4]{0:T(128)} %pad_add_fusion.2.pos, ...), custom_call_target="tpu_custom_call" | custom-call | flops 99999997952 | bytes 1024 | tf_op jit(solution)/shard_map/late_slices/pallas_call | solution.py:81
  115.0 2.3 %add_rows.3 = bf16[128,1536]{1,0:T(8,128)(2,1)S(1)} custom-call(bf16[512,1536]{1,0:T(8,128)(2,1)S(1)} %get-tuple-element.70.refs_0_, bf16[512,1536]{1,0:T(8,128)(2,1)S(1)} %collective-permute-done.12, bf16[256,1536]{1,0:T(8,128)(2,1)S(1)} %bitcast.65), custom_call_target="tpu_custom_call" | custom-call | flops 99999997952 | bytes 1024 | tf_op jit(solution)/shard_map/add_rows/pallas_call | solution.py:81
  117.3 1.3 collective-permute-done.16.refs_1_
  118.6 1.8 %add_rows.4 = bf16[256,1536]{1,0:T(8,128)(2,1)} custom-call(bf16[256,1536]{1,0:T(8,128)(2,1)S(1)} %copy-done.17, bf16[512,1536]{1,0:T(8,128)(2,1)S(1)} %collective-permute-done.16.refs_1_), custom_call_target="tpu_custom_call" | custom-call | flops 99999997952 | bytes 1024 | tf_op jit(solution)/shard_map/add_rows/pallas_call | solution.py:81
  120.4 1.6 collective-permute-start.17
  122.5 14.5 %collective-permute-done.17 = bf16[2,128,1536]{2,1,0:T(8,128)(2,1)} collective-permute-done((bf16[2,128,1536]{2,1,0:T(8,128)(2,1)}, bf16[2,128,1536]{2,1,0:T(8,128)(2,1)}, u32[]{:S(2)}, u32[]{:S(2)}) %collective-permute-start.17) | collective-permute-done | bytes 786464 | tf_op jit(solution)/shard_map/ppermute | solution.py:500
  137.0 1.4 fusion.3
  139.4 1.2 add_rows.5
  140.6 1.4 collective-permute-start.20
  142.3 7.9 %collective-permute-done.20 = bf16[2,128,1024]{2,1,0:T(8,128)(2,1)S(1)} collective-permute-done((bf16[2,128,1024]{2,1,0:T(8,128)(2,1)S(1)}, bf16[2,128,1024]{2,1,0:T(8,128)(2,1)S(1)}, u32[]{:S(2)}, u32[]{:S(2)}) %collective-permute-start.20) | collective-permute-done | bytes 524320 | tf_op jit(solution)/shard_map/ppermute | solution.py:500
  150.1 1.3 convert_add_fusion.5
  152.5 1.3 fusion.2
  153.9 1.7 %collective-permute-start.21 = (bf16[2,128,512]{2,1,0:T(8,128)(2,1)S(1)}, bf16[2,128,512]{2,1,0:T(8,128)(2,1)S(1)}, u32[]{:S(2)}, u32[]{:S(2)}) collective-permute-start(bf16[2,128,512]{2,1,0:T(8,128)(2,1)S(1)} %slice.202), channel_id=1, source_target_pairs={{0,1},{1,0},{2,3},{3,2},{4,5},{5,4},{6,7},{7,6},{8,9},{9,8},{10,11... | collective-permute-start | bytes 786440 | tf_op jit(solution)/shard_map/ppermute | solution.py:500
  (112 shorter events, 14.2 us)
Async XLA Ops:
  3.1 49.5 %collective-permute-start.3 = (bf16[2496,256]{1,0:T(8,128)(2,1)}, bf16[2496,256]{1,0:T(8,128)(2,1)S(1)}, u32[]{:S(2)}, u32[]{:S(2)}) collective-permute-start(bf16[2496,256]{1,0:T(8,128)(2,1)} %projection_slices.1._), channel_id=1, source_target_pairs={{0,8},{1,9},{2,10},{3,11},{4,0},{5,1},{6,2},{7,3},{8,12},{9,13},{1... | collective-permute-start | bytes 3833864 | tf_op jit(solution)/shard_map/ppermute | solution.py:500
  7.2 7.0 %copy-start.21 = (bf16[2496,256]{1,0:T(8,128)(2,1)S(1)}, bf16[2496,256]{1,0:T(8,128)(2,1)}, u32[]{:S(2)}) copy-start(bf16[2496,256]{1,0:T(8,128)(2,1)} %projection_slices.1._) | copy-start | bytes 3833860
  11.2 42.9 %collective-permute-start = (bf16[128,6016]{1,0:T(8,128)(2,1)}, bf16[128,6016]{1,0:T(8,128)(2,1)}, u32[]{:S(2)}, u32[]{:S(2)}) collective-permute-start(bf16[128,6016]{1,0:T(8,128)(2,1)} %get-tuple-element.52.refs_0_), channel_id=1, source_target_pairs={{0,2},{1,17},{2,0},{3,19},{4,6},{5,21},{6,4},{7,23},{8,10},{9,25},... | collective-permute-start | bytes 4620296 | tf_op jit(solution)/shard_map/ppermute | solution.py:500
  12.7 41.4 %collective-permute-start.1 = (bf16[128,6016]{1,0:T(8,128)(2,1)}, bf16[128,6016]{1,0:T(8,128)(2,1)}, u32[]{:S(2)}, u32[]{:S(2)}) collective-permute-start(bf16[128,6016]{1,0:T(8,128)(2,1)} %get-tuple-element.52.refs_0_), channel_id=1, source_target_pairs={{0,16},{1,3},{2,18},{3,1},{4,20},{5,7},{6,22},{7,5},{8,24},{9,11},... | collective-permute-start | bytes 4620296 | tf_op jit(solution)/shard_map/ppermute | solution.py:500
  14.2 39.8 %copy-start.20 = (bf16[1472,256]{1,0:T(8,128)(2,1)}, bf16[1472,256]{1,0:T(8,128)(2,1)S(1)}, u32[]{:S(2)}) copy-start(bf16[1472,256]{1,0:T(8,128)(2,1)S(1)} %slice.148.refs_12_.refs_6_) | copy-start | bytes 2260996
  14.2 38.4 %collective-permute-start.2 = (bf16[1472,256]{1,0:T(8,128)(2,1)S(1)}, bf16[1472,256]{1,0:T(8,128)(2,1)S(1)}, u32[]{:S(2)}, u32[]{:S(2)}) collective-permute-start(bf16[1472,256]{1,0:T(8,128)(2,1)S(1)} %slice.148.refs_12_.refs_6_), channel_id=1, source_target_pairs={{0,4},{1,5},{2,6},{3,7},{4,12},{5,13},{6,14},{7,15},{8,0},{9,1},{1... | collective-permute-start | bytes 2261000 | tf_op jit(solution)/shard_map/ppermute | solution.py:500
  54.1 9.4 %collective-permute-start.4 = (bf16[128,6016]{1,0:T(8,128)(2,1)}, bf16[128,6016]{1,0:T(8,128)(2,1)S(1)}, u32[]{:S(2)}, u32[]{:S(2)}) collective-permute-start(bf16[128,6016]{1,0:T(8,128)(2,1)} %collective-permute-done.refs_2_), channel_id=1, source_target_pairs={{0,1},{1,0},{2,3},{3,2},{4,5},{5,4},{6,7},{7,6},{8,9},{9,8},{10,11... | collective-permute-start | bytes 4620296 | tf_op jit(solution)/shard_map/ppermute | solution.py:500
  54.1 9.4 %collective-permute-start.5 = (bf16[128,6016]{1,0:T(8,128)(2,1)}, bf16[128,6016]{1,0:T(8,128)(2,1)S(1)}, u32[]{:S(2)}, u32[]{:S(2)}) collective-permute-start(bf16[128,6016]{1,0:T(8,128)(2,1)} %collective-permute-done.1.refs_1_), channel_id=1, source_target_pairs={{0,1},{1,0},{2,3},{3,2},{4,5},{5,4},{6,7},{7,6},{8,9},{9,8},{10,11... | collective-permute-start | bytes 4620296 | tf_op jit(solution)/shard_map/ppermute | solution.py:500
  54.6 22.0 %collective-permute-start.10 = (bf16[128,6016]{1,0:T(8,128)(2,1)}, bf16[128,6016]{1,0:T(8,128)(2,1)}, u32[]{:S(2)}, u32[]{:S(2)}) collective-permute-start(bf16[128,6016]{1,0:T(8,128)(2,1)} %collective-permute-done.refs_2_), channel_id=1, source_target_pairs={{0,16},{1,3},{2,18},{3,1},{4,20},{5,7},{6,22},{7,5},{8,24},{9,11},... | collective-permute-start | bytes 4620296 | tf_op jit(solution)/shard_map/ppermute | solution.py:500
  56.2 3.2 %collective-permute-start.6 = (bf16[128,2048]{1,0:T(8,128)(2,1)}, bf16[128,2048]{1,0:T(8,128)(2,1)}, u32[]{:S(2)}, u32[]{:S(2)}) collective-permute-start(bf16[128,2048]{1,0:T(8,128)(2,1)} %hid.1), channel_id=1, source_target_pairs={{0,1},{1,0},{2,3},{3,2},{4,5},{5,4},{6,7},{7,6},{8,9},{9,8},{10,11... | collective-permute-start | bytes 1572872 | tf_op jit(solution)/shard_map/ppermute | solution.py:500
  56.2 20.5 %collective-permute-start.8 = (bf16[1472,256]{1,0:T(8,128)(2,1)}, bf16[1472,256]{1,0:T(8,128)(2,1)}, u32[]{:S(2)}, u32[]{:S(2)}) collective-permute-start(bf16[1472,256]{1,0:T(8,128)(2,1)} %copy-done.23), channel_id=1, source_target_pairs={{0,4},{1,5},{2,6},{3,7},{4,12},{5,13},{6,14},{7,15},{8,0},{9,1},{1... | collective-permute-start | bytes 2261000 | tf_op jit(solution)/shard_map/ppermute | solution.py:500
  59.3 3.4 %collective-permute-start.7 = (bf16[128,2048]{1,0:T(8,128)(2,1)}, bf16[128,2048]{1,0:T(8,128)(2,1)S(1)}, u32[]{:S(2)}, u32[]{:S(2)}) collective-permute-start(bf16[128,2048]{1,0:T(8,128)(2,1)} %grad.1), channel_id=1, source_target_pairs={{0,1},{1,0},{2,3},{3,2},{4,5},{5,4},{6,7},{7,6},{8,9},{9,8},{10,11... | collective-permute-start | bytes 1572872 | tf_op jit(solution)/shard_map/ppermute | solution.py:500
  63.5 16.9 %copy-start = (bf16[128,6016]{1,0:T(8,128)(2,1)}, bf16[128,6016]{1,0:T(8,128)(2,1)S(1)}, u32[]{:S(2)}) copy-start(bf16[128,6016]{1,0:T(8,128)(2,1)S(1)} %collective-permute-done.4.refs_5_.refs_9_) | copy-start | bytes 4620292
  63.5 16.8 %copy-start.2 = (bf16[128,6016]{1,0:T(8,128)(2,1)}, bf16[128,6016]{1,0:T(8,128)(2,1)S(1)}, u32[]{:S(2)}) copy-start(bf16[128,6016]{1,0:T(8,128)(2,1)S(1)} %collective-permute-done.5.refs_6_.refs_10_) | copy-start | bytes 4620292
  76.6 3.7 %collective-permute-start.11 = (bf16[128,6016]{1,0:T(8,128)(2,1)}, bf16[128,6016]{1,0:T(8,128)(2,1)}, u32[]{:S(2)}, u32[]{:S(2)}) collective-permute-start(bf16[128,6016]{1,0:T(8,128)(2,1)} %collective-permute-done.10.refs_3_), channel_id=1, source_target_pairs={{0,1},{1,0},{2,3},{3,2},{4,5},{5,4},{6,7},{7,6},{8,9},{9,8},{10,11... | collective-permute-start | bytes 4620296 | tf_op jit(solution)/shard_map/ppermute | solution.py:500
  77.0 15.6 %collective-permute-start.9 = (bf16[1024,256]{1,0:T(8,128)(2,1)}, bf16[1024,256]{1,0:T(8,128)(2,1)}, u32[]{:S(2)}, u32[]{:S(2)}) collective-permute-start(bf16[1024,256]{1,0:T(8,128)(2,1)} %slice.149.refs_1_.refs_8_), channel_id=1, source_target_pairs={{0,4},{1,5},{2,6},{3,7},{4,12},{5,13},{6,14},{7,15},{8,0},{9,1},{1... | collective-permute-start | bytes 1572872 | tf_op jit(solution)/shard_map/ppermute | solution.py:500
  80.3 12.2 %copy-start.6 = (bf16[2496,256]{1,0:T(8,128)(2,1)S(1)}, bf16[2496,256]{1,0:T(8,128)(2,1)}, u32[]{:S(2)}) copy-start(bf16[2496,256]{1,0:T(8,128)(2,1)} %copy-done.5) | copy-start | bytes 3833860
  92.5 5.1 %copy-start.4 = (bf16[128,6016]{1,0:T(8,128)(2,1)S(1)}, bf16[128,6016]{1,0:T(8,128)(2,1)}, u32[]{:S(2)}) copy-start(bf16[128,6016]{1,0:T(8,128)(2,1)} %get-tuple-element.52.refs_0_) | copy-start | bytes 4620292
  92.5 14.8 %collective-permute-start.13 = (bf16[1024,256]{1,0:T(8,128)(2,1)}, bf16[1024,256]{1,0:T(8,128)(2,1)}, u32[]{:S(2)}, u32[]{:S(2)}) collective-permute-start(bf16[1024,256]{1,0:T(8,128)(2,1)} %collective-permute-done.9.refs_2_.refs_9_), channel_id=1, source_target_pairs={{0,4},{1,5},{2,6},{3,7},{4,12},{5,13},{6,14},{7,15},{8,0},{9,1},{1... | collective-permute-start | bytes 1572872 | tf_op jit(solution)/shard_map/ppermute | solution.py:500
  97.5 4.1 %collective-permute-start.12 = (bf16[512,1536]{1,0:T(8,128)(2,1)S(1)}, bf16[512,1536]{1,0:T(8,128)(2,1)S(1)}, u32[]{:S(2)}, u32[]{:S(2)}) collective-permute-start(bf16[512,1536]{1,0:T(8,128)(2,1)S(1)} %get-tuple-element.71), channel_id=1, source_target_pairs={{0,1},{1,0},{2,3},{3,2},{4,5},{5,4},{6,7},{7,6},{8,9},{9,8},{10,11... | collective-permute-start | bytes 4718600 | tf_op jit(solution)/shard_map/ppermute | solution.py:500
  102.6 12.2 %collective-permute-start.14 = (bf16[2,128,1536]{2,1,0:T(8,128)(2,1)S(1)}, bf16[2,128,1536]{2,1,0:T(8,128)(2,1)S(1)}, u32[]{:S(2)}, u32[]{:S(2)}) collective-permute-start(bf16[2,128,1536]{2,1,0:T(8,128)(2,1)S(1)} %fusion), channel_id=1, source_target_pairs={{0,2},{1,17},{2,0},{3,19},{4,6},{5,21},{6,4},{7,23},{8,10},{9,25},... | collective-permute-start | bytes 2359304 | tf_op jit(solution)/shard_map/ppermute | solution.py:500
  114.9 3.7 %collective-permute-start.16 = (bf16[512,1536]{1,0:T(8,128)(2,1)}, bf16[512,1536]{1,0:T(8,128)(2,1)S(1)}, u32[]{:S(2)}, u32[]{:S(2)}) collective-permute-start(bf16[512,1536]{1,0:T(8,128)(2,1)} %get-tuple-element.83), channel_id=1, source_target_pairs={{0,1},{1,0},{2,3},{3,2},{4,5},{5,4},{6,7},{7,6},{8,9},{9,8},{10,11... | collective-permute-start | bytes 4718600 | tf_op jit(solution)/shard_map/ppermute | solution.py:500
  120.4 16.6 %collective-permute-start.17 = (bf16[2,128,1536]{2,1,0:T(8,128)(2,1)}, bf16[2,128,1536]{2,1,0:T(8,128)(2,1)}, u32[]{:S(2)}, u32[]{:S(2)}) collective-permute-start(bf16[2,128,1536]{2,1,0:T(8,128)(2,1)} %bitcast.18), channel_id=1, source_target_pairs={{0,2},{1,17},{2,0},{3,19},{4,6},{5,21},{6,4},{7,23},{8,10},{9,25},... | collective-permute-start | bytes 2359304 | tf_op jit(solution)/shard_map/ppermute | solution.py:500
  121.9 17.5 %collective-permute-start.19 = (bf16[512,1024]{1,0:T(8,128)(2,1)}, bf16[512,1024]{1,0:T(8,128)(2,1)}, u32[]{:S(2)}, u32[]{:S(2)}) collective-permute-start(bf16[512,1024]{1,0:T(8,128)(2,1)} %get-tuple-element.90), channel_id=1, source_target_pairs={{0,1},{1,0},{2,3},{3,2},{4,5},{5,4},{6,7},{7,6},{8,9},{9,8},{10,11... | collective-permute-start | bytes 3145736 | tf_op jit(solution)/shard_map/ppermute | solution.py:500
  121.9 17.3 %copy-start.11 = (bf16[2,128,1536]{2,1,0:T(8,128)(2,1)S(1)}, bf16[2,128,1536]{2,1,0:T(8,128)(2,1)}, u32[]{:S(2)}) copy-start(bf16[2,128,1536]{2,1,0:T(8,128)(2,1)} %copy-done.10) | copy-start | bytes 2359300
  122.0 17.3 %collective-permute-start.15 = (bf16[128,1536]{1,0:T(8,128)(2,1)S(1)}, bf16[128,1536]{1,0:T(8,128)(2,1)S(1)}, u32[]{:S(2)}, u32[]{:S(2)}) collective-permute-start(bf16[128,1536]{1,0:T(8,128)(2,1)S(1)} %add_rows.3), channel_id=1, source_target_pairs={{0,16},{1,3},{2,18},{3,1},{4,20},{5,7},{6,22},{7,5},{8,24},{9,11},... | collective-permute-start | bytes 1179656 | tf_op jit(solution)/shard_map/ppermute | solution.py:500
  138.4 14.1 %collective-permute-start.18 = (bf16[128,1536]{1,0:T(8,128)(2,1)S(1)}, bf16[128,1536]{1,0:T(8,128)(2,1)S(1)}, u32[]{:S(2)}, u32[]{:S(2)}) collective-permute-start(bf16[128,1536]{1,0:T(8,128)(2,1)S(1)} %fusion.3), channel_id=1, source_target_pairs={{0,16},{1,3},{2,18},{3,1},{4,20},{5,7},{6,22},{7,5},{8,24},{9,11},... | collective-permute-start | bytes 1179656 | tf_op jit(solution)/shard_map/ppermute | solution.py:500
  140.6 9.5 %copy-start.26 = (bf16[256,1024]{1,0:T(8,128)(2,1)S(1)}, bf16[256,1024]{1,0:T(8,128)(2,1)}, u32[]{:S(2)}) copy-start(bf16[256,1024]{1,0:T(8,128)(2,1)} %get-tuple-element.88) | copy-start | bytes 1572868
  140.6 9.5 %collective-permute-start.20 = (bf16[2,128,1024]{2,1,0:T(8,128)(2,1)S(1)}, bf16[2,128,1024]{2,1,0:T(8,128)(2,1)S(1)}, u32[]{:S(2)}, u32[]{:S(2)}) collective-permute-start(bf16[2,128,1024]{2,1,0:T(8,128)(2,1)S(1)} %bitcast.66), channel_id=1, source_target_pairs={{0,2},{1,17},{2,0},{3,19},{4,6},{5,21},{6,4},{7,23},{8,10},{9,25},... | collective-permute-start | bytes 1572872 | tf_op jit(solution)/shard_map/ppermute | solution.py:500
  142.2 10.3 %copy-start.22 = (bf16[256,1536]{1,0:T(8,128)(2,1)S(1)}, bf16[256,1536]{1,0:T(8,128)(2,1)}, u32[]{:S(2)}) copy-start(bf16[256,1536]{1,0:T(8,128)(2,1)} %get-tuple-element.82) | copy-start | bytes 2359300
  151.4 6.5 %collective-permute-start.22 = (bf16[128,1024]{1,0:T(8,128)(2,1)S(1)}, bf16[128,1024]{1,0:T(8,128)(2,1)S(1)}, u32[]{:S(2)}, u32[]{:S(2)}) collective-permute-start(bf16[128,1024]{1,0:T(8,128)(2,1)S(1)} %get-tuple-element.97), channel_id=1, source_target_pairs={{0,16},{1,3},{2,18},{3,1},{4,20},{5,7},{6,22},{7,5},{8,24},{9,11},... | collective-permute-start | bytes 786440 | tf_op jit(solution)/shard_map/ppermute | solution.py:500
  153.9 2.8 %collective-permute-start.21 = (bf16[2,128,512]{2,1,0:T(8,128)(2,1)S(1)}, bf16[2,128,512]{2,1,0:T(8,128)(2,1)S(1)}, u32[]{:S(2)}, u32[]{:S(2)}) collective-permute-start(bf16[2,128,512]{2,1,0:T(8,128)(2,1)S(1)} %slice.202), channel_id=1, source_target_pairs={{0,1},{1,0},{2,3},{3,2},{4,5},{5,4},{6,7},{7,6},{8,9},{9,8},{10,11... | collective-permute-start | bytes 786440 | tf_op jit(solution)/shard_map/ppermute | solution.py:500
  (18 other events, 38.1 us)
